TPU v7x, 32 devices: a whole 2x2x4 slice. The times are simulated.
32 devices in a mesh: seq: 8 (over z, x), tp: 4 (over y, core).
Axes of the slice: x: 2, y: 2, z: 4, core: 2. Of those that a mesh axis runs over, the one named last changes fastest.
Arguments:
- hidden_in: bfloat16 [256, 2048], P('seq'), may hold values from -6 to 6
- query_weight: bfloat16 [2048, 2048], P(None, 'tp'), may hold values from -0.125 to 0.125
- key_weight: bfloat16 [2048, 2048], P(None, 'tp'), may hold values from -0.125 to 0.125
- value_weight: bfloat16 [2048, 2048], P(None, 'tp'), may hold values from -0.125 to 0.125
- out_weight: bfloat16 [2048, 2048], P('tp'), may hold values from -0.125 to 0.125
- query_gain: float32 [2048], P('tp'), may hold values from 0.5 to 1.5
- key_gain: float32 [2048], P('tp'), may hold values from 0.5 to 1.5
- post_gain: float32 [2048], P('tp'), may hold values from 0.5 to 1.5
- key_cache: bfloat16 [4, 1024, 2048], P(None, 'seq', 'tp'), may hold values from -110 to 110
- value_cache: bfloat16 [4, 1024, 2048], P(None, 'seq', 'tp'), may hold values from -6 to 6
- cache_lengths: int32 [4], replicated, may hold values from 128 to 960
- parents: int32 [4, 64], replicated, may hold values from -1 to 62, as said below
- accepted_leaf: int32 [4], replicated, may hold values from 0 to 63
Outputs:
- hidden_out: bfloat16 [256, 2048], P('seq', 'tp')
- new_key_cache: bfloat16 [4, 1024, 2048], P(None, 'seq', 'tp')
- new_value_cache: bfloat16 [4, 1024, 2048], P(None, 'seq', 'tp')
Inputs may be any that keep to these rules, and one draw needn't show every extreme that they name: parents[r, 0] = -1; for i >= 1, parents[r, i] lies in max(0, i - 3) to i - 1; parents[r, 63] = 62.
All inputs are finite; a program needn't handle non-finite values.
Results may differ from a plain program's by a relative error of at most 0.019.
Values may be sent and summed in bfloat16 or wider, within the bound.
No kernel may reach another device: no remote copies, remote signals or barrier semaphores. Data moves between devices by JAX's collectives and lax.ppermute only.
A program may use at most 128 MiB of HBM per device.

v0:
```python
import math

import jax
import jax.numpy as jnp
from jax import lax
from jax.sharding import PartitionSpec as P

HEAD_DIM = 128


EPS = 1e-06
THETA = 500000.0
NEG = -1e30


def joined_2(x, axis, combine):
    everything = jax.tree.map(lambda part: lax.all_gather(part, axis), x)
    initial = jax.tree.map(lambda part: part[0], everything)

    def step(k, so_far):
        return combine(so_far, jax.tree.map(lambda part: part[k], everything))

    return lax.fori_loop(1, lax.axis_size(axis), step, initial)


def ancestry(parents):
    number = parents.shape[-1]
    columns = jnp.arange(number, dtype=jnp.int32)
    single = (parents[:, :, None] == columns[None, None, :]).astype(jnp.float32)
    ancestors = jnp.eye(number, dtype=jnp.float32)[None] + single
    for repeat in range(max(1, (number - 1).bit_length())):
        ancestors = jnp.minimum(
            jnp.einsum("rij,rjk->rik", ancestors, ancestors, precision=lax.Precision.HIGHEST), 1.0
        )
    tree_depth = jnp.sum(ancestors, axis=-1) - 1.0
    return (ancestors, tree_depth)


def rotary(values, positions):
    half_dim = values.shape[-1] // 2
    freqs = THETA ** (-2.0 * jnp.arange(half_dim, dtype=jnp.float32) / values.shape[-1])
    angles = positions[:, None, None] * freqs[None, None, :]
    cosine = jnp.cos(angles)
    sine = jnp.sin(angles)
    first = values[..., :half_dim]
    second = values[..., half_dim:]
    return jnp.concatenate(
        [first * cosine - second * sine, second * cosine + first * sine], axis=-1
    )


def prepare(raw, square_sum, gain, positions, width_all):
    scaled = raw * lax.rsqrt(square_sum / width_all + EPS)[:, None] * gain[None, :]
    rows_here = raw.shape[0]
    heads_here = raw.shape[1] // HEAD_DIM
    turned = rotary(scaled.reshape(rows_here, heads_here, HEAD_DIM), positions)
    return turned.reshape(rows_here, heads_here * HEAD_DIM).astype(jnp.bfloat16)


def join_partials(first, second):
    peak_first, total_first, out_first = first
    peak_second, total_second, out_second = second
    highest = jnp.maximum(peak_first, peak_second)
    scale_first = jnp.exp(peak_first - highest)
    scale_second = jnp.exp(peak_second - highest)
    rows_here, heads_here = highest.shape
    joined = (
        out_first.reshape(rows_here, heads_here, -1) * scale_first[..., None]
        + out_second.reshape(rows_here, heads_here, -1) * scale_second[..., None]
    )
    return (
        highest,
        total_first * scale_first + total_second * scale_second,
        joined.reshape(out_first.shape),
    )


def body(
    hidden_in,
    query_weight,
    key_weight,
    value_weight,
    out_weight,
    query_gain,
    key_gain,
    post_gain,
    key_cache,
    value_cache,
    cache_lengths,
    parents,
    accepted_leaf,
):
    requests, block, local_width = key_cache.shape
    draft = parents.shape[1]
    tokens = requests * draft
    own_rows = hidden_in.shape[0]
    model_width = hidden_in.shape[1]
    heads_here = local_width // HEAD_DIM
    full_width = local_width * lax.axis_size("tp")
    seq_index = lax.axis_index("seq")
    tp_index = lax.axis_index("tp")
    row_start = seq_index * own_rows
    ancestors, tree_depth = ancestry(parents)
    positions = (cache_lengths[:, None].astype(jnp.float32) + tree_depth).reshape(tokens)
    piece = lax.all_gather(hidden_in, "seq", axis=0, tiled=True)
    raw = jnp.concatenate(
        [
            jnp.dot(piece, query_weight, preferred_element_type=jnp.float32),
            jnp.dot(piece, key_weight, preferred_element_type=jnp.float32),
            jnp.dot(piece, value_weight, preferred_element_type=jnp.float32),
        ],
        axis=1,
    )
    query_raw = raw[:, :local_width]
    key_raw = raw[:, local_width : 2 * local_width]
    value_raw = raw[:, 2 * local_width :]
    query_square, key_square = lax.psum(
        (jnp.sum(query_raw * query_raw, axis=1), jnp.sum(key_raw * key_raw, axis=1)), "tp"
    )
    queries = prepare(query_raw, query_square, query_gain, positions, full_width)
    keys = prepare(key_raw, key_square, key_gain, positions, full_width)
    values = value_raw.astype(jnp.bfloat16)
    factor = 1.0 / math.sqrt(HEAD_DIM)
    query_blocks = queries.reshape(requests, draft, heads_here, HEAD_DIM)
    cache_keys = key_cache.reshape(requests, block, heads_here, HEAD_DIM)
    cache_values = value_cache.reshape(requests, block, heads_here, HEAD_DIM)
    places = seq_index * block + jnp.arange(block, dtype=jnp.int32)
    cache_scores = (
        jnp.einsum("rihd,rlhd->rihl", query_blocks, cache_keys, preferred_element_type=jnp.float32)
        * factor
    )
    visible = (places[None, :] < cache_lengths[:, None])[:, None, None, :]
    cache_scores = jnp.where(visible, cache_scores, NEG)
    cache_peak = jnp.max(cache_scores, axis=-1)
    cache_weights = jnp.where(visible, jnp.exp(cache_scores - cache_peak[..., None]), 0.0)
    cache_total = jnp.sum(cache_weights, axis=-1).reshape(tokens, heads_here)
    cache_out = jnp.einsum(
        "rihl,rlhd->rihd",
        cache_weights,
        cache_values.astype(jnp.float32),
        precision=lax.Precision.HIGHEST,
    ).reshape(tokens, local_width)
    cache_peak = cache_peak.reshape(tokens, heads_here)
    request_now = row_start // draft
    own_queries_all = lax.dynamic_slice_in_dim(queries, row_start, own_rows).reshape(
        own_rows, heads_here, HEAD_DIM
    )
    request_keys = lax.dynamic_index_in_dim(
        keys.reshape(requests, draft, local_width), request_now, 0, keepdims=False
    ).reshape(draft, heads_here, HEAD_DIM)
    request_values = lax.dynamic_index_in_dim(
        values.reshape(requests, draft, local_width), request_now, 0, keepdims=False
    ).reshape(draft, heads_here, HEAD_DIM)
    tree_rows = lax.dynamic_slice_in_dim(ancestors.reshape(tokens, draft), row_start, own_rows)
    draft_scores = (
        jnp.einsum(
            "ihd,jhd->ihj", own_queries_all, request_keys, preferred_element_type=jnp.float32
        )
        * factor
    )
    tree_mask = (tree_rows > 0.5)[:, None, :]
    draft_scores = jnp.where(tree_mask, draft_scores, NEG)
    draft_peak = jnp.max(draft_scores, axis=-1)
    draft_weights = jnp.where(tree_mask, jnp.exp(draft_scores - draft_peak[..., None]), 0.0)
    draft_total = jnp.sum(draft_weights, axis=-1)
    draft_out = jnp.einsum(
        "ihj,jhd->ihd",
        draft_weights,
        request_values.astype(jnp.float32),
        precision=lax.Precision.HIGHEST,
    ).reshape(own_rows, local_width)
    merged = joined_2((cache_peak, cache_total, cache_out), "seq", join_partials)
    mine = tuple((lax.dynamic_slice_in_dim(member, row_start, own_rows) for member in merged))
    highest, denominator, summed = join_partials(mine, (draft_peak, draft_total, draft_out))
    attention = (
        (summed.reshape(own_rows, heads_here, HEAD_DIM) / denominator[..., None])
        .reshape(own_rows, local_width)
        .astype(jnp.bfloat16)
    )
    projected = jnp.dot(attention, out_weight, preferred_element_type=jnp.float32)
    feature_count = model_width // lax.axis_size("tp")
    summed_heads = lax.psum(projected, "tp")
    power = jnp.sum(summed_heads * summed_heads, axis=1)
    own_columns = lax.dynamic_slice_in_dim(summed_heads, tp_index * feature_count, feature_count, 1)
    normed = own_columns * lax.rsqrt(power / model_width + EPS)[:, None] * post_gain[None, :]
    residual_columns = lax.dynamic_slice_in_dim(
        hidden_in, tp_index * feature_count, feature_count, 1
    ).astype(jnp.float32)
    hidden_out = (residual_columns + normed).astype(jnp.bfloat16)
    leaf_onehot = (accepted_leaf[:, None] == jnp.arange(draft, dtype=jnp.int32)[None, :]).astype(
        jnp.float32
    )
    on_path = jnp.einsum("ri,rij->rj", leaf_onehot, ancestors, precision=lax.Precision.HIGHEST)
    target = cache_lengths[:, None] + tree_depth.astype(jnp.int32)
    placing = (places[None, :, None] == target[:, None, :]) & (on_path[:, None, :] > 0.5)
    written = jnp.any(placing, axis=-1)[..., None]
    placing_half = placing.astype(jnp.bfloat16)
    fresh_keys = jnp.einsum(
        "rpj,rjw->rpw",
        placing_half,
        keys.reshape(requests, draft, local_width),
        preferred_element_type=jnp.float32,
    ).astype(jnp.bfloat16)
    fresh_values = jnp.einsum(
        "rpj,rjw->rpw",
        placing_half,
        values.reshape(requests, draft, local_width),
        preferred_element_type=jnp.float32,
    ).astype(jnp.bfloat16)
    new_key_cache = jnp.where(written, fresh_keys, key_cache)
    new_value_cache = jnp.where(written, fresh_values, value_cache)
    return (hidden_out, new_key_cache, new_value_cache)


def solution(mesh):
    return jax.shard_map(
        body,
        mesh=mesh,
        in_specs=(
            P("seq", None),
            P(None, "tp"),
            P(None, "tp"),
            P(None, "tp"),
            P("tp", None),
            P("tp"),
            P("tp"),
            P("tp"),
            P(None, "seq", "tp"),
            P(None, "seq", "tp"),
            P(),
            P(),
            P(),
        ),
        out_specs=(P("seq", "tp"), P(None, "seq", "tp"), P(None, "seq", "tp")),
        check_vma=False,
    )
```

profile of v0, /device:TPU:0, one launch (start us, length us, event | category | flops | bytes accessed | tf_op | source)
XLA Modules:
  0.0 202.5 jit_solution(5932844091443974496)
XLA Ops:
  8.0 1.1 convolution_minimum_fusion.5
  12.0 41.0 %all-gather.3.cloned.1.call-done = bf16[256,2048]{1,0:T(8,128)(2,1)} async-done(((bf16[32,2048]{1,0:T(8,128)(2,1)}), bf16[256,2048]{1,0:T(8,128)(2,1)}) %all-gather.3.cloned.1.call-update) | async-done | bytes 1048592 | tf_op jit(solution)/shard_map/all_gather | solution.py:105
  53.0 2.2 %multiply_reduce_fusion.1 = (f32[256]{0:T(256)S(1)}, f32[256,512]{1,0:T(8,128)S(1)}) fusion(bf16[256,2048]{1,0:T(8,128)(2,1)} %all-gather.3.cloned.1.call-done, bf16[2048,512]{1,0:T(8,128)(2,1)S(1)} %copy-done), kind=kOutput, calls=%fused_computation.47 | convolution fusion | flops 537132800 | bytes 3671040 | tf_op jit(solution)/shard_map/dot_general | solution.py:108
  55.2 1.5 multiply_reduce_fusion
  56.7 5.6 %all-reduce = (f32[256]{0:T(256)S(1)}, f32[256]{0:T(256)S(1)}) all-reduce(f32[256]{0:T(256)S(1)} %get-tuple-element.217, f32[256]{0:T(256)S(1)} %get-tuple-element.219), channel_id=1, replica_groups=mesh['seq'=8,'tp'=4] {'tp'}, use_global_device_ids=true, to_apply=%region_1.0 | all-reduce | flops 512 | bytes 4096 | tf_op jit(solution)/shard_map/psum | solution.py:117
  66.0 1.0 all_gather_reshape.11
  69.1 2.7 %convolution_convert_fusion.2 = bf16[256,512]{1,0:T(8,128)(2,1)S(1)} fusion(bf16[256,2048]{1,0:T(8,128)(2,1)} %all-gather.3.cloned.1.call-done, bf16[2048,512]{1,0:T(8,128)(2,1)} %param.18), kind=kOutput, calls=%fused_computation.17 | convolution fusion | flops 537001984 | bytes 3407872 | tf_op jit(solution)/shard_map/dot_general | solution.py:110
  74.8 30.9 %all_gather.13 = f32[8,256,4]{1,2,0:T(4,128)S(1)} all-gather(f32[1,256,4]{1,2,0:T(4,128)S(1)} %all_gather_reshape.9), channel_id=1, replica_groups=mesh['seq'=8,'tp'=4] {'seq'}, dimensions={0}, use_global_device_ids=true | all-gather | bytes 36864 | tf_op jit(solution)/shard_map/all_gather | solution.py:17
  105.7 30.7 %all_gather.14 = f32[8,256,4]{1,2,0:T(4,128)S(1)} all-gather(f32[1,256,4]{1,2,0:T(4,128)S(1)} %all_gather_reshape.10), channel_id=1, replica_groups=mesh['seq'=8,'tp'=4] {'seq'}, dimensions={0}, use_global_device_ids=true | all-gather | bytes 36864 | tf_op jit(solution)/shard_map/all_gather | solution.py:17
  137.6 2.3 %fusion.3 = bf16[4,128,512]{2,1,0:T(8,128)(2,1)} fusion(bf16[4,128,512]{2,1,0:T(8,128)(2,1)} %param.23, bf16[4,64,512]{2,1,0:T(8,128)(2,1)S(1)} %convert_element_type.67, pred[4,128]{1,0:T(4,128)(4,1)} %fusion.25, s32[4,64]{1,0:T(4,128)S(1)} %convert_add_fusion, s32[128]{0:T(128)} %copy-done.12, pred[4,64]{1,0:T(4,128)(4,1)} %copy-done.11), kind=kOutput, calls=%fused_computation.11 | convolution fusion | flops 34144256 | bytes 1313024 | tf_op jit(solution)/shard_map/rpj,rjw->rpw/dot_general | solution.py:198
  140.3 1.1 slice_bitcast_fusion
  141.4 16.7 %while.19 = (s32[]{:T(128)}, f32[256,4]{0,1:T(4,128)S(1)}, f32[256,4]{0,1:T(4,128)S(1)}, f32[256,512]{1,0:T(8,128)S(1)}, f32[8,256,4]{1,2,0:T(4,128)S(1)}, /*ind...) while((s32[]{:T(128)}, f32[256,4]{0,1:T(4,128)S(1)}, ...), condition=%wide.region_6.7_spmd, body=%wide.region_5.6_spmd.sunk | while | flops 399365 | bytes 3727511 | solution.py:23
  142.4 1.4 fusion.87
  144.8 1.4 fusion.87
  147.2 1.4 fusion.87
  149.6 1.4 fusion.87
  152.0 1.4 fusion.87
  154.4 1.4 fusion.87
  156.8 1.4 fusion.87
  160.0 2.8 %fusion.37 = f32[32,2048]{1,0:T(8,128)} fusion(bf16[512,2048]{1,0:T(8,128)(2,1)} %param.19, bf16[4,4,8,128]{3,2,1,0:T(8,128)(2,1)S(1)} %fusion.13), kind=kOutput, calls=%fused_computation.77 | convolution fusion | flops 67108864 | bytes 2392064 | tf_op jit(solution)/shard_map/dot_general | solution.py:180
  162.8 2.0 fusion.4
  164.7 28.5 %all-reduce.3.cloned.1.call-done = f32[32,2048]{1,0:T(8,128)} async-done(((f32[32,2048]{1,0:T(8,128)}), f32[32,2048]{1,0:T(8,128)}) %all-reduce.3.cloned.1.call-update) | async-done | bytes 262160 | tf_op jit(solution)/shard_map/psum | solution.py:182
  193.3 1.1 multiply_reduce_fusion.2
  194.4 1.5 add_convert_fusion.1
  (145 shorter events, 22.2 us)
Async XLA Ops:
  7.2 45.9 %copy-start = (bf16[2048,512]{1,0:T(8,128)(2,1)S(1)}, bf16[2048,512]{1,0:T(8,128)(2,1)}, u32[]{:S(2)}) copy-start(bf16[2048,512]{1,0:T(8,128)(2,1)} %param.16) | copy-start | bytes 6291460
  7.2 4.2 %copy-start.20 = (s32[4]{0:T(128)S(1)}, s32[4]{0:T(128)}, u32[]{:S(2)}) copy-start(s32[4]{0:T(128)} %param.25) | copy-start | bytes 52
  7.2 45.8 %all-gather.3.cloned.1.call-start = ((), (), s32[]{:S(2)}) async-start(), calls=%async_computation | async-start | bytes 1179648 | tf_op jit(solution)/shard_map/all_gather | solution.py:105
  7.9 132.4 %all-gather.5.cloned.1.call-start = ((), (), s32[]{:S(2)}) async-start(), calls=%async_computation.1 | async-start | bytes 4718592 | tf_op jit(solution)/shard_map/all_gather | solution.py:17
  11.5 53.4 %copy-start.18 = (pred[4,128]{1,0:T(4,128)(4,1)}, pred[4,128]{1,0:T(4,128)(4,1)S(1)}, u32[]{:S(2)}) copy-start(pred[4,128]{1,0:T(4,128)(4,1)S(1)} %broadcast_compare_fusion.1) | copy-start | bytes 1540
  53.0 2.2 %copy-start.22 = (bf16[2048,512]{1,0:T(8,128)(2,1)S(1)}, bf16[2048,512]{1,0:T(8,128)(2,1)}, u32[]{:S(2)}) copy-start(bf16[2048,512]{1,0:T(8,128)(2,1)} %param.17) | copy-start | bytes 6291460
  53.0 2.2 %copy-start.23 = (bf16[256,2048]{1,0:T(8,128)(2,1)S(1)}, bf16[256,2048]{1,0:T(8,128)(2,1)}, u32[]{:S(2)}) copy-start(bf16[256,2048]{1,0:T(8,128)(2,1)} %all-gather.3.cloned.1.call-done) | copy-start | bytes 3145732
  55.2 7.7 %copy-start.15 = (f32[512]{0:T(512)S(1)}, f32[512]{0:T(512)}, u32[]{:S(2)}) copy-start(f32[512]{0:T(512)} %param.20) | copy-start | bytes 6148
  63.6 1.3 copy-start.1
  64.9 2.3 %copy-start.24 = (s32[4]{0:T(128)S(1)}, s32[4]{0:T(128)}, u32[]{:S(2)}) copy-start(s32[4]{0:T(128)} %param.27) | copy-start | bytes 52
  64.9 2.5 %copy-start.21 = (s32[4]{0:T(128)S(1)}, s32[4]{0:T(128)}, u32[]{:S(2)}) copy-start(s32[4]{0:T(128)} %param.25) | copy-start | bytes 52
  64.9 2.6 %copy-start.13 = (s32[128]{0:T(128)S(1)}, s32[128]{0:T(128)}, u32[]{:S(2)}) copy-start(s32[128]{0:T(128)} %copy-done.12) | copy-start | bytes 1540
  67.0 126.2 %all-reduce.3.cloned.1.call-start = ((), (), s32[]{:S(2)}) async-start(), calls=%async_computation.2 | async-start | bytes 524288 | tf_op jit(solution)/shard_map/psum | solution.py:182
  67.4 4.4 %copy-start.11 = (pred[4,64]{1,0:T(4,128)(4,1)}, pred[4,64]{1,0:T(4,128)(4,1)S(1)}, u32[]{:S(2)}) copy-start(pred[4,64]{1,0:T(4,128)(4,1)S(1)} %broadcast_compare_fusion) | copy-start | bytes 772
  69.1 3.4 %copy-start.6 = (f32[256,512]{1,0:T(8,128)S(1)}, f32[256,512]{1,0:T(8,128)}, u32[]{:S(2)}) copy-start(f32[256,512]{1,0:T(8,128)} %get-tuple-element.220) | copy-start | bytes 1572868
  69.1 3.4 %copy-start.14 = (f32[256]{0:T(256)S(1)}, f32[256]{0:T(256)}, u32[]{:S(2)}) copy-start(f32[256]{0:T(256)} %get-tuple-element.227) | copy-start | bytes 3076
  69.1 3.4 %copy-start.16 = (f32[512]{0:T(512)S(1)}, f32[512]{0:T(512)}, u32[]{:S(2)}) copy-start(f32[512]{0:T(512)} %param.21) | copy-start | bytes 6148
  73.2 1.1 copy-start.4
  73.2 1.1 copy-start.19
  73.4 63.0 %copy-start.5 = (bf16[256,4,128]{0,2,1:T(8,128)(2,1)S(1)}, bf16[256,4,128]{0,2,1:T(8,128)(2,1)}, u32[]{:S(2)}) copy-start(bf16[256,4,128]{0,2,1:T(8,128)(2,1)} %copy.129) | copy-start | bytes 786436
  136.8 4.6 %copy-start.10 = (f32[32,4]{0,1:T(4,128)}, f32[32,4]{0,1:T(4,128)S(1)}, u32[]{:S(2)}) copy-start(f32[32,4]{0,1:T(4,128)S(1)} %get-tuple-element.225) | copy-start | bytes 1540
  158.2 4.6 %copy-start.2 = (bf16[4,128,512]{2,1,0:T(8,128)(2,1)S(1)}, bf16[4,128,512]{2,1,0:T(8,128)(2,1)}, u32[]{:S(2)}) copy-start(bf16[4,128,512]{2,1,0:T(8,128)(2,1)} %param.24) | copy-start | bytes 1572868
  158.2 4.6 %copy-start.9 = (bf16[256,512]{1,0:T(8,128)(2,1)S(1)}, bf16[256,512]{1,0:T(8,128)(2,1)}, u32[]{:S(2)}) copy-start(bf16[256,512]{1,0:T(8,128)(2,1)} %copy-done.8) | copy-start | bytes 786436
  160.0 34.4 %copy-start.17 = (f32[512]{0:T(512)S(1)}, f32[512]{0:T(512)}, u32[]{:S(2)}) copy-start(f32[512]{0:T(512)} %param.22) | copy-start | bytes 6148
  (4 other events, 3.2 us)
Sparse Core Ops, SparseCore 0:
  10.2 42.8 all-gather.2
  67.2 73.1 all-gather.4
  162.9 30.3 all-reduce.2
where the time goes:
time: 203 us; the launch traced here: 202 us
  waiting for transfers between devices  70.7 us (35%)
  blocking collectives  67.2 us (33%)
  matrix products  18.4 us (9%)
  other arithmetic  18.1 us (9%)
  between operations  14.3 us (7%)
  local copies, waits for them, and re-layouts  13.3 us (7%)
    all_gather x2, blocking collectives, joined_2(): everything = jax.tree.map(lambda part: lax.all_gather(part, axis), x)  61.6 us
    all_gather x1, waiting for transfers between devices, body(): piece = lax.all_gather(hidden_in, 'seq', axis=0, tiled=True)  41 us
    psum x1, waiting for transfers between devices, body(): summed_heads = lax.psum(projected, 'tp')  28.5 us
    add x7, other arithmetic, join_partials(): out_first.reshape(rows_here, heads_here, -1) * scale_first[..., None]  9.66 us
    psum x1, blocking collectives, body(): lax.psum((jnp.sum(query_raw * query_raw, axis=1), jnp.sum(key_raw * key_r...  5.63 us
  transfers between devices with their start and end apart: 3, of which 3 were waited for; matrix products, arithmetic and copies ran while one was open for 8% of the time, Pallas kernels for 0%

commit v1 on v0

v1 whole, which is shorter than its diff:
```python
import functools
import math

import jax
import jax.numpy as jnp
from jax import lax
from jax.experimental import pallas as pl
from jax.experimental.pallas import tpu as pltpu
from jax.sharding import PartitionSpec as P

HEAD_DIM = 128
LANES = 128
EPS = 1e-06
THETA = 500000.0
NEG = -1e30
F32 = jnp.float32
BF16 = jnp.bfloat16
VMEM = pl.BlockSpec(memory_space=pltpu.VMEM)
SMEM = pl.BlockSpec(memory_space=pltpu.SMEM)
ANY = pl.BlockSpec(memory_space=pl.ANY)


def params(mib):
    return pltpu.CompilerParams(vmem_limit_bytes=mib * 1024 * 1024)


def dot(a, b):
    return jnp.dot(a, b, preferred_element_type=F32)


def dot_t(a, b):
    return lax.dot_general(a, b, (((1,), (1,)), ((), ())), preferred_element_type=F32)


def iota(shape, axis):
    return lax.broadcasted_iota(jnp.int32, shape, axis)


def stacked(parts):
    if len(parts) == 1:
        return parts[0]
    if parts[0].shape[0] % 16 == 0:
        return jnp.concatenate(parts, axis=0)
    return jnp.concatenate([part.astype(F32) for part in parts], axis=0).astype(BF16)


def sum_squares(raw):
    return jnp.sum(raw * raw, axis=1, keepdims=True)


def project_qk(hidden, wq, wk, query_raw, key_raw, squares, wq_v, wk_v, sems):
    chunks, depth = wq_v.shape[0], wq_v.shape[1]
    copies = []
    for c in range(chunks):
        for at, (source, target) in enumerate(((wq, wq_v), (wk, wk_v))):
            copy = pltpu.make_async_copy(
                source.at[pl.ds(c * depth, depth)], target.at[c], sems.at[2 * c + at]
            )
            copy.start()
            copies.append(copy)
    q_sum, k_sum = None, None
    for c in range(chunks):
        part = hidden[:, c * depth : (c + 1) * depth]
        copies[2 * c].wait()
        q = dot(part, wq_v[c])
        copies[2 * c + 1].wait()
        k = dot(part, wk_v[c])
        q_sum = q if c == 0 else q_sum + q
        k_sum = k if c == 0 else k_sum + k
    query_raw[...] = q_sum
    key_raw[...] = k_sum
    lane = iota(squares.shape[1:], 1)
    both = jnp.where(lane == 0, sum_squares(q_sum), sum_squares(k_sum))
    for t in range(squares.shape[0]):
        squares[t] = both


def project_v_and_tree(
    lengths, leaves, hidden, parents, freqs, wv, value, own_tree, targets, cosine, sine, wv_v, anc_v, sems
):
    chunks, depth = wv_v.shape[0], wv_v.shape[1]
    copies = []
    for c in range(chunks):
        copy = pltpu.make_async_copy(wv.at[pl.ds(c * depth, depth)], wv_v.at[c], sems.at[c])
        copy.start()
        copies.append(copy)
    requests, draft = parents.shape
    own = hidden.shape[0]
    first = lax.axis_index("seq") * own
    row, col = iota((draft, draft), 0), iota((draft, draft), 1)
    eye = (row == col).astype(BF16)
    trees = [
        jnp.where((parents[pl.ds(r, 1), :] == row) | (row == col), 1.0, 0.0).astype(BF16)
        for r in range(requests)
    ]
    for _ in range(max(1, (draft - 1).bit_length())):
        trees = [jnp.minimum(dot(tree, tree), 1.0).astype(BF16) for tree in trees]
    for r in range(requests):
        upright = lax.dot_general(
            trees[r], eye, (((0,), (0,)), ((), ())), preferred_element_type=F32
        )
        anc_v[pl.ds(r * draft, draft), :] = upright
        level = jnp.sum(trees[r].astype(F32), axis=0, keepdims=True) - 1.0
        on_path = jnp.sum(jnp.where(row == leaves[r], upright, 0.0), axis=0, keepdims=True)
        place = lengths[r] + level.astype(jnp.int32)
        targets[r] = jnp.where(on_path > 0.5, place, -1)
    mine = anc_v[pl.ds(pl.multiple_of(first, own), own), :]
    own_tree[...] = mine
    level = jnp.sum(mine, axis=1, keepdims=True) - 1.0
    position = lengths[first // draft].astype(F32) + level
    angles = position * freqs[...]
    cosine[...] = jnp.cos(angles)
    half = jnp.sin(angles)
    sine[...] = jnp.where(iota(half.shape, 1) < HEAD_DIM // 2, -half, half)
    total = None
    for c in range(chunks):
        copies[c].wait()
        v = dot(hidden[:, c * depth : (c + 1) * depth], wv_v[c])
        total = v if c == 0 else total + v
    value[...] = total.astype(BF16)


def prepare(
    width_all, query_raw, key_raw, value, q_gain, k_gain, cosine, sine, squares, queries, keys_values
):
    width = query_raw.shape[1]
    total = sum(squares[k] for k in range(squares.shape[0]))
    cos, sin = cosine[...], sine[...]
    for at, (raw, gain, out) in enumerate(
        ((query_raw, q_gain, queries), (key_raw, k_gain, keys_values))
    ):
        scale = lax.rsqrt(total[:, at : at + 1] / width_all + EPS)
        for h in range(width // HEAD_DIM):
            lanes = slice(h * HEAD_DIM, (h + 1) * HEAD_DIM)
            x = raw[:, lanes] * scale * gain[:, lanes]
            turned = x * cos + pltpu.roll(x, HEAD_DIM // 2, 1) * sin
            turned = turned.astype(BF16)
            for s in range(out.shape[0]):
                out[s, :, lanes] = turned
    for s in range(keys_values.shape[0]):
        keys_values[s, :, width:] = value[...]


def attend_cache(group, lengths, key_cache, value_cache, queries, partials):
    requests, block, width = key_cache.shape
    own = queries.shape[1]
    heads = width // HEAD_DIM
    me = lax.axis_index("seq")
    factor = 1.0 / math.sqrt(HEAD_DIM)
    rows = group * own
    place = me * block + iota((rows, block), 1)
    lane = iota((rows, LANES), 1)
    for request in range(requests):
        q = stacked([queries[request * group + j] for j in range(group)])
        visible = place < lengths[request]
        stats = jnp.zeros((rows, LANES), F32)
        for h in range(heads):
            lanes = slice(h * HEAD_DIM, (h + 1) * HEAD_DIM)
            scores = dot_t(q[:, lanes], key_cache[request, :, lanes]) * factor
            scores = jnp.where(visible, scores, NEG)
            peak = jnp.max(scores, axis=1, keepdims=True).astype(BF16).astype(F32)
            weights = jnp.exp(jnp.where(visible, scores - peak, NEG))
            total = jnp.sum(weights, axis=1, keepdims=True)
            high = total.astype(BF16).astype(F32)
            out = dot(weights.astype(BF16), value_cache[request, :, lanes]).astype(BF16)
            for j in range(group):
                partials[request * group + j, :, lanes] = out[j * own : (j + 1) * own]
            stats = jnp.where(lane == h, peak, stats)
            stats = jnp.where(lane == heads + h, high, stats)
            stats = jnp.where(lane == 2 * heads + h, total - high, stats)
        stats = stats.astype(BF16)
        for j in range(group):
            partials[request * group + j, :, width:] = stats[j * own : (j + 1) * own]


def attend_draft(group, own_tree, queries, keys_values, out, stats):
    own, width = queries.shape[1:]
    heads = width // HEAD_DIM
    me = lax.axis_index("seq")
    first = me // group * group
    q = queries[me]
    pair = stacked([keys_values[first + j] for j in range(group)])
    factor = 1.0 / math.sqrt(HEAD_DIM)
    allowed = own_tree[...] > 0.5
    lane = iota((own, LANES), 1)
    kept = jnp.zeros((own, LANES), F32)
    for h in range(heads):
        lanes = slice(h * HEAD_DIM, (h + 1) * HEAD_DIM)
        there = slice(width + h * HEAD_DIM, width + (h + 1) * HEAD_DIM)
        scores = dot_t(q[:, lanes], pair[:, lanes]) * factor
        scores = jnp.where(allowed, scores, NEG)
        peak = jnp.max(scores, axis=1, keepdims=True)
        weights = jnp.exp(jnp.where(allowed, scores - peak, NEG))
        out[:, lanes] = dot(weights.astype(BF16), pair[:, there])
        kept = jnp.where(lane == h, peak, kept)
        kept = jnp.where(lane == heads + h, jnp.sum(weights, axis=1, keepdims=True), kept)
    stats[...] = kept


def merge_and_project(draft_out, draft_stats, wo, partials, projected, wo_v, sems):
    count, width, columns = wo_v.shape
    heads = width // HEAD_DIM
    copies = []
    for k in range(count):
        copy = pltpu.make_async_copy(
            wo.at[:, pl.ds(k * columns, columns)], wo_v.at[k], sems.at[k]
        )
        copy.start()
        copies.append(copy)
    parts = range(partials.shape[0])
    stats = [partials[s, :, width:].astype(F32) for s in parts]
    own_stats = draft_stats[...]
    attention = []
    for h in range(heads):
        lanes = slice(h * HEAD_DIM, (h + 1) * HEAD_DIM)
        peaks = [s[:, h : h + 1] for s in stats] + [own_stats[:, h : h + 1]]
        highest = functools.reduce(jnp.maximum, peaks)
        scales = [jnp.exp(peak - highest) for peak in peaks]
        total = own_stats[:, heads + h : heads + h + 1] * scales[-1]
        summed = draft_out[:, lanes] * scales[-1]
        for at in parts:
            s = stats[at]
            own_total = s[:, heads + h : heads + h + 1] + s[:, 2 * heads + h : 2 * heads + h + 1]
            total = total + own_total * scales[at]
            summed = summed + partials[at, :, lanes].astype(F32) * scales[at]
        attention.append((summed / total).astype(BF16))
    attention = jnp.concatenate(attention, axis=1)
    for k in range(count):
        copies[k].wait()
        projected[k] = dot(attention, wo_v[k]).astype(projected.dtype)


def add_up(parts, summed, power):
    total = sum(parts[k].astype(F32) for k in range(parts.shape[0]))
    summed[...] = total
    own_power = jnp.broadcast_to(sum_squares(total), power.shape[1:])
    for k in range(power.shape[0]):
        power[k] = own_power


def finish(model_width, summed, gain, hidden, powers, out):
    columns = summed.shape[1]
    power = sum(powers[k] for k in range(powers.shape[0]))[:, :1]
    start = pl.multiple_of(lax.axis_index("tp") * columns, columns)
    normed = summed[...] * lax.rsqrt(power / model_width + EPS) * gain[...]
    out[...] = (hidden[:, pl.ds(start, columns)].astype(F32) + normed).astype(BF16)


def compact(group, targets, key_cache, value_cache, keys_values, new_keys, new_values):
    requests, block, width = key_cache.shape
    own = keys_values.shape[1]
    me = lax.axis_index("seq")
    place = me * block + iota((block, group * own), 0)
    for request in range(requests):
        kv = stacked([keys_values[request * group + j] for j in range(group)])
        placing = place == targets[request]
        written = jnp.max(placing.astype(F32), axis=1, keepdims=True) > 0.5
        fresh = dot(placing.astype(BF16), kv)
        new_keys[request] = jnp.where(
            written, fresh[:, :width], key_cache[request].astype(F32)
        ).astype(BF16)
        new_values[request] = jnp.where(
            written, fresh[:, width:], value_cache[request].astype(F32)
        ).astype(BF16)


def shaped(shape, dtype):
    return jax.ShapeDtypeStruct(shape, dtype)


def body_general(
    hidden_in,
    query_weight,
    key_weight,
    value_weight,
    out_weight,
    query_gain,
    key_gain,
    post_gain,
    key_cache,
    value_cache,
    cache_lengths,
    parents,
    accepted_leaf,
):
    requests, block, width = key_cache.shape
    draft = parents.shape[1]
    own, model = hidden_in.shape
    tp = lax.axis_size("tp")
    seq = lax.axis_size("seq")
    group = draft // own
    columns = model // tp
    chunks = 4
    depth = model // chunks

    def exchange(x, axis):
        return lax.all_to_all(x, axis, 0, 0, tiled=True)

    query_raw, key_raw, squares = pl.pallas_call(
        project_qk,
        out_shape=(
            shaped((own, width), F32),
            shaped((own, width), F32),
            shaped((tp, own, LANES), F32),
        ),
        in_specs=[VMEM, ANY, ANY],
        out_specs=(VMEM, VMEM, VMEM),
        scratch_shapes=[
            pltpu.VMEM((chunks, depth, width), BF16),
            pltpu.VMEM((chunks, depth, width), BF16),
            pltpu.SemaphoreType.DMA((2 * chunks,)),
        ],
        compiler_params=params(56),
        cost_estimate=pl.CostEstimate(
            flops=4 * own * model * width, bytes_accessed=4 * model * width, transcendentals=0
        ),
        name="project_qk",
    )(hidden_in, query_weight, key_weight)
    squares = exchange(squares, "tp")

    exponents = -2.0 * (jnp.arange(HEAD_DIM) % (HEAD_DIM // 2)).astype(F32) / HEAD_DIM
    freqs = (THETA**exponents)[None, :]
    value, own_tree, targets, cosine, sine = pl.pallas_call(
        project_v_and_tree,
        out_shape=(
            shaped((own, width), BF16),
            shaped((own, draft), F32),
            shaped((requests, 1, draft), jnp.int32),
            shaped((own, HEAD_DIM), F32),
            shaped((own, HEAD_DIM), F32),
        ),
        in_specs=[SMEM, SMEM, VMEM, VMEM, VMEM, ANY],
        out_specs=(VMEM,) * 5,
        scratch_shapes=[
            pltpu.VMEM((chunks, depth, width), BF16),
            pltpu.VMEM((requests * draft, draft), F32),
            pltpu.SemaphoreType.DMA((chunks,)),
        ],
        compiler_params=params(16),
        cost_estimate=pl.CostEstimate(
            flops=2 * own * model * width, bytes_accessed=2 * model * width, transcendentals=0
        ),
        name="project_v_and_tree",
    )(cache_lengths, accepted_leaf, hidden_in, parents, freqs, value_weight)

    queries, keys_values = pl.pallas_call(
        functools.partial(prepare, tp * width),
        out_shape=(shaped((seq, own, width), BF16), shaped((seq, own, 2 * width), BF16)),
        in_specs=[VMEM] * 8,
        out_specs=(VMEM, VMEM),
        compiler_params=params(16),
        name="prepare",
    )(
        query_raw,
        key_raw,
        value,
        query_gain[None, :],
        key_gain[None, :],
        cosine,
        sine,
        squares,
    )
    queries = exchange(queries, "seq")
    keys_values = exchange(keys_values, "seq")

    partials = pl.pallas_call(
        functools.partial(attend_cache, group),
        out_shape=shaped((seq, own, width + LANES), BF16),
        in_specs=[SMEM, VMEM, VMEM, VMEM],
        out_specs=VMEM,
        compiler_params=params(16),
        name="attend_cache",
    )(cache_lengths, key_cache, value_cache, queries)
    partials = exchange(partials, "seq")

    draft_out, draft_stats = pl.pallas_call(
        functools.partial(attend_draft, group),
        out_shape=(shaped((own, width), F32), shaped((own, LANES), F32)),
        in_specs=[VMEM] * 3,
        out_specs=(VMEM, VMEM),
        compiler_params=params(16),
        name="attend_draft",
    )(own_tree, queries, keys_values)

    projected = pl.pallas_call(
        merge_and_project,
        out_shape=shaped((tp, own, columns), BF16),
        in_specs=[VMEM, VMEM, ANY, VMEM],
        out_specs=VMEM,
        scratch_shapes=[
            pltpu.VMEM((tp, width, columns), BF16),
            pltpu.SemaphoreType.DMA((tp,)),
        ],
        compiler_params=params(16),
        name="merge_and_project",
    )(draft_out, draft_stats, out_weight, partials)
    projected = exchange(projected, "tp")

    summed, power = pl.pallas_call(
        add_up,
        out_shape=(shaped((own, columns), F32), shaped((tp, own, LANES), F32)),
        in_specs=[VMEM],
        out_specs=(VMEM, VMEM),
        compiler_params=params(16),
        name="add_up",
    )(projected)
    power = exchange(power, "tp")

    hidden_out = pl.pallas_call(
        functools.partial(finish, model),
        out_shape=shaped((own, columns), BF16),
        in_specs=[VMEM] * 4,
        out_specs=VMEM,
        compiler_params=params(16),
        name="finish",
    )(summed, post_gain[None, :], hidden_in, power)

    new_key_cache, new_value_cache = pl.pallas_call(
        functools.partial(compact, group),
        out_shape=(shaped(key_cache.shape, BF16), shaped(value_cache.shape, BF16)),
        in_specs=[VMEM] * 4,
        out_specs=(VMEM, VMEM),
        compiler_params=params(24),
        name="compact",
    )(targets, key_cache, value_cache, keys_values)
    return (hidden_out, new_key_cache, new_value_cache)


def across(column):
    rows = column.shape[0]
    eye = iota((rows, rows), 0) == iota((rows, rows), 1)
    return jnp.sum(jnp.where(eye, column, 0.0), axis=0, keepdims=True)


def upright(line):
    rows = line.shape[1]
    eye = iota((rows, rows), 0) == iota((rows, rows), 1)
    return jnp.sum(jnp.where(eye, line, 0.0), axis=1, keepdims=True)


def eye_of(size):
    return (iota((size, size), 0) == iota((size, size), 1)).astype(BF16)


def plane():
    return lax.axis_index("seq") // 2


def twin_load(wq, wk, wq_v, wk_v, sems):
    chunks = sems.shape[1]
    depth = wq.shape[0] // chunks
    copies = []
    for at, (source, target) in enumerate(((wq, wq_v), (wk, wk_v))):
        for c in range(chunks):
            rows = pl.ds(c * depth, depth)
            copies.append(
                pltpu.make_async_copy(source.at[rows], target.at[rows], sems.at[at, c])
            )
    for copy in copies:
        copy.start()
    for copy in copies:
        copy.wait()


def twin_project_qk(hidden, wq, wk, query_raw, key_raw, squares):
    rows = hidden[...]
    own = rows.shape[0]
    for at, (weight, raw) in enumerate(((wq, query_raw), (wk, key_raw))):
        product = dot(rows, weight[...])
        raw[...] = product
        line = across(sum_squares(product))
        line = jnp.concatenate([line, jnp.zeros((1, LANES - own), F32)], axis=1)
        squares[:, at * LANES : (at + 1) * LANES] = jnp.broadcast_to(
            line, (squares.shape[0], LANES)
        )


def twin_project_v(hidden, wv, value):
    value[...] = dot(hidden[...], wv[...]).astype(BF16)


def twin_tree(
    turns, lengths, leaves, parents, freqs, own_tree, targets, cosine, sine, limits, held
):
    requests, draft = parents.shape
    own = own_tree.shape[1]
    row, col = iota((draft, draft), 0), iota((draft, draft), 1)
    eye = eye_of(draft)

    def length_of(request):
        picked = iota(lengths.shape, 1) == request
        return jnp.sum(jnp.where(picked, lengths[...], 0), axis=1, keepdims=True)

    for at, turn in enumerate(turns):
        limits[at : at + 1, :] = jnp.broadcast_to(
            length_of(plane() ^ turn), (1, limits.shape[1])
        )
    trees = [
        jnp.where((parents[pl.ds(r, 1), :] == row) | (row == col), 1.0, 0.0).astype(BF16)
        for r in range(requests)
    ]
    for _ in range(max(1, (draft - 1).bit_length())):
        trees = [jnp.minimum(dot(tree, tree), 1.0).astype(BF16) for tree in trees]
    for r in range(requests):
        standing = lax.dot_general(
            trees[r], eye, (((0,), (0,)), ((), ())), preferred_element_type=F32
        )
        held[r] = standing
        level = jnp.sum(trees[r].astype(F32), axis=0, keepdims=True) - 1.0
        on_path = jnp.where(row == leaves[:, r : r + 1], standing, 0.0)
        on_path = jnp.sum(on_path, axis=0, keepdims=True)
        place = lengths[:, r : r + 1] + level.astype(jnp.int32)
        targets[r] = jnp.where(on_path > 0.5, place, -1)
    within = lax.rem(lax.axis_index("seq"), 2)
    for at in range(2):
        first = (within ^ at) * own
        rows = held[plane(), pl.ds(pl.multiple_of(first, own), own), :]
        own_tree[at * own : (at + 1) * own, :] = jnp.where(
            within == 0, rows[:, :own], rows[:, own:]
        )
        mine = rows if at == 0 else mine
    level = jnp.sum(mine, axis=1, keepdims=True) - 1.0
    angles = (length_of(plane()).astype(F32) + level) * freqs[...]
    cosine[...] = jnp.cos(angles)
    half = jnp.sin(angles)
    sine[...] = jnp.where(iota(half.shape, 1) < HEAD_DIM // 2, -half, half)


def turned(raw, scale, gain, cos, sin):
    x = raw * scale * gain
    return (x * cos + pltpu.roll(x, HEAD_DIM // 2, 1) * sin).astype(BF16)


def twin_prepare(width_all, query_raw, key_raw, value, q_gain, k_gain, cosine, sine, *refs):
    squares, (queries, packed) = refs[:-2], refs[-2:]
    own, width = query_raw.shape
    cos, sin = cosine[...], sine[...]
    total = sum(ref[:1, :] for ref in squares)
    for at, (raw, gain) in enumerate(((query_raw, q_gain), (key_raw, k_gain))):
        scale = upright(total[:, at * LANES : at * LANES + own])
        scale = lax.rsqrt(scale / width_all + EPS)
        for h in range(width // HEAD_DIM):
            lanes = slice(h * HEAD_DIM, (h + 1) * HEAD_DIM)
            there = slice(at * width + h * HEAD_DIM, at * width + (h + 1) * HEAD_DIM)
            found = turned(raw[:, lanes], scale, gain[:, lanes], cos, sin)
            packed[:, there] = found
            if at == 0:
                queries[:, lanes] = found
    packed[:, 2 * width :] = value[...]


def weigh(s, visible):
    peak = jnp.max(s, axis=1, keepdims=True).astype(BF16).astype(F32)
    weights = jnp.exp(jnp.where(visible, s - peak, NEG))
    total = jnp.sum(weights, axis=1, keepdims=True)
    high = total.astype(BF16).astype(F32)
    return weights.astype(BF16), (peak, high, total - high)


def kept(stats, h, heads, found):
    lane = iota(stats.shape, 1)
    for at, column in enumerate(found):
        stats = jnp.where(lane == at * heads + h, column, stats)
    return stats


def write_stats(stats, out):
    own, width = stats.shape[0], out.shape[1]
    flat = lax.dot_general(
        stats.astype(BF16), eye_of(own), (((0,), (0,)), ((), ())), preferred_element_type=F32
    )
    flat = jnp.concatenate([flat[:16], jnp.zeros((16, width - own), F32)], axis=1)
    out[own : own + 16, :] = flat.astype(BF16)


def twin_attend(far, limits, key_cache, value_cache, swapped, own_tree, mine, other, *refs):
    count = len(far)
    queries, outs = refs[:count], refs[count : 2 * count]
    crossing, local, scores, own_scores = refs[2 * count :]
    block, width = key_cache.shape[1:]
    heads = width // HEAD_DIM
    own = other.shape[0]
    me = lax.axis_index("seq")
    factor = 1.0 / math.sqrt(HEAD_DIM)
    place = iota((1, block), 1)
    both = jnp.concatenate([me * block + place, (me ^ 1) * block + place], axis=1)
    visible = [both < limits[at + 1 : at + 2, :] for at in range(count)]
    here = jnp.broadcast_to((me * block + place) < limits[:1, :block], (2 * own, block))
    near = jnp.concatenate(
        [
            jnp.where(here, 1.0, 0.0),
            own_tree[...],
            jnp.zeros((2 * own, own_scores.shape[2] - block - own), F32),
        ],
        axis=1,
    )
    near = near > 0.5
    for at, turn in enumerate(far):
        for h in range(heads):
            lanes = slice(h * HEAD_DIM, (h + 1) * HEAD_DIM)
            q = queries[at][:, lanes]
            first = dot_t(q, key_cache[plane() ^ turn, :, lanes])
            second = dot_t(q, swapped[at, 0, :, lanes])
            product = jnp.concatenate([first, second], axis=1) * factor
            scores[at, h] = jnp.where(visible[at], product, NEG)
    pair = stacked([mine[:, :width], other[...]])
    rest = own_scores.shape[2] - block - own
    for h in range(heads):
        lanes = slice(h * HEAD_DIM, (h + 1) * HEAD_DIM)
        keys = jnp.concatenate(
            [mine[:, width + h * HEAD_DIM : width + (h + 1) * HEAD_DIM]] * (1 + rest // own), axis=0
        )
        first = dot_t(pair[:, lanes], key_cache[plane(), :, lanes])
        product = jnp.concatenate([first, dot_t(pair[:, lanes], keys)], axis=1) * factor
        own_scores[h] = jnp.where(near, product, NEG)
    for at, turn in enumerate(far):
        stats = jnp.zeros((own, LANES), F32)
        for h in range(heads):
            lanes = slice(h * HEAD_DIM, (h + 1) * HEAD_DIM)
            weights, found = weigh(scores[at, h], visible[at])
            out = dot(weights[:, :block], value_cache[plane() ^ turn, :, lanes])
            out = out + dot(weights[:, block:], swapped[at, 1, :, lanes])
            outs[at][:own, lanes] = out.astype(BF16)
            stats = kept(stats, h, heads, found)
        write_stats(stats, outs[at])
    stats = jnp.zeros((2 * own, LANES), F32)
    for h in range(heads):
        lanes = slice(h * HEAD_DIM, (h + 1) * HEAD_DIM)
        weights, found = weigh(own_scores[h], near)
        out = dot(weights[:, :block], value_cache[plane(), :, lanes])
        values = mine[:, 2 * width + h * HEAD_DIM : 2 * width + (h + 1) * HEAD_DIM]
        out = out + dot(weights[:, block : block + own], values)
        out = out.astype(BF16)
        local[:own, lanes] = out[:own]
        crossing[:own, lanes] = out[own:]
        stats = kept(stats, h, heads, found)
    write_stats(stats[:own], local)
    write_stats(stats[own:], crossing)


def twin_rows(mine, theirs, held):
    within = lax.rem(lax.axis_index("seq"), 2)
    held[within] = mine
    held[1 - within] = theirs
    return stacked([held[0], held[1]])


def twin_merge_and_project(*refs):
    partials, (wo, mine), refs = refs[:5], refs[5:7], refs[7:]
    gathered, (total_out, rounded, keys, values) = refs[:-4], refs[-4:]
    own, width = mine.shape[0], keys.shape[1]
    heads = width // HEAD_DIM
    for at, ref in enumerate((mine, *gathered)):
        keys[at * own : (at + 1) * own, :] = ref[:, width : 2 * width]
        values[at * own : (at + 1) * own, :] = ref[:, 2 * width :]
    stats = [dot_t(eye_of(own), ref[own : own + 16, :own]) for ref in partials]
    attention = []
    for h in range(heads):
        lanes = slice(h * HEAD_DIM, (h + 1) * HEAD_DIM)
        peaks = [s[:, h : h + 1] for s in stats]
        highest = functools.reduce(jnp.maximum, peaks)
        total, summed = 0.0, 0.0
        for ref, s, peak in zip(partials, stats, peaks):
            scale = jnp.exp(peak - highest)
            own_total = s[:, heads + h : heads + h + 1] + s[:, 2 * heads + h : 2 * heads + h + 1]
            total = total + own_total * scale
            summed = summed + ref[:own, lanes].astype(F32) * scale
        attention.append((summed / total).astype(BF16))
    product = dot(jnp.concatenate(attention, axis=1), wo[...])
    total_out[...] = product
    rounded[...] = product.astype(BF16)


def twin_add(mine, theirs, total, rounded):
    both = mine[...] + theirs[...].astype(F32)
    total[...] = both
    rounded[...] = both.astype(BF16)


def twin_finish(mine, theirs, gain, hidden, out):
    model_width = mine.shape[1]
    columns = out.shape[1]
    total = mine[...] + theirs[...].astype(F32)
    scale = lax.rsqrt(sum_squares(total) / model_width + EPS)
    lanes = pl.ds(pl.multiple_of(lax.axis_index("tp") * columns, columns), columns)
    normed = (mine[:, lanes] + theirs[:, lanes].astype(F32)) * scale * gain[...]
    out[...] = (hidden[:, lanes].astype(F32) + normed).astype(BF16)


def twin_compact(far, targets, key_cache, value_cache, *refs):
    count = len(far) + 1
    ours, (keys, values, new_keys, new_values, held) = refs[:count], refs[count:]
    block, width = key_cache.shape[1:]
    own = ours[0].shape[0]
    me = lax.axis_index("seq")
    place = me * block + iota((block, targets.shape[2]), 0)
    for at, turn in enumerate((0, *far)):
        request = plane() ^ turn
        placing = place == targets[request]
        written = jnp.max(placing.astype(F32), axis=1, keepdims=True) > 0.5
        placing = placing.astype(BF16)
        for part, (crossed, cache, out) in enumerate(
            ((keys, key_cache, new_keys), (values, value_cache, new_values))
        ):
            lanes = slice((part + 1) * width, (part + 2) * width)
            theirs = crossed[at * own : (at + 1) * own, :]
            fresh = twin_rows(ours[at][:, lanes], theirs, held.at[at, part])
            moved = dot(placing, fresh)
            out[request] = jnp.where(written, moved, cache[request].astype(F32)).astype(BF16)


def body_twin(
    hidden_in,
    query_weight,
    key_weight,
    value_weight,
    out_weight,
    query_gain,
    key_gain,
    post_gain,
    key_cache,
    value_cache,
    cache_lengths,
    parents,
    accepted_leaf,
):
    requests, block, width = key_cache.shape
    draft = parents.shape[1]
    own, model = hidden_in.shape
    tp = lax.axis_size("tp")
    seq = lax.axis_size("seq")
    columns = model // tp
    heads = width // HEAD_DIM
    far = tuple(range(requests - 1, 0, -1))

    def call(kernel, outs, inputs, scratch=(), mib=16, specs=None, ties=()):
        count = len(inputs)

        def run(*refs):
            kernel(*refs[:count], *refs[count + len(ties) :])

        return pl.pallas_call(
            run,
            out_shape=outs,
            in_specs=([VMEM] * count if specs is None else specs) + [ANY] * len(ties),
            out_specs=jax.tree.map(lambda _: VMEM, outs),
            scratch_shapes=list(scratch),
            compiler_params=params(mib),
            name=getattr(kernel, "func", kernel).__name__,
        )(*inputs, *ties)

    def over_tp(x, k):
        return lax.ppermute(x, "tp", [(i, i ^ k) for i in range(tp)])

    def beside(x):
        return lax.ppermute(x, "seq", [(i, i ^ 1) for i in range(seq)])

    def over_planes(x, turn):
        return lax.ppermute(x, "seq", [(i, (i // 2 ^ turn) * 2 + i % 2) for i in range(seq)])

    me = lax.axis_index("seq") // 2
    picked = jnp.stack(
        [
            jnp.stack([lax.dynamic_index_in_dim(x, me ^ turn, 0, False) for x in (key_cache, value_cache)])
            for turn in far
        ]
    )
    swapped = beside(picked)
    wq, wk = call(
        twin_load,
        (shaped(query_weight.shape, BF16), shaped(key_weight.shape, BF16)),
        (query_weight, key_weight),
        [pltpu.SemaphoreType.DMA((2, 4))],
        mib=48,
        specs=[ANY] * 2,
    )
    query_raw, key_raw, squares = call(
        twin_project_qk,
        (shaped((own, width), F32), shaped((own, width), F32), shaped((8, 2 * LANES), F32)),
        (hidden_in, wq, wk),
    )
    all_squares = [squares] + [over_tp(squares, k) for k in range(tp - 1, 0, -1)]

    exponents = -2.0 * (jnp.arange(HEAD_DIM) % (HEAD_DIM // 2)).astype(F32) / HEAD_DIM
    freqs = (THETA**exponents)[None, :]
    own_tree, targets, cosine, sine, limits = call(
        functools.partial(twin_tree, (0, *far)),
        (
            shaped((draft, own), F32),
            shaped((requests, 1, draft), jnp.int32),
            shaped((own, HEAD_DIM), F32),
            shaped((own, HEAD_DIM), F32),
            shaped((requests, 2 * block), jnp.int32),
        ),
        (cache_lengths[None, :], accepted_leaf[None, :], parents, freqs),
        [pltpu.VMEM((requests, draft, draft), F32)],
    )
    value = call(twin_project_v, shaped((own, width), BF16), (hidden_in, value_weight))
    queries, packed = call(
        functools.partial(twin_prepare, tp * width),
        (shaped((own, width), BF16), shaped((own, 3 * width), BF16)),
        (
            query_raw,
            key_raw,
            value,
            query_gain[None, :],
            key_gain[None, :],
            cosine,
            sine,
            *all_squares,
        ),
    )
    from_far = [over_planes(packed, turn) for turn in far]
    other = beside(queries)

    rows = own + 16
    *partials, crossing, local = call(
        functools.partial(twin_attend, far),
        (shaped((rows, width), BF16),) * (len(far) + 2),
        (limits, key_cache, value_cache, swapped, own_tree, packed, other, *from_far),
        [
            pltpu.VMEM((len(far), heads, own, 2 * block), F32),
            pltpu.VMEM((heads, 2 * own, block + LANES), F32),
        ],
    )
    partials = [over_planes(part, turn) for part, turn in zip(partials, far)]
    partials += [beside(crossing)]
    partials = [partials[2], partials[3], partials[0], partials[1], local]

    total, rounded, keys, values = call(
        twin_merge_and_project,
        (
            shaped((own, model), F32),
            shaped((own, model), BF16),
            shaped((requests * own, width), BF16),
            shaped((requests * own, width), BF16),
        ),
        (*partials, out_weight, packed, *from_far),
    )
    keys, values = beside(keys), beside(values)
    bit = 1
    while 2 * bit < tp:
        total, rounded = call(
            twin_add,
            (shaped((own, model), F32), shaped((own, model), BF16)),
            (total, over_tp(rounded, bit)),
        )
        bit *= 2
    arrived = over_tp(rounded, bit)
    new_key_cache, new_value_cache = call(
        functools.partial(twin_compact, far),
        (shaped(key_cache.shape, BF16), shaped(value_cache.shape, BF16)),
        (targets, key_cache, value_cache, packed, *from_far, keys, values),
        [pltpu.VMEM((requests, 2, 2, own, width), BF16)],
    )
    hidden_out = call(
        twin_finish,
        shaped((own, columns), BF16),
        (total, arrived, post_gain[None, :], hidden_in),
    )
    return (hidden_out, new_key_cache, new_value_cache)


def body(*args):
    hidden_in, key_cache, parents = args[0], args[8], args[11]
    tp = lax.axis_size("tp")
    own, draft = hidden_in.shape[0], parents.shape[1]
    requests, _, width = key_cache.shape
    twin = (
        own % 16 == 0
        and draft == 2 * own
        and requests == 4
        and lax.axis_size("seq") == 2 * requests
        and own <= LANES
        and LANES % own == 0
        and own <= width
        and 3 * (width // HEAD_DIM) <= 16
        and tp > 1
        and tp & (tp - 1) == 0
    )
    return (body_twin if twin else body_general)(*args)


def solution(mesh):
    return jax.shard_map(
        body,
        mesh=mesh,
        in_specs=(
            P("seq", None),
            P(None, "tp"),
            P(None, "tp"),
            P(None, "tp"),
            P("tp", None),
            P("tp"),
            P("tp"),
            P("tp"),
            P(None, "seq", "tp"),
            P(None, "seq", "tp"),
            P(),
            P(),
            P(),
        ),
        out_specs=(P("seq", "tp"), P(None, "seq", "tp"), P(None, "seq", "tp")),
        check_vma=False,
    )
```

time: 203 us -> 46.8 us (0.23)
  blocking collectives: 67.2 us -> 0 us
  waiting for transfers between devices: 70.7 us -> 17.5 us
  matrix products: 18.4 us -> 0 us
  other arithmetic: 18.1 us -> 0.18 us
  starting transfers between devices: 0.12 us -> 17.7 us
  between operations: 14.3 us -> 0.89 us
  local copies, waits for them, and re-layouts: 13.3 us -> 1.36 us
  Pallas kernels: 0 us -> 8.98 us
    all_gather x2 -> x0, blocking collectives: 61.6 us -> none  [joined_2(): everything = jax.tree.map(lambda part: lax.all_gather(part, axis), x)]
    all_gather x2 -> x0, waiting for transfers between devices: 41.5 us -> none  [the longest x1 41 us: body(): piece = lax.all_gather(hidden_in, 'seq', axis=0, tiled=True)]
    psum x1 -> x0, waiting for transfers between devices: 28.5 us -> none  [body(): summed_heads = lax.psum(projected, 'tp')]
    dot_general x17 -> x0, matrix products: 18.4 us -> none  [the longest x1 2.77 us: body(): jnp.dot(attention, out_weight, preferred_element_type=jnp.float32)]
    ppermute x0 -> x16, starting transfers between devices: none -> 17.7 us  [the longest x6 8.91 us: over_planes(): lax.ppermute(x, 'seq', [(i, (i // 2 ^ turn) * 2 + i % 2) for i in range(s...]
    ppermute x0 -> x16, waiting for transfers between devices: none -> 17.5 us  [the longest x5 12.2 us: beside(): return lax.ppermute(x, 'seq', [(i, i ^ 1) for i in range(seq)])]
    add x18 -> x0, other arithmetic: 10.9 us -> none  [the longest x7 9.66 us: join_partials(): out_first.reshape(rows_here, heads_here, -1) * scale_first[..., None]]
    pallas_call x0 -> x10, Pallas kernels: none -> 8.98 us  [call(): pl.pallas_call(run, out_shape=outs, in_specs=([VMEM] * count if specs is...]
  transfers between devices with their start and end apart: 3 -> 16, of which waited for: 3 -> 8; matrix products, arithmetic and copies ran while one was open for 8% -> 0% of each run, Pallas kernels for 0% -> 14%
where the time goes in v1:
time: 46.8 us; the launch traced here: 46.6 us
  starting transfers between devices  17.7 us (38%)
  waiting for transfers between devices  17.5 us (37%)
  Pallas kernels  8.98 us (19%)
  local copies, waits for them, and re-layouts  1.36 us (3%)
  between operations  0.89 us (2%)
    ppermute x5, waiting for transfers between devices, beside(): return lax.ppermute(x, 'seq', [(i, i ^ 1) for i in range(seq)])  12.2 us
    pallas_call x10, Pallas kernels, call(): pl.pallas_call(run, out_shape=outs, in_specs=([VMEM] * count if specs is...  8.98 us
    ppermute x6, starting transfers between devices, over_planes(): lax.ppermute(x, 'seq', [(i, (i // 2 ^ turn) * 2 + i % 2) for i in range(s...  8.91 us
    ppermute x5, starting transfers between devices, beside(): return lax.ppermute(x, 'seq', [(i, i ^ 1) for i in range(seq)])  6.16 us
    ppermute x6, waiting for transfers between devices, over_planes(): lax.ppermute(x, 'seq', [(i, (i // 2 ^ turn) * 2 + i % 2) for i in range(s...  4.43 us
    ppermute x5, starting transfers between devices, over_tp(): return lax.ppermute(x, 'tp', [(i, i ^ k) for i in range(tp)])  2.65 us
    dynamic_slice x1, local copies, waits for them, and re-layouts, body_twin(): lax.dynamic_index_in_dim(x, me ^ turn, 0, False)  1.29 us
  transfers between devices with their start and end apart: 16, of which 8 were waited for; matrix products, arithmetic and copies ran while one was open for 0% of the time, Pallas kernels for 14%

profile of v1, /device:TPU:0, one launch (start us, length us, event | category | flops | bytes accessed | tf_op | source)
XLA Modules:
  0.0 46.6 jit_solution(11442647251825594639)
XLA Ops:
  0.7 1.3 %constant_dynamic-slice_fusion.4 = (bf16[1,128,512]{2,1,0:T(8,128)(2,1)S(1)}, bf16[1,128,512]{2,1,0:T(8,128)(2,1)S(1)}, bf16[1,128,512]{2,1,0:T(8,128)(2,1)S(1)}...) fusion(bf16[4,128,512]{2,1,0:T(8,128)(2,1)} %refs_2_.5, ...), kind=kLoop, calls=%fused_computation.9 | loop fusion | bytes 1572876 | tf_op jit(solution)/shard_map/jit(dynamic_index_in_dim)/dynamic_slice | solution.py:764
  2.2 3.0 %collective-permute-start = (bf16[3,2,128,512]{3,2,1,0:T(8,128)(2,1)S(1)}, bf16[3,2,128,512]{3,2,1,0:T(8,128)(2,1)S(1)}, u32[]{:S(2)}, u32[]{:S(2)}) collective-permute-start(bf16[3,2,128,512]{3,2,1,0:T(8,128)(2,1)S(1)} %pad_maximum_fusion), channel_id=1, source_target_pairs={{0,4},{4,0},{8,12},{12,8},{16,20},{20,16},{24,28},{28,24},{1,5},{5... | collective-permute-start | bytes 2359304 | tf_op jit(solution)/shard_map/ppermute | solution.py:756
  5.2 2.2 %twin_load.1 = (bf16[2048,512]{1,0:T(8,128)(2,1)S(1)}, bf16[2048,512]{1,0:T(8,128)(2,1)S(1)}) custom-call(bf16[2048,512]{1,0:T(8,128)(2,1)} %refs_0_.3, bf16[2048,512]{1,0:T(8,128)(2,1)} %refs_1_.4), custom_call_target="tpu_custom_call" | custom-call | tf_op jit(solution)/shard_map/twin_load/pallas_call | solution.py:742
  7.4 0.9 %twin_project_qk.1 = (f32[32,512]{1,0:T(8,128)S(1)}, f32[32,512]{1,0:T(8,128)S(1)}, f32[8,256]{1,0:T(8,128)S(1)}) custom-call(bf16[32,2048]{1,0:T(8,128)(2,1)S(1)} %copy-done.4, bf16[2048,512]{1,0:T(8,128)(2,1)S(1)} %get-tuple-element.30.refs_1_, bf16[2048,512]{1,0:T(8,128)(2,1)S(1)} %get-tuple-element.31.refs_2_), custom_call_target="tpu_custom_call" | custom-call | tf_op jit(solution)/shard_map/twin_project_qk/pallas_call | solution.py:742
  8.4 0.7 %collective-permute-start.1 = (f32[8,256]{1,0:T(8,128)S(1)}, f32[8,256]{1,0:T(8,128)S(1)}, u32[]{:S(2)}, u32[]{:S(2)}) collective-permute-start(f32[8,256]{1,0:T(8,128)S(1)} %get-tuple-element.36.refs_7_), channel_id=1, source_target_pairs={{0,3},{1,2},{2,1},{3,0},{4,7},{5,6},{6,5},{7,4},{8,11},{9,10},{10,... | collective-permute-start | bytes 24584 | tf_op jit(solution)/shard_map/ppermute | solution.py:753
  9.2 0.9 %collective-permute-start.2 = (f32[8,256]{1,0:T(8,128)S(1)}, f32[8,256]{1,0:T(8,128)S(1)}, u32[]{:S(2)}, u32[]{:S(2)}) collective-permute-start(f32[8,256]{1,0:T(8,128)S(1)} %get-tuple-element.36.refs_7_), channel_id=1, source_target_pairs={{0,2},{1,3},{2,0},{3,1},{4,6},{5,7},{6,4},{7,5},{8,10},{9,11},{10,... | collective-permute-start | bytes 24584 | tf_op jit(solution)/shard_map/ppermute | solution.py:753
  10.9 1.2 %twin_tree.1 = (f32[64,32]{1,0:T(8,128)S(1)}, s32[4,1,64]{2,1,0:T(1,128)S(1)}, f32[32,128]{1,0:T(8,128)S(1)}, f32[32,128]{1,0:T(8,128)S(1)}, s32[4,256]{1,0:T(4,128)S(1)}) custom-call(s32[1,4]{1,0:T(1,128)S(1)} %bitcast.14, s32[1,4]{1,0:T(1,128)S(1)} %bitcast.15, s32[4,64]{1,0:T(4,128)S(1)} %copy-done.8, f32[1,128]{1,0:T(1,128)S(1)} %fusion.2.refs_3_), custom_call_target="tpu_custom_call" | custom-call | tf_op jit(solution)/shard_map/twin_tree/pallas_call | solution.py:742
  12.0 0.8 %collective-permute-done.2.refs_9_ = f32[8,256]{1,0:T(8,128)S(1)} collective-permute-done((f32[8,256]{1,0:T(8,128)S(1)}, f32[8,256]{1,0:T(8,128)S(1)}, u32[]{:S(2)}, u32[]{:S(2)}) %collective-permute-start.2) | collective-permute-done | bytes 8224 | tf_op jit(solution)/shard_map/ppermute | solution.py:753
  13.1 3.7 %collective-permute-start.5 = (bf16[32,1536]{1,0:T(8,128)(2,1)S(1)}, bf16[32,1536]{1,0:T(8,128)(2,1)S(1)}, u32[]{:S(2)}, u32[]{:S(2)}) collective-permute-start(bf16[32,1536]{1,0:T(8,128)(2,1)S(1)} %get-tuple-element.37.refs_5_.refs_6_.refs_3_), channel_id=1, source_target_pairs={{0,24},{4,28},{8,16},{12,20},{16,8},{20,12},{24,0},{28,4},{1,25},{... | collective-permute-start | bytes 294920 | tf_op jit(solution)/shard_map/ppermute | solution.py:759
  16.8 0.8 %collective-permute-start.7 = (bf16[32,1536]{1,0:T(8,128)(2,1)S(1)}, bf16[32,1536]{1,0:T(8,128)(2,1)S(1)}, u32[]{:S(2)}, u32[]{:S(2)}) collective-permute-start(bf16[32,1536]{1,0:T(8,128)(2,1)S(1)} %get-tuple-element.37.refs_5_.refs_6_.refs_3_), channel_id=1, source_target_pairs={{0,8},{4,12},{8,0},{12,4},{16,24},{20,28},{24,16},{28,20},{1,9},{5... | collective-permute-start | bytes 294920 | tf_op jit(solution)/shard_map/ppermute | solution.py:759
  18.1 5.3 %collective-permute-done.4.refs_6_ = bf16[32,512]{1,0:T(8,128)(2,1)S(1)} collective-permute-done((bf16[32,512]{1,0:T(8,128)(2,1)S(1)}, bf16[32,512]{1,0:T(8,128)(2,1)S(1)}, u32[]{:S(2)}, u32[]{:S(2)}) %collective-permute-start.4) | collective-permute-done | bytes 32800 | tf_op jit(solution)/shard_map/ppermute | solution.py:756
  23.4 1.9 %collective-permute-done.6.refs_8_.refs_5_ = bf16[32,1536]{1,0:T(8,128)(2,1)S(1)} collective-permute-done((bf16[32,1536]{1,0:T(8,128)(2,1)S(1)}, bf16[32,1536]{1,0:T(8,128)(2,1)S(1)}, u32[]{:S(2)}, u32[]{:S(2)}) %collective-permute-start.6) | collective-permute-done | bytes 98336 | tf_op jit(solution)/shard_map/ppermute | solution.py:759
  25.3 1.1 %twin_attend.1 = (bf16[48,512]{1,0:T(8,128)(2,1)S(1)}, bf16[48,512]{1,0:T(8,128)(2,1)S(1)}, bf16[48,512]{1,0:T(8,128)(2,1)S(1)}, bf16[48,512]{1,0:T(8,128)(2,1)S(1)}, bf16[48,512]{1,0:T(8,128)(2,1)S(1)}) custom-call(s32[4,256]{1,0:T(4,128)S(1)} %get-tuple-element.28.refs_0_, bf16[4,128,512]{2,1,0:T(8,128)(2,1)S(1)} %copy-done, ...), custom_call_target="tpu_custom_call" | custom-call | tf_op jit(solution)/shard_map/twin_attend/pallas_call | solution.py:742
  26.4 2.5 %collective-permute-start.10 = (bf16[48,512]{1,0:T(8,128)(2,1)S(1)}, bf16[48,512]{1,0:T(8,128)(2,1)S(1)}, u32[]{:S(2)}, u32[]{:S(2)}) collective-permute-start(bf16[48,512]{1,0:T(8,128)(2,1)S(1)} %get-tuple-element.41), channel_id=1, source_target_pairs={{0,24},{4,28},{8,16},{12,20},{16,8},{20,12},{24,0},{28,4},{1,25},{... | collective-permute-start | bytes 147464 | tf_op jit(solution)/shard_map/ppermute | solution.py:759
  29.0 1.9 %collective-permute-start.8 = (bf16[48,512]{1,0:T(8,128)(2,1)S(1)}, bf16[48,512]{1,0:T(8,128)(2,1)S(1)}, u32[]{:S(2)}, u32[]{:S(2)}) collective-permute-start(bf16[48,512]{1,0:T(8,128)(2,1)S(1)} %get-tuple-element.39), channel_id=1, source_target_pairs={{0,8},{4,12},{8,0},{12,4},{16,24},{20,28},{24,16},{28,20},{1,9},{5... | collective-permute-start | bytes 147464 | tf_op jit(solution)/shard_map/ppermute | solution.py:759
  31.4 1.1 %collective-permute-done.10.refs_2_ = bf16[48,512]{1,0:T(8,128)(2,1)S(1)} collective-permute-done((bf16[48,512]{1,0:T(8,128)(2,1)S(1)}, bf16[48,512]{1,0:T(8,128)(2,1)S(1)}, u32[]{:S(2)}, u32[]{:S(2)}) %collective-permute-start.10) | collective-permute-done | bytes 49184 | tf_op jit(solution)/shard_map/ppermute | solution.py:759
  32.5 1.5 %collective-permute-done.11.refs_3_ = bf16[48,512]{1,0:T(8,128)(2,1)S(1)} collective-permute-done((bf16[48,512]{1,0:T(8,128)(2,1)S(1)}, bf16[48,512]{1,0:T(8,128)(2,1)S(1)}, u32[]{:S(2)}, u32[]{:S(2)}) %collective-permute-start.11) | collective-permute-done | bytes 49184 | tf_op jit(solution)/shard_map/ppermute | solution.py:759
  33.9 1.0 %collective-permute-done.9.refs_1_ = bf16[48,512]{1,0:T(8,128)(2,1)S(1)} collective-permute-done((bf16[48,512]{1,0:T(8,128)(2,1)S(1)}, bf16[48,512]{1,0:T(8,128)(2,1)S(1)}, u32[]{:S(2)}, u32[]{:S(2)}) %collective-permute-start.9) | collective-permute-done | bytes 49184 | tf_op jit(solution)/shard_map/ppermute | solution.py:756
  35.0 0.8 %twin_merge_and_project.1 = (f32[32,2048]{1,0:T(8,128)S(1)}, bf16[32,2048]{1,0:T(8,128)(2,1)S(1)}, bf16[128,512]{1,0:T(8,128)(2,1)S(1)}, bf16[128,512]{1,0:T(8,128)(2,1)S(1)}) custom-call(bf16[48,512]{1,0:T(8,128)(2,1)S(1)} %collective-permute-done.8.refs_0_, bf16[48,512]{1,0:T(8,128)(2,1)S(1)} %collective-permute-done.9.refs_1_, ...), custom_call_target="tpu_custom_call" | custom-call | tf_op jit(solution)/shard_map/twin_merge_and_project/pallas_call | solution.py:742
  36.4 1.5 %collective-permute-start.15 = (bf16[128,512]{1,0:T(8,128)(2,1)S(1)}, bf16[128,512]{1,0:T(8,128)(2,1)S(1)}, u32[]{:S(2)}, u32[]{:S(2)}) collective-permute-start(bf16[128,512]{1,0:T(8,128)(2,1)S(1)} %get-tuple-element.50), channel_id=1, source_target_pairs={{0,4},{4,0},{8,12},{12,8},{16,20},{20,16},{24,28},{28,24},{1,5},{5... | collective-permute-start | bytes 393224 | tf_op jit(solution)/shard_map/ppermute | solution.py:756
  38.6 3.5 %collective-permute-done.14.refs_7_ = bf16[128,512]{1,0:T(8,128)(2,1)S(1)} collective-permute-done((bf16[128,512]{1,0:T(8,128)(2,1)S(1)}, bf16[128,512]{1,0:T(8,128)(2,1)S(1)}, u32[]{:S(2)}, u32[]{:S(2)}) %collective-permute-start.14) | collective-permute-done | bytes 131104 | tf_op jit(solution)/shard_map/ppermute | solution.py:756
  42.2 2.4 %collective-permute-done.15.refs_8_ = bf16[128,512]{1,0:T(8,128)(2,1)S(1)} collective-permute-done((bf16[128,512]{1,0:T(8,128)(2,1)S(1)}, bf16[128,512]{1,0:T(8,128)(2,1)S(1)}, u32[]{:S(2)}, u32[]{:S(2)}) %collective-permute-start.15) | collective-permute-done | bytes 131104 | tf_op jit(solution)/shard_map/ppermute | solution.py:756
  44.5 1.4 %twin_compact.1 = (bf16[4,128,512]{2,1,0:T(8,128)(2,1)}, bf16[4,128,512]{2,1,0:T(8,128)(2,1)}) custom-call(s32[4,1,64]{2,1,0:T(1,128)S(1)} %get-tuple-element.48.refs_0_, bf16[4,128,512]{2,1,0:T(8,128)(2,1)S(1)} %copy-done, bf16[4,128,512]{2,1,0:T(8,128)(2,1)S(1)} %copy-done.1, bf16[32,1536]{1,0:T(8,128)(2,1)S(1)} %get-tuple-element.37.refs_5_.refs_6_.refs_3_, ...), custom_call_target="tpu_custom_call" | custom-call | tf_op jit(solution)/shard_map/twin_compact/pallas_call | solution.py:742
  45.9 0.7 %twin_finish.1 = bf16[32,512]{1,0:T(8,128)(2,1)} custom-call(f32[32,2048]{1,0:T(8,128)S(1)} %get-tuple-element.46.refs_0_, bf16[32,2048]{1,0:T(8,128)(2,1)S(1)} %collective-permute-done.13.refs_1_, f32[1,512]{1,0:T(1,128)S(1)} %bitcast.13, bf16[32,2048]{1,0:T(8,128)(2,1)S(1)} %copy-done.4), custom_call_target="tpu_custom_call" | custom-call | tf_op jit(solution)/shard_map/twin_finish/pallas_call | solution.py:742
  (46 shorter events, 3.6 us)
Async XLA Ops:
  2.2 5.2 %copy-start.4 = (bf16[32,2048]{1,0:T(8,128)(2,1)S(1)}, bf16[32,2048]{1,0:T(8,128)(2,1)}, u32[]{:S(2)}) copy-start(bf16[32,2048]{1,0:T(8,128)(2,1)} %refs_3_.1) | copy-start | bytes 393220
  2.2 23.1 %collective-permute-start = (bf16[3,2,128,512]{3,2,1,0:T(8,128)(2,1)S(1)}, bf16[3,2,128,512]{3,2,1,0:T(8,128)(2,1)S(1)}, u32[]{:S(2)}, u32[]{:S(2)}) collective-permute-start(bf16[3,2,128,512]{3,2,1,0:T(8,128)(2,1)S(1)} %pad_maximum_fusion), channel_id=1, source_target_pairs={{0,4},{4,0},{8,12},{12,8},{16,20},{20,16},{24,28},{28,24},{1,5},{5... | collective-permute-start | bytes 2359304 | tf_op jit(solution)/shard_map/ppermute | solution.py:756
  7.4 3.0 %copy-start.2 = (bf16[2048,512]{1,0:T(8,128)(2,1)S(1)}, bf16[2048,512]{1,0:T(8,128)(2,1)}, u32[]{:S(2)}) copy-start(bf16[2048,512]{1,0:T(8,128)(2,1)} %refs_1_.5) | copy-start | bytes 6291460
  8.4 4.5 %copy-start.5 = (f32[512]{0:T(512)S(1)}, f32[512]{0:T(512)}, u32[]{:S(2)}) copy-start(f32[512]{0:T(512)} %param.18) | copy-start | bytes 6148
  8.4 4.5 %copy-start.6 = (f32[512]{0:T(512)S(1)}, f32[512]{0:T(512)}, u32[]{:S(2)}) copy-start(f32[512]{0:T(512)} %param.19) | copy-start | bytes 6148
  8.4 16.9 %copy-start = (bf16[4,128,512]{2,1,0:T(8,128)(2,1)S(1)}, bf16[4,128,512]{2,1,0:T(8,128)(2,1)}, u32[]{:S(2)}) copy-start(bf16[4,128,512]{2,1,0:T(8,128)(2,1)} %refs_1_.7) | copy-start | bytes 1572868
  8.4 16.9 %copy-start.1 = (bf16[4,128,512]{2,1,0:T(8,128)(2,1)S(1)}, bf16[4,128,512]{2,1,0:T(8,128)(2,1)}, u32[]{:S(2)}) copy-start(bf16[4,128,512]{2,1,0:T(8,128)(2,1)} %refs_2_.5) | copy-start | bytes 1572868
  8.4 3.6 %collective-permute-start.1 = (f32[8,256]{1,0:T(8,128)S(1)}, f32[8,256]{1,0:T(8,128)S(1)}, u32[]{:S(2)}, u32[]{:S(2)}) collective-permute-start(f32[8,256]{1,0:T(8,128)S(1)} %get-tuple-element.36.refs_7_), channel_id=1, source_target_pairs={{0,3},{1,2},{2,1},{3,0},{4,7},{5,6},{6,5},{7,4},{8,11},{9,10},{10,... | collective-permute-start | bytes 24584 | tf_op jit(solution)/shard_map/ppermute | solution.py:753
  9.2 3.7 %collective-permute-start.2 = (f32[8,256]{1,0:T(8,128)S(1)}, f32[8,256]{1,0:T(8,128)S(1)}, u32[]{:S(2)}, u32[]{:S(2)}) collective-permute-start(f32[8,256]{1,0:T(8,128)S(1)} %get-tuple-element.36.refs_7_), channel_id=1, source_target_pairs={{0,2},{1,3},{2,0},{3,1},{4,6},{5,7},{6,4},{7,5},{8,10},{9,11},{10,... | collective-permute-start | bytes 24584 | tf_op jit(solution)/shard_map/ppermute | solution.py:753
  10.1 2.8 %collective-permute-start.3 = (f32[8,256]{1,0:T(8,128)S(1)}, f32[8,256]{1,0:T(8,128)S(1)}, u32[]{:S(2)}, u32[]{:S(2)}) collective-permute-start(f32[8,256]{1,0:T(8,128)S(1)} %get-tuple-element.36.refs_7_), channel_id=1, source_target_pairs={{0,1},{1,0},{2,3},{3,2},{4,5},{5,4},{6,7},{7,6},{8,9},{9,8},{10,11... | collective-permute-start | bytes 24584 | tf_op jit(solution)/shard_map/ppermute | solution.py:753
  10.4 24.6 %copy-start.3 = (bf16[512,2048]{1,0:T(8,128)(2,1)S(1)}, bf16[512,2048]{1,0:T(8,128)(2,1)}, u32[]{:S(2)}) copy-start(bf16[512,2048]{1,0:T(8,128)(2,1)} %refs_5_.1) | copy-start | bytes 6291460
  13.1 10.3 %collective-permute-start.5 = (bf16[32,1536]{1,0:T(8,128)(2,1)S(1)}, bf16[32,1536]{1,0:T(8,128)(2,1)S(1)}, u32[]{:S(2)}, u32[]{:S(2)}) collective-permute-start(bf16[32,1536]{1,0:T(8,128)(2,1)S(1)} %get-tuple-element.37.refs_5_.refs_6_.refs_3_), channel_id=1, source_target_pairs={{0,24},{4,28},{8,16},{12,20},{16,8},{20,12},{24,0},{28,4},{1,25},{... | collective-permute-start | bytes 294920 | tf_op jit(solution)/shard_map/ppermute | solution.py:759
  16.8 8.5 %collective-permute-start.6 = (bf16[32,1536]{1,0:T(8,128)(2,1)S(1)}, bf16[32,1536]{1,0:T(8,128)(2,1)S(1)}, u32[]{:S(2)}, u32[]{:S(2)}) collective-permute-start(bf16[32,1536]{1,0:T(8,128)(2,1)S(1)} %get-tuple-element.37.refs_5_.refs_6_.refs_3_), channel_id=1, source_target_pairs={{0,16},{4,20},{8,24},{12,28},{16,0},{20,4},{24,8},{28,12},{1,17},{... | collective-permute-start | bytes 294920 | tf_op jit(solution)/shard_map/ppermute | solution.py:759
  16.8 8.5 %collective-permute-start.7 = (bf16[32,1536]{1,0:T(8,128)(2,1)S(1)}, bf16[32,1536]{1,0:T(8,128)(2,1)S(1)}, u32[]{:S(2)}, u32[]{:S(2)}) collective-permute-start(bf16[32,1536]{1,0:T(8,128)(2,1)S(1)} %get-tuple-element.37.refs_5_.refs_6_.refs_3_), channel_id=1, source_target_pairs={{0,8},{4,12},{8,0},{12,4},{16,24},{20,28},{24,16},{28,20},{1,9},{5... | collective-permute-start | bytes 294920 | tf_op jit(solution)/shard_map/ppermute | solution.py:759
  17.6 5.9 %collective-permute-start.4 = (bf16[32,512]{1,0:T(8,128)(2,1)S(1)}, bf16[32,512]{1,0:T(8,128)(2,1)S(1)}, u32[]{:S(2)}, u32[]{:S(2)}) collective-permute-start(bf16[32,512]{1,0:T(8,128)(2,1)S(1)} %get-tuple-element.38), channel_id=1, source_target_pairs={{0,4},{4,0},{8,12},{12,8},{16,20},{20,16},{24,28},{28,24},{1,5},{5... | collective-permute-start | bytes 98312 | tf_op jit(solution)/shard_map/ppermute | solution.py:756
  26.4 6.1 %collective-permute-start.10 = (bf16[48,512]{1,0:T(8,128)(2,1)S(1)}, bf16[48,512]{1,0:T(8,128)(2,1)S(1)}, u32[]{:S(2)}, u32[]{:S(2)}) collective-permute-start(bf16[48,512]{1,0:T(8,128)(2,1)S(1)} %get-tuple-element.41), channel_id=1, source_target_pairs={{0,24},{4,28},{8,16},{12,20},{16,8},{20,12},{24,0},{28,4},{1,25},{... | collective-permute-start | bytes 147464 | tf_op jit(solution)/shard_map/ppermute | solution.py:759
  29.0 5.0 %collective-permute-start.11 = (bf16[48,512]{1,0:T(8,128)(2,1)S(1)}, bf16[48,512]{1,0:T(8,128)(2,1)S(1)}, u32[]{:S(2)}, u32[]{:S(2)}) collective-permute-start(bf16[48,512]{1,0:T(8,128)(2,1)S(1)} %get-tuple-element.42), channel_id=1, source_target_pairs={{0,16},{4,20},{8,24},{12,28},{16,0},{20,4},{24,8},{28,12},{1,17},{... | collective-permute-start | bytes 147464 | tf_op jit(solution)/shard_map/ppermute | solution.py:759
  29.0 5.0 %collective-permute-start.8 = (bf16[48,512]{1,0:T(8,128)(2,1)S(1)}, bf16[48,512]{1,0:T(8,128)(2,1)S(1)}, u32[]{:S(2)}, u32[]{:S(2)}) collective-permute-start(bf16[48,512]{1,0:T(8,128)(2,1)S(1)} %get-tuple-element.39), channel_id=1, source_target_pairs={{0,8},{4,12},{8,0},{12,4},{16,24},{20,28},{24,16},{28,20},{1,9},{5... | collective-permute-start | bytes 147464 | tf_op jit(solution)/shard_map/ppermute | solution.py:759
  30.9 4.1 %collective-permute-start.9 = (bf16[48,512]{1,0:T(8,128)(2,1)S(1)}, bf16[48,512]{1,0:T(8,128)(2,1)S(1)}, u32[]{:S(2)}, u32[]{:S(2)}) collective-permute-start(bf16[48,512]{1,0:T(8,128)(2,1)S(1)} %get-tuple-element.40), channel_id=1, source_target_pairs={{0,4},{4,0},{8,12},{12,8},{16,20},{20,16},{24,28},{28,24},{1,5},{5... | collective-permute-start | bytes 147464 | tf_op jit(solution)/shard_map/ppermute | solution.py:756
  35.0 10.9 %copy-start.7 = (f32[512]{0:T(512)S(1)}, f32[512]{0:T(512)}, u32[]{:S(2)}) copy-start(f32[512]{0:T(512)} %param.20) | copy-start | bytes 6148
  35.8 2.1 %collective-permute-start.12 = (bf16[32,2048]{1,0:T(8,128)(2,1)S(1)}, bf16[32,2048]{1,0:T(8,128)(2,1)S(1)}, u32[]{:S(2)}, u32[]{:S(2)}) collective-permute-start(bf16[32,2048]{1,0:T(8,128)(2,1)S(1)} %get-tuple-element.45), channel_id=1, source_target_pairs={{0,1},{1,0},{2,3},{3,2},{4,5},{5,4},{6,7},{7,6},{8,9},{9,8},{10,11... | collective-permute-start | bytes 393224 | tf_op jit(solution)/shard_map/ppermute | solution.py:753
  35.8 6.4 %collective-permute-start.14 = (bf16[128,512]{1,0:T(8,128)(2,1)S(1)}, bf16[128,512]{1,0:T(8,128)(2,1)S(1)}, u32[]{:S(2)}, u32[]{:S(2)}) collective-permute-start(bf16[128,512]{1,0:T(8,128)(2,1)S(1)} %get-tuple-element.49), channel_id=1, source_target_pairs={{0,4},{4,0},{8,12},{12,8},{16,20},{20,16},{24,28},{28,24},{1,5},{5... | collective-permute-start | bytes 393224 | tf_op jit(solution)/shard_map/ppermute | solution.py:756
  36.4 8.1 %collective-permute-start.15 = (bf16[128,512]{1,0:T(8,128)(2,1)S(1)}, bf16[128,512]{1,0:T(8,128)(2,1)S(1)}, u32[]{:S(2)}, u32[]{:S(2)}) collective-permute-start(bf16[128,512]{1,0:T(8,128)(2,1)S(1)} %get-tuple-element.50), channel_id=1, source_target_pairs={{0,4},{4,0},{8,12},{12,8},{16,20},{20,16},{24,28},{28,24},{1,5},{5... | collective-permute-start | bytes 393224 | tf_op jit(solution)/shard_map/ppermute | solution.py:756
  37.9 8.0 %collective-permute-start.13 = (bf16[32,2048]{1,0:T(8,128)(2,1)S(1)}, bf16[32,2048]{1,0:T(8,128)(2,1)S(1)}, u32[]{:S(2)}, u32[]{:S(2)}) collective-permute-start(bf16[32,2048]{1,0:T(8,128)(2,1)S(1)} %get-tuple-element.47), channel_id=1, source_target_pairs={{0,2},{1,3},{2,0},{3,1},{4,6},{5,7},{6,4},{7,5},{8,10},{9,11},{10,... | collective-permute-start | bytes 393224 | tf_op jit(solution)/shard_map/ppermute | solution.py:753
  (3 other events, 7.5 us)

commit v2 on v1

--- a/solution.py
+++ b/solution.py
@@ -576,7 +576,7 @@
 def twin_attend(far, limits, key_cache, value_cache, swapped, own_tree, mine, other, *refs):
     count = len(far)
     queries, outs = refs[:count], refs[count : 2 * count]
-    crossing, local, scores, own_scores = refs[2 * count :]
+    crossing, local, copied, scores, own_scores = refs[2 * count :]
     block, width = key_cache.shape[1:]
     heads = width // HEAD_DIM
     own = other.shape[0]
@@ -636,6 +636,12 @@
         stats = kept(stats, h, heads, found)
     write_stats(stats[:own], local)
     write_stats(stats[own:], crossing)
+    for at, ref in enumerate((mine, *queries)):
+        for part in range(2):
+            rows = slice((2 * at + part) * own, (2 * at + part + 1) * own)
+            copied[rows, :] = ref[:, (part + 1) * width : (part + 2) * width]
+    rest = copied.shape[0] - 2 * (count + 1) * own
+    copied[2 * (count + 1) * own :, :] = jnp.zeros((rest, width), BF16)
 
 
 def twin_rows(mine, theirs, held):
@@ -646,13 +652,9 @@
 
 
 def twin_merge_and_project(*refs):
-    partials, (wo, mine), refs = refs[:5], refs[5:7], refs[7:]
-    gathered, (total_out, rounded, keys, values) = refs[:-4], refs[-4:]
-    own, width = mine.shape[0], keys.shape[1]
+    partials, (wo, total_out, rounded) = refs[:-3], refs[-3:]
+    own, width = total_out.shape[0], partials[0].shape[1]
     heads = width // HEAD_DIM
-    for at, ref in enumerate((mine, *gathered)):
-        keys[at * own : (at + 1) * own, :] = ref[:, width : 2 * width]
-        values[at * own : (at + 1) * own, :] = ref[:, 2 * width :]
     stats = [dot_t(eye_of(own), ref[own : own + 16, :own]) for ref in partials]
     attention = []
     for h in range(heads):
@@ -689,7 +691,7 @@
 
 def twin_compact(far, targets, key_cache, value_cache, *refs):
     count = len(far) + 1
-    ours, (keys, values, new_keys, new_values, held) = refs[:count], refs[count:]
+    ours, (copied, new_keys, new_values, held) = refs[:count], refs[count:]
     block, width = key_cache.shape[1:]
     own = ours[0].shape[0]
     me = lax.axis_index("seq")
@@ -699,11 +701,10 @@
         placing = place == targets[request]
         written = jnp.max(placing.astype(F32), axis=1, keepdims=True) > 0.5
         placing = placing.astype(BF16)
-        for part, (crossed, cache, out) in enumerate(
-            ((keys, key_cache, new_keys), (values, value_cache, new_values))
-        ):
+        for part, (cache, out) in enumerate(((key_cache, new_keys), (value_cache, new_values))):
             lanes = slice((part + 1) * width, (part + 2) * width)
-            theirs = crossed[at * own : (at + 1) * own, :]
+            rows = slice((2 * at + part) * own, (2 * at + part + 1) * own)
+            theirs = copied[rows, :]
             fresh = twin_rows(ours[at][:, lanes], theirs, held.at[at, part])
             moved = dot(placing, fresh)
             out[request] = jnp.where(written, moved, cache[request].astype(F32)).astype(BF16)
@@ -814,9 +815,10 @@
     other = beside(queries)
 
     rows = own + 16
-    *partials, crossing, local = call(
+    *partials, crossing, local, copied = call(
         functools.partial(twin_attend, far),
-        (shaped((rows, width), BF16),) * (len(far) + 2),
+        (shaped((rows, width), BF16),) * (len(far) + 2)
+        + (shaped((2 * requests * own + own, width), BF16),),
         (limits, key_cache, value_cache, swapped, own_tree, packed, other, *from_far),
         [
             pltpu.VMEM((len(far), heads, own, 2 * block), F32),
@@ -827,17 +829,12 @@
     partials += [beside(crossing)]
     partials = [partials[2], partials[3], partials[0], partials[1], local]
 
-    total, rounded, keys, values = call(
+    total, rounded = call(
         twin_merge_and_project,
-        (
-            shaped((own, model), F32),
-            shaped((own, model), BF16),
-            shaped((requests * own, width), BF16),
-            shaped((requests * own, width), BF16),
-        ),
-        (*partials, out_weight, packed, *from_far),
-    )
-    keys, values = beside(keys), beside(values)
+        (shaped((own, model), F32), shaped((own, model), BF16)),
+        (*partials, out_weight),
+    )
+    copied = beside(copied)
     bit = 1
     while 2 * bit < tp:
         total, rounded = call(
@@ -850,7 +847,7 @@
     new_key_cache, new_value_cache = call(
         functools.partial(twin_compact, far),
         (shaped(key_cache.shape, BF16), shaped(value_cache.shape, BF16)),
-        (targets, key_cache, value_cache, packed, *from_far, keys, values),
+        (targets, key_cache, value_cache, packed, *from_far, copied),
         [pltpu.VMEM((requests, 2, 2, own, width), BF16)],
     )
     hidden_out = call(

time: 46.8 us -> 44.3 us (0.947)
  waiting for transfers between devices: 17.5 us -> 15.6 us
  starting transfers between devices: 17.7 us -> 17.1 us
    ppermute x5 -> x4, waiting for transfers between devices: 12.2 us -> 7.76 us  [beside(): return lax.ppermute(x, 'seq', [(i, i ^ 1) for i in range(seq)])]
    ppermute x5, waiting for transfers between devices: 0.85 us -> 4.89 us  [over_tp(): return lax.ppermute(x, 'tp', [(i, i ^ k) for i in range(tp)])]
    ppermute x6, waiting for transfers between devices: 4.43 us -> 2.94 us  [over_planes(): lax.ppermute(x, 'seq', [(i, (i // 2 ^ turn) * 2 + i % 2) for i in range(s...]
    ppermute x5 -> x4, starting transfers between devices: 6.16 us -> 5.56 us  [beside(): return lax.ppermute(x, 'seq', [(i, i ^ 1) for i in range(seq)])]
  transfers between devices with their start and end apart: 16 -> 15, of which waited for: 8 -> 8; matrix products, arithmetic and copies ran while one was open for 0% -> 0% of each run, Pallas kernels for 14% -> 16%
where the time goes in v2:
time: 44.3 us; the launch traced here: 44.1 us
  starting transfers between devices  17.1 us (39%)
  waiting for transfers between devices  15.6 us (35%)
  Pallas kernels  9 us (20%)
  local copies, waits for them, and re-layouts  1.36 us (3%)
  between operations  0.89 us (2%)
    pallas_call x10, Pallas kernels, call(): pl.pallas_call(run, out_shape=outs, in_specs=([VMEM] * count if specs is...  9 us
    ppermute x6, starting transfers between devices, over_planes(): lax.ppermute(x, 'seq', [(i, (i // 2 ^ turn) * 2 + i % 2) for i in range(s...  8.91 us
    ppermute x4, waiting for transfers between devices, beside(): return lax.ppermute(x, 'seq', [(i, i ^ 1) for i in range(seq)])  7.76 us
    ppermute x4, starting transfers between devices, beside(): return lax.ppermute(x, 'seq', [(i, i ^ 1) for i in range(seq)])  5.56 us
    ppermute x5, waiting for transfers between devices, over_tp(): return lax.ppermute(x, 'tp', [(i, i ^ k) for i in range(tp)])  4.89 us
    ppermute x6, waiting for transfers between devices, over_planes(): lax.ppermute(x, 'seq', [(i, (i // 2 ^ turn) * 2 + i % 2) for i in range(s...  2.94 us
    ppermute x5, starting transfers between devices, over_tp(): return lax.ppermute(x, 'tp', [(i, i ^ k) for i in range(tp)])  2.66 us
    dynamic_slice x1, local copies, waits for them, and re-layouts, body_twin(): lax.dynamic_index_in_dim(x, me ^ turn, 0, False)  1.29 us
  transfers between devices with their start and end apart: 15, of which 8 were waited for; matrix products, arithmetic and copies ran while one was open for 0% of the time, Pallas kernels for 16%

profile of v2, /device:TPU:0, one launch (start us, length us, event | category | flops | bytes accessed | tf_op | source)
XLA Modules:
  0.0 44.1 jit_solution(7566764597738573830)
XLA Ops:
  0.7 1.3 %constant_dynamic-slice_fusion.4 = (bf16[1,128,512]{2,1,0:T(8,128)(2,1)S(1)}, bf16[1,128,512]{2,1,0:T(8,128)(2,1)S(1)}, bf16[1,128,512]{2,1,0:T(8,128)(2,1)S(1)}...) fusion(bf16[4,128,512]{2,1,0:T(8,128)(2,1)} %refs_2_.5, ...), kind=kLoop, calls=%fused_computation.9 | loop fusion | bytes 1572876 | tf_op jit(solution)/shard_map/jit(dynamic_index_in_dim)/dynamic_slice | solution.py:765
  2.2 3.0 %collective-permute-start = (bf16[3,2,128,512]{3,2,1,0:T(8,128)(2,1)S(1)}, bf16[3,2,128,512]{3,2,1,0:T(8,128)(2,1)S(1)}, u32[]{:S(2)}, u32[]{:S(2)}) collective-permute-start(bf16[3,2,128,512]{3,2,1,0:T(8,128)(2,1)S(1)} %pad_maximum_fusion), channel_id=1, source_target_pairs={{0,4},{4,0},{8,12},{12,8},{16,20},{20,16},{24,28},{28,24},{1,5},{5... | collective-permute-start | bytes 2359304 | tf_op jit(solution)/shard_map/ppermute | solution.py:757
  5.2 2.2 %twin_load.1 = (bf16[2048,512]{1,0:T(8,128)(2,1)S(1)}, bf16[2048,512]{1,0:T(8,128)(2,1)S(1)}) custom-call(bf16[2048,512]{1,0:T(8,128)(2,1)} %refs_0_.3, bf16[2048,512]{1,0:T(8,128)(2,1)} %refs_1_.4), custom_call_target="tpu_custom_call" | custom-call | tf_op jit(solution)/shard_map/twin_load/pallas_call | solution.py:743
  7.4 0.9 %twin_project_qk.1 = (f32[32,512]{1,0:T(8,128)S(1)}, f32[32,512]{1,0:T(8,128)S(1)}, f32[8,256]{1,0:T(8,128)S(1)}) custom-call(bf16[32,2048]{1,0:T(8,128)(2,1)S(1)} %copy-done.4, bf16[2048,512]{1,0:T(8,128)(2,1)S(1)} %get-tuple-element.29.refs_1_, bf16[2048,512]{1,0:T(8,128)(2,1)S(1)} %get-tuple-element.30.refs_2_), custom_call_target="tpu_custom_call" | custom-call | tf_op jit(solution)/shard_map/twin_project_qk/pallas_call | solution.py:743
  8.4 0.7 %collective-permute-start.1 = (f32[8,256]{1,0:T(8,128)S(1)}, f32[8,256]{1,0:T(8,128)S(1)}, u32[]{:S(2)}, u32[]{:S(2)}) collective-permute-start(f32[8,256]{1,0:T(8,128)S(1)} %get-tuple-element.35.refs_7_), channel_id=1, source_target_pairs={{0,3},{1,2},{2,1},{3,0},{4,7},{5,6},{6,5},{7,4},{8,11},{9,10},{10,... | collective-permute-start | bytes 24584 | tf_op jit(solution)/shard_map/ppermute | solution.py:754
  9.2 0.9 %collective-permute-start.2 = (f32[8,256]{1,0:T(8,128)S(1)}, f32[8,256]{1,0:T(8,128)S(1)}, u32[]{:S(2)}, u32[]{:S(2)}) collective-permute-start(f32[8,256]{1,0:T(8,128)S(1)} %get-tuple-element.35.refs_7_), channel_id=1, source_target_pairs={{0,2},{1,3},{2,0},{3,1},{4,6},{5,7},{6,4},{7,5},{8,10},{9,11},{10,... | collective-permute-start | bytes 24584 | tf_op jit(solution)/shard_map/ppermute | solution.py:754
  10.9 1.2 %twin_tree.1 = (f32[64,32]{1,0:T(8,128)S(1)}, s32[4,1,64]{2,1,0:T(1,128)S(1)}, f32[32,128]{1,0:T(8,128)S(1)}, f32[32,128]{1,0:T(8,128)S(1)}, s32[4,256]{1,0:T(4,128)S(1)}) custom-call(s32[1,4]{1,0:T(1,128)S(1)} %bitcast.14, s32[1,4]{1,0:T(1,128)S(1)} %bitcast.15, s32[4,64]{1,0:T(4,128)S(1)} %copy-done.8, f32[1,128]{1,0:T(1,128)S(1)} %fusion.2.refs_3_), custom_call_target="tpu_custom_call" | custom-call | tf_op jit(solution)/shard_map/twin_tree/pallas_call | solution.py:743
  12.0 0.8 %collective-permute-done.2.refs_9_ = f32[8,256]{1,0:T(8,128)S(1)} collective-permute-done((f32[8,256]{1,0:T(8,128)S(1)}, f32[8,256]{1,0:T(8,128)S(1)}, u32[]{:S(2)}, u32[]{:S(2)}) %collective-permute-start.2) | collective-permute-done | bytes 8224 | tf_op jit(solution)/shard_map/ppermute | solution.py:754
  13.1 3.7 %collective-permute-start.5 = (bf16[32,1536]{1,0:T(8,128)(2,1)S(1)}, bf16[32,1536]{1,0:T(8,128)(2,1)S(1)}, u32[]{:S(2)}, u32[]{:S(2)}) collective-permute-start(bf16[32,1536]{1,0:T(8,128)(2,1)S(1)} %get-tuple-element.36.refs_5_.refs_3_), channel_id=1, source_target_pairs={{0,24},{4,28},{8,16},{12,20},{16,8},{20,12},{24,0},{28,4},{1,25},{... | collective-permute-start | bytes 294920 | tf_op jit(solution)/shard_map/ppermute | solution.py:760
  16.8 0.8 %collective-permute-start.7 = (bf16[32,1536]{1,0:T(8,128)(2,1)S(1)}, bf16[32,1536]{1,0:T(8,128)(2,1)S(1)}, u32[]{:S(2)}, u32[]{:S(2)}) collective-permute-start(bf16[32,1536]{1,0:T(8,128)(2,1)S(1)} %get-tuple-element.36.refs_5_.refs_3_), channel_id=1, source_target_pairs={{0,8},{4,12},{8,0},{12,4},{16,24},{20,28},{24,16},{28,20},{1,9},{5... | collective-permute-start | bytes 294920 | tf_op jit(solution)/shard_map/ppermute | solution.py:760
  18.1 5.3 %collective-permute-done.4.refs_6_ = bf16[32,512]{1,0:T(8,128)(2,1)S(1)} collective-permute-done((bf16[32,512]{1,0:T(8,128)(2,1)S(1)}, bf16[32,512]{1,0:T(8,128)(2,1)S(1)}, u32[]{:S(2)}, u32[]{:S(2)}) %collective-permute-start.4) | collective-permute-done | bytes 32800 | tf_op jit(solution)/shard_map/ppermute | solution.py:757
  23.4 1.9 %collective-permute-done.6.refs_8_.refs_5_ = bf16[32,1536]{1,0:T(8,128)(2,1)S(1)} collective-permute-done((bf16[32,1536]{1,0:T(8,128)(2,1)S(1)}, bf16[32,1536]{1,0:T(8,128)(2,1)S(1)}, u32[]{:S(2)}, u32[]{:S(2)}) %collective-permute-start.6) | collective-permute-done | bytes 98336 | tf_op jit(solution)/shard_map/ppermute | solution.py:760
  25.3 1.1 %twin_attend.1 = (bf16[48,512]{1,0:T(8,128)(2,1)S(1)}, bf16[48,512]{1,0:T(8,128)(2,1)S(1)}, bf16[48,512]{1,0:T(8,128)(2,1)S(1)}, bf16[48,512]{1,0:T(8,128)(2,1)S...) custom-call(s32[4,256]{1,0:T(4,128)S(1)} %get-tuple-element.27.refs_0_, bf16[4,128,512]{2,1,0:T(8,128)(2,1)S(1)} %copy-done, ...), custom_call_target="tpu_custom_call" | custom-call | tf_op jit(solution)/shard_map/twin_attend/pallas_call | solution.py:743
  26.4 2.5 %collective-permute-start.10 = (bf16[48,512]{1,0:T(8,128)(2,1)S(1)}, bf16[48,512]{1,0:T(8,128)(2,1)S(1)}, u32[]{:S(2)}, u32[]{:S(2)}) collective-permute-start(bf16[48,512]{1,0:T(8,128)(2,1)S(1)} %get-tuple-element.40), channel_id=1, source_target_pairs={{0,24},{4,28},{8,16},{12,20},{16,8},{20,12},{24,0},{28,4},{1,25},{... | collective-permute-start | bytes 147464 | tf_op jit(solution)/shard_map/ppermute | solution.py:760
  29.0 1.9 %collective-permute-start.8 = (bf16[48,512]{1,0:T(8,128)(2,1)S(1)}, bf16[48,512]{1,0:T(8,128)(2,1)S(1)}, u32[]{:S(2)}, u32[]{:S(2)}) collective-permute-start(bf16[48,512]{1,0:T(8,128)(2,1)S(1)} %get-tuple-element.38), channel_id=1, source_target_pairs={{0,8},{4,12},{8,0},{12,4},{16,24},{20,28},{24,16},{28,20},{1,9},{5... | collective-permute-start | bytes 147464 | tf_op jit(solution)/shard_map/ppermute | solution.py:760
  31.4 1.5 %collective-permute-start.14 = (bf16[288,512]{1,0:T(8,128)(2,1)S(1)}, bf16[288,512]{1,0:T(8,128)(2,1)S(1)}, u32[]{:S(2)}, u32[]{:S(2)}) collective-permute-start(bf16[288,512]{1,0:T(8,128)(2,1)S(1)} %get-tuple-element.48), channel_id=1, source_target_pairs={{0,4},{4,0},{8,12},{12,8},{16,20},{20,16},{24,28},{28,24},{1,5},{5... | collective-permute-start | bytes 884744 | tf_op jit(solution)/shard_map/ppermute | solution.py:757
  32.9 1.0 %collective-permute-done.11.refs_3_ = bf16[48,512]{1,0:T(8,128)(2,1)S(1)} collective-permute-done((bf16[48,512]{1,0:T(8,128)(2,1)S(1)}, bf16[48,512]{1,0:T(8,128)(2,1)S(1)}, u32[]{:S(2)}, u32[]{:S(2)}) %collective-permute-start.11) | collective-permute-done | bytes 49184 | tf_op jit(solution)/shard_map/ppermute | solution.py:760
  34.0 1.6 %collective-permute-done.9.refs_1_ = bf16[48,512]{1,0:T(8,128)(2,1)S(1)} collective-permute-done((bf16[48,512]{1,0:T(8,128)(2,1)S(1)}, bf16[48,512]{1,0:T(8,128)(2,1)S(1)}, u32[]{:S(2)}, u32[]{:S(2)}) %collective-permute-start.9) | collective-permute-done | bytes 49184 | tf_op jit(solution)/shard_map/ppermute | solution.py:757
  35.6 0.8 %twin_merge_and_project.1 = (f32[32,2048]{1,0:T(8,128)S(1)}, bf16[32,2048]{1,0:T(8,128)(2,1)S(1)}) custom-call(bf16[48,512]{1,0:T(8,128)(2,1)S(1)} %collective-permute-done.8.refs_0_, bf16[48,512]{1,0:T(8,128)(2,1)S(1)} %collective-permute-done.9.refs_1_, bf16[48,512]{1,0:T(8,128)(2,1)S(1)} %collective-permute-done.10.refs_2_, ...), custom_call_target="tpu_custom_call" | custom-call | tf_op jit(solution)/shard_map/twin_merge_and_project/pallas_call | solution.py:743
  36.4 1.3 %collective-permute-done.12.refs_1_ = bf16[32,2048]{1,0:T(8,128)(2,1)S(1)} collective-permute-done((bf16[32,2048]{1,0:T(8,128)(2,1)S(1)}, bf16[32,2048]{1,0:T(8,128)(2,1)S(1)}, u32[]{:S(2)}, u32[]{:S(2)}) %collective-permute-start.12) | collective-permute-done | bytes 131104 | tf_op jit(solution)/shard_map/ppermute | solution.py:754
  38.5 0.8 %collective-permute-done.14.refs_7_ = bf16[288,512]{1,0:T(8,128)(2,1)S(1)} collective-permute-done((bf16[288,512]{1,0:T(8,128)(2,1)S(1)}, bf16[288,512]{1,0:T(8,128)(2,1)S(1)}, u32[]{:S(2)}, u32[]{:S(2)}) %collective-permute-start.14) | collective-permute-done | bytes 294944 | tf_op jit(solution)/shard_map/ppermute | solution.py:757
  39.3 1.4 %twin_compact.1 = (bf16[4,128,512]{2,1,0:T(8,128)(2,1)}, bf16[4,128,512]{2,1,0:T(8,128)(2,1)}) custom-call(s32[4,1,64]{2,1,0:T(1,128)S(1)} %get-tuple-element.47.refs_0_, bf16[4,128,512]{2,1,0:T(8,128)(2,1)S(1)} %copy-done, bf16[4,128,512]{2,1,0:T(8,128)(2,1)S(1)} %copy-done.1, bf16[32,1536]{1,0:T(8,128)(2,1)S(1)} %get-tuple-element.36.refs_5_.refs_3_, ...), custom_call_target="tpu_custom_call" | custom-call | tf_op jit(solution)/shard_map/twin_compact/pallas_call | solution.py:743
  40.7 2.7 %collective-permute-done.13.refs_1_ = bf16[32,2048]{1,0:T(8,128)(2,1)S(1)} collective-permute-done((bf16[32,2048]{1,0:T(8,128)(2,1)S(1)}, bf16[32,2048]{1,0:T(8,128)(2,1)S(1)}, u32[]{:S(2)}, u32[]{:S(2)}) %collective-permute-start.13) | collective-permute-done | bytes 131104 | tf_op jit(solution)/shard_map/ppermute | solution.py:754
  43.4 0.7 %twin_finish.1 = bf16[32,512]{1,0:T(8,128)(2,1)} custom-call(f32[32,2048]{1,0:T(8,128)S(1)} %get-tuple-element.45.refs_0_, bf16[32,2048]{1,0:T(8,128)(2,1)S(1)} %collective-permute-done.13.refs_1_, f32[1,512]{1,0:T(1,128)S(1)} %bitcast.13, bf16[32,2048]{1,0:T(8,128)(2,1)S(1)} %copy-done.4), custom_call_target="tpu_custom_call" | custom-call | tf_op jit(solution)/shard_map/twin_finish/pallas_call | solution.py:743
  (44 shorter events, 3.0 us)
Async XLA Ops:
  2.2 5.2 %copy-start.4 = (bf16[32,2048]{1,0:T(8,128)(2,1)S(1)}, bf16[32,2048]{1,0:T(8,128)(2,1)}, u32[]{:S(2)}) copy-start(bf16[32,2048]{1,0:T(8,128)(2,1)} %refs_3_.1) | copy-start | bytes 393220
  2.2 23.1 %collective-permute-start = (bf16[3,2,128,512]{3,2,1,0:T(8,128)(2,1)S(1)}, bf16[3,2,128,512]{3,2,1,0:T(8,128)(2,1)S(1)}, u32[]{:S(2)}, u32[]{:S(2)}) collective-permute-start(bf16[3,2,128,512]{3,2,1,0:T(8,128)(2,1)S(1)} %pad_maximum_fusion), channel_id=1, source_target_pairs={{0,4},{4,0},{8,12},{12,8},{16,20},{20,16},{24,28},{28,24},{1,5},{5... | collective-permute-start | bytes 2359304 | tf_op jit(solution)/shard_map/ppermute | solution.py:757
  7.4 3.0 %copy-start.3 = (bf16[2048,512]{1,0:T(8,128)(2,1)S(1)}, bf16[2048,512]{1,0:T(8,128)(2,1)}, u32[]{:S(2)}) copy-start(bf16[2048,512]{1,0:T(8,128)(2,1)} %refs_1_.5) | copy-start | bytes 6291460
  8.3 2.5 %copy-start.9 = (s32[4]{0:T(128)S(1)}, s32[4]{0:T(128)}, u32[]{:S(2)}) copy-start(s32[4]{0:T(128)} %param.23) | copy-start | bytes 52
  8.4 4.5 %copy-start.5 = (f32[512]{0:T(512)S(1)}, f32[512]{0:T(512)}, u32[]{:S(2)}) copy-start(f32[512]{0:T(512)} %param.18) | copy-start | bytes 6148
  8.4 4.5 %copy-start.6 = (f32[512]{0:T(512)S(1)}, f32[512]{0:T(512)}, u32[]{:S(2)}) copy-start(f32[512]{0:T(512)} %param.19) | copy-start | bytes 6148
  8.4 16.9 %copy-start = (bf16[4,128,512]{2,1,0:T(8,128)(2,1)S(1)}, bf16[4,128,512]{2,1,0:T(8,128)(2,1)}, u32[]{:S(2)}) copy-start(bf16[4,128,512]{2,1,0:T(8,128)(2,1)} %refs_1_.7) | copy-start | bytes 1572868
  8.4 16.9 %copy-start.1 = (bf16[4,128,512]{2,1,0:T(8,128)(2,1)S(1)}, bf16[4,128,512]{2,1,0:T(8,128)(2,1)}, u32[]{:S(2)}) copy-start(bf16[4,128,512]{2,1,0:T(8,128)(2,1)} %refs_2_.5) | copy-start | bytes 1572868
  8.4 3.6 %collective-permute-start.1 = (f32[8,256]{1,0:T(8,128)S(1)}, f32[8,256]{1,0:T(8,128)S(1)}, u32[]{:S(2)}, u32[]{:S(2)}) collective-permute-start(f32[8,256]{1,0:T(8,128)S(1)} %get-tuple-element.35.refs_7_), channel_id=1, source_target_pairs={{0,3},{1,2},{2,1},{3,0},{4,7},{5,6},{6,5},{7,4},{8,11},{9,10},{10,... | collective-permute-start | bytes 24584 | tf_op jit(solution)/shard_map/ppermute | solution.py:754
  9.2 3.7 %collective-permute-start.2 = (f32[8,256]{1,0:T(8,128)S(1)}, f32[8,256]{1,0:T(8,128)S(1)}, u32[]{:S(2)}, u32[]{:S(2)}) collective-permute-start(f32[8,256]{1,0:T(8,128)S(1)} %get-tuple-element.35.refs_7_), channel_id=1, source_target_pairs={{0,2},{1,3},{2,0},{3,1},{4,6},{5,7},{6,4},{7,5},{8,10},{9,11},{10,... | collective-permute-start | bytes 24584 | tf_op jit(solution)/shard_map/ppermute | solution.py:754
  10.1 2.8 %collective-permute-start.3 = (f32[8,256]{1,0:T(8,128)S(1)}, f32[8,256]{1,0:T(8,128)S(1)}, u32[]{:S(2)}, u32[]{:S(2)}) collective-permute-start(f32[8,256]{1,0:T(8,128)S(1)} %get-tuple-element.35.refs_7_), channel_id=1, source_target_pairs={{0,1},{1,0},{2,3},{3,2},{4,5},{5,4},{6,7},{7,6},{8,9},{9,8},{10,11... | collective-permute-start | bytes 24584 | tf_op jit(solution)/shard_map/ppermute | solution.py:754
  10.4 25.2 %copy-start.2 = (bf16[512,2048]{1,0:T(8,128)(2,1)S(1)}, bf16[512,2048]{1,0:T(8,128)(2,1)}, u32[]{:S(2)}) copy-start(bf16[512,2048]{1,0:T(8,128)(2,1)} %refs_5_.1) | copy-start | bytes 6291460
  13.1 10.3 %collective-permute-start.5 = (bf16[32,1536]{1,0:T(8,128)(2,1)S(1)}, bf16[32,1536]{1,0:T(8,128)(2,1)S(1)}, u32[]{:S(2)}, u32[]{:S(2)}) collective-permute-start(bf16[32,1536]{1,0:T(8,128)(2,1)S(1)} %get-tuple-element.36.refs_5_.refs_3_), channel_id=1, source_target_pairs={{0,24},{4,28},{8,16},{12,20},{16,8},{20,12},{24,0},{28,4},{1,25},{... | collective-permute-start | bytes 294920 | tf_op jit(solution)/shard_map/ppermute | solution.py:760
  16.8 8.5 %collective-permute-start.6 = (bf16[32,1536]{1,0:T(8,128)(2,1)S(1)}, bf16[32,1536]{1,0:T(8,128)(2,1)S(1)}, u32[]{:S(2)}, u32[]{:S(2)}) collective-permute-start(bf16[32,1536]{1,0:T(8,128)(2,1)S(1)} %get-tuple-element.36.refs_5_.refs_3_), channel_id=1, source_target_pairs={{0,16},{4,20},{8,24},{12,28},{16,0},{20,4},{24,8},{28,12},{1,17},{... | collective-permute-start | bytes 294920 | tf_op jit(solution)/shard_map/ppermute | solution.py:760
  16.8 8.5 %collective-permute-start.7 = (bf16[32,1536]{1,0:T(8,128)(2,1)S(1)}, bf16[32,1536]{1,0:T(8,128)(2,1)S(1)}, u32[]{:S(2)}, u32[]{:S(2)}) collective-permute-start(bf16[32,1536]{1,0:T(8,128)(2,1)S(1)} %get-tuple-element.36.refs_5_.refs_3_), channel_id=1, source_target_pairs={{0,8},{4,12},{8,0},{12,4},{16,24},{20,28},{24,16},{28,20},{1,9},{5... | collective-permute-start | bytes 294920 | tf_op jit(solution)/shard_map/ppermute | solution.py:760
  17.6 5.9 %collective-permute-start.4 = (bf16[32,512]{1,0:T(8,128)(2,1)S(1)}, bf16[32,512]{1,0:T(8,128)(2,1)S(1)}, u32[]{:S(2)}, u32[]{:S(2)}) collective-permute-start(bf16[32,512]{1,0:T(8,128)(2,1)S(1)} %get-tuple-element.37), channel_id=1, source_target_pairs={{0,4},{4,0},{8,12},{12,8},{16,20},{20,16},{24,28},{28,24},{1,5},{5... | collective-permute-start | bytes 98312 | tf_op jit(solution)/shard_map/ppermute | solution.py:757
  26.4 6.5 %collective-permute-start.10 = (bf16[48,512]{1,0:T(8,128)(2,1)S(1)}, bf16[48,512]{1,0:T(8,128)(2,1)S(1)}, u32[]{:S(2)}, u32[]{:S(2)}) collective-permute-start(bf16[48,512]{1,0:T(8,128)(2,1)S(1)} %get-tuple-element.40), channel_id=1, source_target_pairs={{0,24},{4,28},{8,16},{12,20},{16,8},{20,12},{24,0},{28,4},{1,25},{... | collective-permute-start | bytes 147464 | tf_op jit(solution)/shard_map/ppermute | solution.py:760
  29.0 5.0 %collective-permute-start.11 = (bf16[48,512]{1,0:T(8,128)(2,1)S(1)}, bf16[48,512]{1,0:T(8,128)(2,1)S(1)}, u32[]{:S(2)}, u32[]{:S(2)}) collective-permute-start(bf16[48,512]{1,0:T(8,128)(2,1)S(1)} %get-tuple-element.41), channel_id=1, source_target_pairs={{0,16},{4,20},{8,24},{12,28},{16,0},{20,4},{24,8},{28,12},{1,17},{... | collective-permute-start | bytes 147464 | tf_op jit(solution)/shard_map/ppermute | solution.py:760
  29.0 5.0 %collective-permute-start.8 = (bf16[48,512]{1,0:T(8,128)(2,1)S(1)}, bf16[48,512]{1,0:T(8,128)(2,1)S(1)}, u32[]{:S(2)}, u32[]{:S(2)}) collective-permute-start(bf16[48,512]{1,0:T(8,128)(2,1)S(1)} %get-tuple-element.38), channel_id=1, source_target_pairs={{0,8},{4,12},{8,0},{12,4},{16,24},{20,28},{24,16},{28,20},{1,9},{5... | collective-permute-start | bytes 147464 | tf_op jit(solution)/shard_map/ppermute | solution.py:760
  30.9 4.7 %collective-permute-start.9 = (bf16[48,512]{1,0:T(8,128)(2,1)S(1)}, bf16[48,512]{1,0:T(8,128)(2,1)S(1)}, u32[]{:S(2)}, u32[]{:S(2)}) collective-permute-start(bf16[48,512]{1,0:T(8,128)(2,1)S(1)} %get-tuple-element.39), channel_id=1, source_target_pairs={{0,4},{4,0},{8,12},{12,8},{16,20},{20,16},{24,28},{28,24},{1,5},{5... | collective-permute-start | bytes 147464 | tf_op jit(solution)/shard_map/ppermute | solution.py:757
  31.4 7.9 %collective-permute-start.14 = (bf16[288,512]{1,0:T(8,128)(2,1)S(1)}, bf16[288,512]{1,0:T(8,128)(2,1)S(1)}, u32[]{:S(2)}, u32[]{:S(2)}) collective-permute-start(bf16[288,512]{1,0:T(8,128)(2,1)S(1)} %get-tuple-element.48), channel_id=1, source_target_pairs={{0,4},{4,0},{8,12},{12,8},{16,20},{20,16},{24,28},{28,24},{1,5},{5... | collective-permute-start | bytes 884744 | tf_op jit(solution)/shard_map/ppermute | solution.py:757
  35.6 7.8 %copy-start.7 = (f32[512]{0:T(512)S(1)}, f32[512]{0:T(512)}, u32[]{:S(2)}) copy-start(f32[512]{0:T(512)} %param.20) | copy-start | bytes 6148
  36.3 1.4 %collective-permute-start.12 = (bf16[32,2048]{1,0:T(8,128)(2,1)S(1)}, bf16[32,2048]{1,0:T(8,128)(2,1)S(1)}, u32[]{:S(2)}, u32[]{:S(2)}) collective-permute-start(bf16[32,2048]{1,0:T(8,128)(2,1)S(1)} %get-tuple-element.44), channel_id=1, source_target_pairs={{0,1},{1,0},{2,3},{3,2},{4,5},{5,4},{6,7},{7,6},{8,9},{9,8},{10,11... | collective-permute-start | bytes 393224 | tf_op jit(solution)/shard_map/ppermute | solution.py:754
  37.8 5.6 %collective-permute-start.13 = (bf16[32,2048]{1,0:T(8,128)(2,1)S(1)}, bf16[32,2048]{1,0:T(8,128)(2,1)S(1)}, u32[]{:S(2)}, u32[]{:S(2)}) collective-permute-start(bf16[32,2048]{1,0:T(8,128)(2,1)S(1)} %get-tuple-element.46), channel_id=1, source_target_pairs={{0,2},{1,3},{2,0},{3,1},{4,6},{5,7},{6,4},{7,5},{8,10},{9,11},{10,... | collective-permute-start | bytes 393224 | tf_op jit(solution)/shard_map/ppermute | solution.py:754
  (2 other events, 5.0 us)

commit v3 on v2

--- a/solution.py
+++ b/solution.py
@@ -446,22 +446,6 @@
     return lax.axis_index("seq") // 2
 
 
-def twin_load(wq, wk, wq_v, wk_v, sems):
-    chunks = sems.shape[1]
-    depth = wq.shape[0] // chunks
-    copies = []
-    for at, (source, target) in enumerate(((wq, wq_v), (wk, wk_v))):
-        for c in range(chunks):
-            rows = pl.ds(c * depth, depth)
-            copies.append(
-                pltpu.make_async_copy(source.at[rows], target.at[rows], sems.at[at, c])
-            )
-    for copy in copies:
-        copy.start()
-    for copy in copies:
-        copy.wait()
-
-
 def twin_project_qk(hidden, wq, wk, query_raw, key_raw, squares):
     rows = hidden[...]
     own = rows.shape[0]
@@ -573,29 +557,16 @@
     out[own : own + 16, :] = flat.astype(BF16)
 
 
-def twin_attend(far, limits, key_cache, value_cache, swapped, own_tree, mine, other, *refs):
-    count = len(far)
-    queries, outs = refs[:count], refs[count : 2 * count]
-    crossing, local, copied, scores, own_scores = refs[2 * count :]
+def attend_planes(turns, row, limits, key_cache, value_cache, swapped, queries, outs, scores):
     block, width = key_cache.shape[1:]
     heads = width // HEAD_DIM
-    own = other.shape[0]
+    own = queries[0].shape[0]
     me = lax.axis_index("seq")
     factor = 1.0 / math.sqrt(HEAD_DIM)
     place = iota((1, block), 1)
     both = jnp.concatenate([me * block + place, (me ^ 1) * block + place], axis=1)
-    visible = [both < limits[at + 1 : at + 2, :] for at in range(count)]
-    here = jnp.broadcast_to((me * block + place) < limits[:1, :block], (2 * own, block))
-    near = jnp.concatenate(
-        [
-            jnp.where(here, 1.0, 0.0),
-            own_tree[...],
-            jnp.zeros((2 * own, own_scores.shape[2] - block - own), F32),
-        ],
-        axis=1,
-    )
-    near = near > 0.5
-    for at, turn in enumerate(far):
+    visible = [both < limits[row + at : row + at + 1, :] for at in range(len(turns))]
+    for at, turn in enumerate(turns):
         for h in range(heads):
             lanes = slice(h * HEAD_DIM, (h + 1) * HEAD_DIM)
             q = queries[at][:, lanes]
@@ -603,17 +574,7 @@
             second = dot_t(q, swapped[at, 0, :, lanes])
             product = jnp.concatenate([first, second], axis=1) * factor
             scores[at, h] = jnp.where(visible[at], product, NEG)
-    pair = stacked([mine[:, :width], other[...]])
-    rest = own_scores.shape[2] - block - own
-    for h in range(heads):
-        lanes = slice(h * HEAD_DIM, (h + 1) * HEAD_DIM)
-        keys = jnp.concatenate(
-            [mine[:, width + h * HEAD_DIM : width + (h + 1) * HEAD_DIM]] * (1 + rest // own), axis=0
-        )
-        first = dot_t(pair[:, lanes], key_cache[plane(), :, lanes])
-        product = jnp.concatenate([first, dot_t(pair[:, lanes], keys)], axis=1) * factor
-        own_scores[h] = jnp.where(near, product, NEG)
-    for at, turn in enumerate(far):
+    for at, turn in enumerate(turns):
         stats = jnp.zeros((own, LANES), F32)
         for h in range(heads):
             lanes = slice(h * HEAD_DIM, (h + 1) * HEAD_DIM)
@@ -623,6 +584,43 @@
             outs[at][:own, lanes] = out.astype(BF16)
             stats = kept(stats, h, heads, found)
         write_stats(stats, outs[at])
+
+
+def twin_attend_far(turns, limits, key_cache, value_cache, swapped, *refs):
+    count = len(turns)
+    queries, outs, scores = refs[:count], refs[count : 2 * count], refs[2 * count]
+    attend_planes(turns, 1, limits, key_cache, value_cache, swapped, queries, outs, scores)
+
+
+def twin_attend_near(
+    turns, row, limits, key_cache, value_cache, swapped, own_tree, mine, other, *refs
+):
+    count = row - 1 + len(turns)
+    queries, outs = refs[:count], refs[count : count + len(turns)]
+    crossing, local, copied, scores, own_scores = refs[count + len(turns) :]
+    attend_planes(
+        turns, row, limits, key_cache, value_cache, swapped, queries[row - 1 :], outs, scores
+    )
+    block, width = key_cache.shape[1:]
+    heads = width // HEAD_DIM
+    own = other.shape[0]
+    factor = 1.0 / math.sqrt(HEAD_DIM)
+    place = lax.axis_index("seq") * block + iota((1, block), 1)
+    here = jnp.broadcast_to(place < limits[:1, :block], (2 * own, block))
+    rest = own_scores.shape[2] - block - own
+    near = jnp.concatenate(
+        [jnp.where(here, 1.0, 0.0), own_tree[...], jnp.zeros((2 * own, rest), F32)], axis=1
+    )
+    near = near > 0.5
+    pair = stacked([mine[:, :width], other[...]])
+    for h in range(heads):
+        lanes = slice(h * HEAD_DIM, (h + 1) * HEAD_DIM)
+        keys = jnp.concatenate(
+            [mine[:, width + h * HEAD_DIM : width + (h + 1) * HEAD_DIM]] * (1 + rest // own), axis=0
+        )
+        first = dot_t(pair[:, lanes], key_cache[plane(), :, lanes])
+        product = jnp.concatenate([first, dot_t(pair[:, lanes], keys)], axis=1) * factor
+        own_scores[h] = jnp.where(near, product, NEG)
     stats = jnp.zeros((2 * own, LANES), F32)
     for h in range(heads):
         lanes = slice(h * HEAD_DIM, (h + 1) * HEAD_DIM)
@@ -640,8 +638,8 @@
         for part in range(2):
             rows = slice((2 * at + part) * own, (2 * at + part + 1) * own)
             copied[rows, :] = ref[:, (part + 1) * width : (part + 2) * width]
-    rest = copied.shape[0] - 2 * (count + 1) * own
-    copied[2 * (count + 1) * own :, :] = jnp.zeros((rest, width), BF16)
+    last = 2 * (count + 1) * own
+    copied[last:, :] = jnp.zeros((copied.shape[0] - last, width), BF16)
 
 
 def twin_rows(mine, theirs, held):
@@ -760,25 +758,19 @@
         return lax.ppermute(x, "seq", [(i, (i // 2 ^ turn) * 2 + i % 2) for i in range(seq)])
 
     me = lax.axis_index("seq") // 2
-    picked = jnp.stack(
-        [
-            jnp.stack([lax.dynamic_index_in_dim(x, me ^ turn, 0, False) for x in (key_cache, value_cache)])
-            for turn in far
+
+    def picked(turns):
+        parts = [
+            [lax.dynamic_index_in_dim(x, me ^ turn, 0, False) for x in (key_cache, value_cache)]
+            for turn in turns
         ]
-    )
-    swapped = beside(picked)
-    wq, wk = call(
-        twin_load,
-        (shaped(query_weight.shape, BF16), shaped(key_weight.shape, BF16)),
-        (query_weight, key_weight),
-        [pltpu.SemaphoreType.DMA((2, 4))],
-        mib=48,
-        specs=[ANY] * 2,
-    )
+        return jnp.stack([jnp.stack(part) for part in parts])
+
+    swapped, swapped_near = beside(picked(far[:2])), beside(picked(far[2:]))
     query_raw, key_raw, squares = call(
         twin_project_qk,
         (shaped((own, width), F32), shaped((own, width), F32), shaped((8, 2 * LANES), F32)),
-        (hidden_in, wq, wk),
+        (hidden_in, query_weight, key_weight),
     )
     all_squares = [squares] + [over_tp(squares, k) for k in range(tp - 1, 0, -1)]
 
@@ -815,26 +807,32 @@
     other = beside(queries)
 
     rows = own + 16
-    *partials, crossing, local, copied = call(
-        functools.partial(twin_attend, far),
-        (shaped((rows, width), BF16),) * (len(far) + 2)
-        + (shaped((2 * requests * own + own, width), BF16),),
-        (limits, key_cache, value_cache, swapped, own_tree, packed, other, *from_far),
+    partials = call(
+        functools.partial(twin_attend_far, far[:2]),
+        (shaped((rows, width), BF16),) * 2,
+        (limits, key_cache, value_cache, swapped, *from_far[:2]),
+        [pltpu.VMEM((2, heads, own, 2 * block), F32)],
+    )
+    near, crossing, local, copied = call(
+        functools.partial(twin_attend_near, far[2:], 3),
+        (shaped((rows, width), BF16),) * 3 + (shaped((2 * requests * own + own, width), BF16),),
+        (limits, key_cache, value_cache, swapped_near, own_tree, packed, other, *from_far),
         [
-            pltpu.VMEM((len(far), heads, own, 2 * block), F32),
+            pltpu.VMEM((1, heads, own, 2 * block), F32),
             pltpu.VMEM((heads, 2 * own, block + LANES), F32),
         ],
-    )
-    partials = [over_planes(part, turn) for part, turn in zip(partials, far)]
+        ties=partials[:1],
+    )
+    partials = [over_planes(part, turn) for part, turn in zip((*partials, near), far)]
     partials += [beside(crossing)]
-    partials = [partials[2], partials[3], partials[0], partials[1], local]
+    partials = [partials[0], partials[1], partials[2], partials[3], local]
+    copied = beside(copied)
 
     total, rounded = call(
         twin_merge_and_project,
         (shaped((own, model), F32), shaped((own, model), BF16)),
         (*partials, out_weight),
     )
-    copied = beside(copied)
     bit = 1
     while 2 * bit < tp:
         total, rounded = call(

time: 44.3 us -> 44.4 us (level)
  Pallas kernels: 9 us -> 7.53 us
  starting transfers between devices: 17.1 us -> 18.4 us
  local copies, waits for them, and re-layouts: 1.36 us -> 2.53 us
  waiting for transfers between devices: 15.6 us -> 14.8 us
    ppermute x6, waiting for transfers between devices: 2.94 us -> 6.94 us  [over_planes(): lax.ppermute(x, 'seq', [(i, (i // 2 ^ turn) * 2 + i % 2) for i in range(s...]
    ppermute x4 -> x5, waiting for transfers between devices: 7.76 us -> 3.93 us  [beside(): return lax.ppermute(x, 'seq', [(i, i ^ 1) for i in range(seq)])]
    pallas_call x10, Pallas kernels: 9 us -> 7.53 us  [call(): pl.pallas_call(run, out_shape=outs, in_specs=([VMEM] * count if specs is...]
    unnamed x22 -> x28, local copies, waits for them, and re-layouts: 0.08 us -> 1.11 us
    ppermute x5, waiting for transfers between devices: 4.89 us -> 3.9 us  [over_tp(): return lax.ppermute(x, 'tp', [(i, i ^ k) for i in range(tp)])]
    ppermute x4 -> x5, starting transfers between devices: 5.56 us -> 6.44 us  [beside(): return lax.ppermute(x, 'seq', [(i, i ^ 1) for i in range(seq)])]
  transfers between devices with their start and end apart: 15 -> 16, of which waited for: 8 -> 8; matrix products, arithmetic and copies ran while one was open for 0% -> 0% of each run, Pallas kernels for 16% -> 15%
where the time goes in v3:
time: 44.4 us; the launch traced here: 44.3 us
  starting transfers between devices  18.4 us (41%)
  waiting for transfers between devices  14.8 us (33%)
  Pallas kernels  7.53 us (17%)
  local copies, waits for them, and re-layouts  2.53 us (6%)
  between operations  0.9 us (2%)
    ppermute x6, starting transfers between devices, over_planes(): lax.ppermute(x, 'seq', [(i, (i // 2 ^ turn) * 2 + i % 2) for i in range(s...  8.96 us
    pallas_call x10, Pallas kernels, call(): pl.pallas_call(run, out_shape=outs, in_specs=([VMEM] * count if specs is...  7.53 us
    ppermute x6, waiting for transfers between devices, over_planes(): lax.ppermute(x, 'seq', [(i, (i // 2 ^ turn) * 2 + i % 2) for i in range(s...  6.94 us
    ppermute x5, starting transfers between devices, beside(): return lax.ppermute(x, 'seq', [(i, i ^ 1) for i in range(seq)])  6.44 us
    ppermute x5, waiting for transfers between devices, beside(): return lax.ppermute(x, 'seq', [(i, i ^ 1) for i in range(seq)])  3.93 us
    ppermute x5, waiting for transfers between devices, over_tp(): return lax.ppermute(x, 'tp', [(i, i ^ k) for i in range(tp)])  3.9 us
    ppermute x5, starting transfers between devices, over_tp(): return lax.ppermute(x, 'tp', [(i, i ^ k) for i in range(tp)])  2.96 us
    dynamic_slice x1, local copies, waits for them, and re-layouts, picked(): lax.dynamic_index_in_dim(x, me ^ turn, 0, False)  1.42 us
  transfers between devices with their start and end apart: 16, of which 8 were waited for; matrix products, arithmetic and copies ran while one was open for 0% of the time, Pallas kernels for 15%

profile of v3, /device:TPU:0, one launch (start us, length us, event | category | flops | bytes accessed | tf_op | source)
XLA Modules:
  0.0 44.3 jit_solution(68055514256580230)
XLA Ops:
  0.7 1.4 %constant_dynamic-slice_fusion = (bf16[1,128,512]{2,1,0:T(8,128)(2,1)S(1)}, bf16[1,128,512]{2,1,0:T(8,128)(2,1)S(1)}, bf16[1,128,512]{2,1,0:T(8,128)(2,1)S(1)}, ...) fusion(bf16[4,128,512]{2,1,0:T(8,128)(2,1)} %refs_2_.9, ...), kind=kLoop, calls=%fused_computation.5 | loop fusion | bytes 1572876 | tf_op jit(solution)/shard_map/jit(dynamic_index_in_dim)/dynamic_slice | solution.py:764
  2.2 3.0 %collective-permute-start = (bf16[2,2,128,512]{3,2,1,0:T(8,128)(2,1)S(1)}, bf16[2,2,128,512]{3,2,1,0:T(8,128)(2,1)S(1)}, u32[]{:S(2)}, u32[]{:S(2)}) collective-permute-start(bf16[2,2,128,512]{3,2,1,0:T(8,128)(2,1)S(1)} %pad_maximum_fusion), channel_id=1, source_target_pairs={{0,4},{4,0},{8,12},{12,8},{16,20},{20,16},{24,28},{28,24},{1,5},{5... | collective-permute-start | bytes 1572872 | tf_op jit(solution)/shard_map/ppermute | solution.py:755
  5.4 1.0 %copy-done.6 = bf16[32,2048]{1,0:T(8,128)(2,1)S(1)} copy-done((bf16[32,2048]{1,0:T(8,128)(2,1)S(1)}, bf16[32,2048]{1,0:T(8,128)(2,1)}, u32[]{:S(2)}) %copy-start.6) | copy-done | bytes 131096
  6.4 0.9 %twin_project_qk.1 = (f32[32,512]{1,0:T(8,128)S(1)}, f32[32,512]{1,0:T(8,128)S(1)}, f32[8,256]{1,0:T(8,128)S(1)}) custom-call(bf16[32,2048]{1,0:T(8,128)(2,1)S(1)} %copy-done.6, bf16[2048,512]{1,0:T(8,128)(2,1)S(1)} %copy-done.3, bf16[2048,512]{1,0:T(8,128)(2,1)S(1)} %copy-done.4), custom_call_target="tpu_custom_call" | custom-call | tf_op jit(solution)/shard_map/twin_project_qk/pallas_call | solution.py:741
  7.4 1.0 %collective-permute-start.1 = (f32[8,256]{1,0:T(8,128)S(1)}, f32[8,256]{1,0:T(8,128)S(1)}, u32[]{:S(2)}, u32[]{:S(2)}) collective-permute-start(f32[8,256]{1,0:T(8,128)S(1)} %get-tuple-element.30.refs_7_), channel_id=1, source_target_pairs={{0,3},{1,2},{2,1},{3,0},{4,7},{5,6},{6,5},{7,4},{8,11},{9,10},{10,... | collective-permute-start | bytes 24584 | tf_op jit(solution)/shard_map/ppermute | solution.py:752
  8.4 1.1 %collective-permute-start.2 = (f32[8,256]{1,0:T(8,128)S(1)}, f32[8,256]{1,0:T(8,128)S(1)}, u32[]{:S(2)}, u32[]{:S(2)}) collective-permute-start(f32[8,256]{1,0:T(8,128)S(1)} %get-tuple-element.30.refs_7_), channel_id=1, source_target_pairs={{0,2},{1,3},{2,0},{3,1},{4,6},{5,7},{6,4},{7,5},{8,10},{9,11},{10,... | collective-permute-start | bytes 24584 | tf_op jit(solution)/shard_map/ppermute | solution.py:752
  10.0 1.2 %twin_tree.1 = (f32[64,32]{1,0:T(8,128)S(1)}, s32[4,1,64]{2,1,0:T(1,128)S(1)}, f32[32,128]{1,0:T(8,128)S(1)}, f32[32,128]{1,0:T(8,128)S(1)}, s32[4,256]{1,0:T(4,128)S(1)}) custom-call(s32[1,4]{1,0:T(1,128)S(1)} %bitcast.14, s32[1,4]{1,0:T(1,128)S(1)} %bitcast.15, s32[4,64]{1,0:T(4,128)S(1)} %copy-done.11, f32[1,128]{1,0:T(1,128)S(1)} %fusion.2.refs_3_), custom_call_target="tpu_custom_call" | custom-call | tf_op jit(solution)/shard_map/twin_tree/pallas_call | solution.py:741
  11.2 0.8 %collective-permute-done.2.refs_9_ = f32[8,256]{1,0:T(8,128)S(1)} collective-permute-done((f32[8,256]{1,0:T(8,128)S(1)}, f32[8,256]{1,0:T(8,128)S(1)}, u32[]{:S(2)}, u32[]{:S(2)}) %collective-permute-start.2) | collective-permute-done | bytes 8224 | tf_op jit(solution)/shard_map/ppermute | solution.py:752
  12.3 3.7 %collective-permute-start.4 = (bf16[32,1536]{1,0:T(8,128)(2,1)S(1)}, bf16[32,1536]{1,0:T(8,128)(2,1)S(1)}, u32[]{:S(2)}, u32[]{:S(2)}) collective-permute-start(bf16[32,1536]{1,0:T(8,128)(2,1)S(1)} %get-tuple-element.31.refs_5_.refs_3_), channel_id=1, source_target_pairs={{0,24},{4,28},{8,16},{12,20},{16,8},{20,12},{24,0},{28,4},{1,25},{... | collective-permute-start | bytes 294920 | tf_op jit(solution)/shard_map/ppermute | solution.py:758
  16.0 0.8 %collective-permute-start.10 = (bf16[32,1536]{1,0:T(8,128)(2,1)S(1)}, bf16[32,1536]{1,0:T(8,128)(2,1)S(1)}, u32[]{:S(2)}, u32[]{:S(2)}) collective-permute-start(bf16[32,1536]{1,0:T(8,128)(2,1)S(1)} %get-tuple-element.31.refs_5_.refs_3_), channel_id=1, source_target_pairs={{0,8},{4,12},{8,0},{12,4},{16,24},{20,28},{24,16},{28,20},{1,9},{5... | collective-permute-start | bytes 294920 | tf_op jit(solution)/shard_map/ppermute | solution.py:758
  16.7 3.1 %collective-permute-done.4.refs_4_.refs_7_ = bf16[32,1536]{1,0:T(8,128)(2,1)S(1)} collective-permute-done((bf16[32,1536]{1,0:T(8,128)(2,1)S(1)}, bf16[32,1536]{1,0:T(8,128)(2,1)S(1)}, u32[]{:S(2)}, u32[]{:S(2)}) %collective-permute-start.4) | collective-permute-done | bytes 98336 | tf_op jit(solution)/shard_map/ppermute | solution.py:758
  19.9 1.3 %collective-permute-start.9 = (bf16[32,512]{1,0:T(8,128)(2,1)S(1)}, bf16[32,512]{1,0:T(8,128)(2,1)S(1)}, u32[]{:S(2)}, u32[]{:S(2)}) collective-permute-start(bf16[32,512]{1,0:T(8,128)(2,1)S(1)} %get-tuple-element.35), channel_id=1, source_target_pairs={{0,4},{4,0},{8,12},{12,8},{16,20},{20,16},{24,28},{28,24},{1,5},{5... | collective-permute-start | bytes 98312 | tf_op jit(solution)/shard_map/ppermute | solution.py:755
  21.2 3.4 %collective-permute-done.5.refs_5_.refs_8_ = bf16[32,1536]{1,0:T(8,128)(2,1)S(1)} collective-permute-done((bf16[32,1536]{1,0:T(8,128)(2,1)S(1)}, bf16[32,1536]{1,0:T(8,128)(2,1)S(1)}, u32[]{:S(2)}, u32[]{:S(2)}) %collective-permute-start.5) | collective-permute-done | bytes 98336 | tf_op jit(solution)/shard_map/ppermute | solution.py:758
  25.4 2.5 %collective-permute-start.6 = (bf16[48,512]{1,0:T(8,128)(2,1)S(1)}, bf16[48,512]{1,0:T(8,128)(2,1)S(1)}, u32[]{:S(2)}, u32[]{:S(2)}) collective-permute-start(bf16[48,512]{1,0:T(8,128)(2,1)S(1)} %get-tuple-element.32.refs_10_), channel_id=1, source_target_pairs={{0,24},{4,28},{8,16},{12,20},{16,8},{20,12},{24,0},{28,4},{1,25},{... | collective-permute-start | bytes 147464 | tf_op jit(solution)/shard_map/ppermute | solution.py:758
  28.0 1.1 %twin_attend_near.1 = (bf16[48,512]{1,0:T(8,128)(2,1)S(1)}, bf16[48,512]{1,0:T(8,128)(2,1)S(1)}, bf16[48,512]{1,0:T(8,128)(2,1)S(1)}, bf16[288,512]{1,0:T(8,128)(2,1)S(1)}) custom-call(s32[4,256]{1,0:T(4,128)S(1)} %get-tuple-element.25.refs_0_, bf16[4,128,512]{2,1,0:T(8,128)(2,1)S(1)} %copy-done, bf16[4,128,512]{2,1,0:T(8,128)(2,1)S(1)} %copy-done.1, ...), custom_call_target="tpu_custom_call" | custom-call | tf_op jit(solution)/shard_map/twin_attend_near/pallas_call | solution.py:741
  29.1 2.0 %collective-permute-start.11 = (bf16[48,512]{1,0:T(8,128)(2,1)S(1)}, bf16[48,512]{1,0:T(8,128)(2,1)S(1)}, u32[]{:S(2)}, u32[]{:S(2)}) collective-permute-start(bf16[48,512]{1,0:T(8,128)(2,1)S(1)} %get-tuple-element.36), channel_id=1, source_target_pairs={{0,8},{4,12},{8,0},{12,4},{16,24},{20,28},{24,16},{28,20},{1,9},{5... | collective-permute-start | bytes 147464 | tf_op jit(solution)/shard_map/ppermute | solution.py:758
  31.1 1.5 %collective-permute-start.12 = (bf16[48,512]{1,0:T(8,128)(2,1)S(1)}, bf16[48,512]{1,0:T(8,128)(2,1)S(1)}, u32[]{:S(2)}, u32[]{:S(2)}) collective-permute-start(bf16[48,512]{1,0:T(8,128)(2,1)S(1)} %get-tuple-element.37), channel_id=1, source_target_pairs={{0,4},{4,0},{8,12},{12,8},{16,20},{20,16},{24,28},{28,24},{1,5},{5... | collective-permute-start | bytes 147464 | tf_op jit(solution)/shard_map/ppermute | solution.py:755
  33.5 2.2 %collective-permute-done.12.refs_3_ = bf16[48,512]{1,0:T(8,128)(2,1)S(1)} collective-permute-done((bf16[48,512]{1,0:T(8,128)(2,1)S(1)}, bf16[48,512]{1,0:T(8,128)(2,1)S(1)}, u32[]{:S(2)}, u32[]{:S(2)}) %collective-permute-start.12) | collective-permute-done | bytes 49184 | tf_op jit(solution)/shard_map/ppermute | solution.py:755
  35.7 0.8 %twin_merge_and_project.1 = (f32[32,2048]{1,0:T(8,128)S(1)}, bf16[32,2048]{1,0:T(8,128)(2,1)S(1)}) custom-call(bf16[48,512]{1,0:T(8,128)(2,1)S(1)} %collective-permute-done.6.refs_0_, bf16[48,512]{1,0:T(8,128)(2,1)S(1)} %collective-permute-done.7.refs_1_, bf16[48,512]{1,0:T(8,128)(2,1)S(1)} %collective-permute-done.11.refs_2_, ...), custom_call_target="tpu_custom_call" | custom-call | tf_op jit(solution)/shard_map/twin_merge_and_project/pallas_call | solution.py:741
  36.5 1.3 %collective-permute-done.13.refs_1_ = bf16[32,2048]{1,0:T(8,128)(2,1)S(1)} collective-permute-done((bf16[32,2048]{1,0:T(8,128)(2,1)S(1)}, bf16[32,2048]{1,0:T(8,128)(2,1)S(1)}, u32[]{:S(2)}, u32[]{:S(2)}) %collective-permute-start.13) | collective-permute-done | bytes 131104 | tf_op jit(solution)/shard_map/ppermute | solution.py:752
  37.9 0.8 %collective-permute-start.14 = (bf16[32,2048]{1,0:T(8,128)(2,1)S(1)}, bf16[32,2048]{1,0:T(8,128)(2,1)S(1)}, u32[]{:S(2)}, u32[]{:S(2)}) collective-permute-start(bf16[32,2048]{1,0:T(8,128)(2,1)S(1)} %get-tuple-element.42), channel_id=1, source_target_pairs={{0,2},{1,3},{2,0},{3,1},{4,6},{5,7},{6,4},{7,5},{8,10},{9,11},{10,... | collective-permute-start | bytes 393224 | tf_op jit(solution)/shard_map/ppermute | solution.py:752
  38.7 1.7 %collective-permute-done.15.refs_7_ = bf16[288,512]{1,0:T(8,128)(2,1)S(1)} collective-permute-done((bf16[288,512]{1,0:T(8,128)(2,1)S(1)}, bf16[288,512]{1,0:T(8,128)(2,1)S(1)}, u32[]{:S(2)}, u32[]{:S(2)}) %collective-permute-start.15) | collective-permute-done | bytes 294944 | tf_op jit(solution)/shard_map/ppermute | solution.py:755
  40.4 1.4 %twin_compact.1 = (bf16[4,128,512]{2,1,0:T(8,128)(2,1)}, bf16[4,128,512]{2,1,0:T(8,128)(2,1)}) custom-call(s32[4,1,64]{2,1,0:T(1,128)S(1)} %get-tuple-element.43.refs_0_, bf16[4,128,512]{2,1,0:T(8,128)(2,1)S(1)} %copy-done, bf16[4,128,512]{2,1,0:T(8,128)(2,1)S(1)} %copy-done.1, bf16[32,1536]{1,0:T(8,128)(2,1)S(1)} %get-tuple-element.31.refs_5_.refs_3_, ...), custom_call_target="tpu_custom_call" | custom-call | tf_op jit(solution)/shard_map/twin_compact/pallas_call | solution.py:741
  41.8 1.7 %collective-permute-done.14.refs_1_ = bf16[32,2048]{1,0:T(8,128)(2,1)S(1)} collective-permute-done((bf16[32,2048]{1,0:T(8,128)(2,1)S(1)}, bf16[32,2048]{1,0:T(8,128)(2,1)S(1)}, u32[]{:S(2)}, u32[]{:S(2)}) %collective-permute-start.14) | collective-permute-done | bytes 131104 | tf_op jit(solution)/shard_map/ppermute | solution.py:752
  (52 shorter events, 3.5 us)
Async XLA Ops:
  0.7 4.7 %copy-start.3 = (bf16[2048,512]{1,0:T(8,128)(2,1)S(1)}, bf16[2048,512]{1,0:T(8,128)(2,1)}, u32[]{:S(2)}) copy-start(bf16[2048,512]{1,0:T(8,128)(2,1)} %refs_1_.5) | copy-start | bytes 6291460
  0.7 4.7 %copy-start.4 = (bf16[2048,512]{1,0:T(8,128)(2,1)S(1)}, bf16[2048,512]{1,0:T(8,128)(2,1)}, u32[]{:S(2)}) copy-start(bf16[2048,512]{1,0:T(8,128)(2,1)} %refs_2_.6) | copy-start | bytes 6291460
  2.2 22.4 %collective-permute-start = (bf16[2,2,128,512]{3,2,1,0:T(8,128)(2,1)S(1)}, bf16[2,2,128,512]{3,2,1,0:T(8,128)(2,1)S(1)}, u32[]{:S(2)}, u32[]{:S(2)}) collective-permute-start(bf16[2,2,128,512]{3,2,1,0:T(8,128)(2,1)S(1)} %pad_maximum_fusion), channel_id=1, source_target_pairs={{0,4},{4,0},{8,12},{12,8},{16,20},{20,16},{24,28},{28,24},{1,5},{5... | collective-permute-start | bytes 1572872 | tf_op jit(solution)/shard_map/ppermute | solution.py:755
  5.3 22.7 %collective-permute-start.8 = (bf16[1,2,128,512]{3,2,1,0:T(8,128)(2,1)S(1)}, bf16[1,2,128,512]{3,2,1,0:T(8,128)(2,1)S(1)}, u32[]{:S(2)}, u32[]{:S(2)}) collective-permute-start(bf16[1,2,128,512]{3,2,1,0:T(8,128)(2,1)S(1)} %maximum_bitcast_fusion.2), channel_id=1, source_target_pairs={{0,4},{4,0},{8,12},{12,8},{16,20},{20,16},{24,28},{28,24},{1,5},{5... | collective-permute-start | bytes 786440 | tf_op jit(solution)/shard_map/ppermute | solution.py:755
  7.4 4.7 %copy-start.8 = (f32[512]{0:T(512)S(1)}, f32[512]{0:T(512)}, u32[]{:S(2)}) copy-start(f32[512]{0:T(512)} %param.18) | copy-start | bytes 6148
  7.4 17.2 %copy-start = (bf16[4,128,512]{2,1,0:T(8,128)(2,1)S(1)}, bf16[4,128,512]{2,1,0:T(8,128)(2,1)}, u32[]{:S(2)}) copy-start(bf16[4,128,512]{2,1,0:T(8,128)(2,1)} %refs_1_.9) | copy-start | bytes 1572868
  7.4 17.2 %copy-start.1 = (bf16[4,128,512]{2,1,0:T(8,128)(2,1)S(1)}, bf16[4,128,512]{2,1,0:T(8,128)(2,1)}, u32[]{:S(2)}) copy-start(bf16[4,128,512]{2,1,0:T(8,128)(2,1)} %refs_2_.9) | copy-start | bytes 1572868
  7.4 3.8 %collective-permute-start.1 = (f32[8,256]{1,0:T(8,128)S(1)}, f32[8,256]{1,0:T(8,128)S(1)}, u32[]{:S(2)}, u32[]{:S(2)}) collective-permute-start(f32[8,256]{1,0:T(8,128)S(1)} %get-tuple-element.30.refs_7_), channel_id=1, source_target_pairs={{0,3},{1,2},{2,1},{3,0},{4,7},{5,6},{6,5},{7,4},{8,11},{9,10},{10,... | collective-permute-start | bytes 24584 | tf_op jit(solution)/shard_map/ppermute | solution.py:752
  8.4 3.7 %collective-permute-start.2 = (f32[8,256]{1,0:T(8,128)S(1)}, f32[8,256]{1,0:T(8,128)S(1)}, u32[]{:S(2)}, u32[]{:S(2)}) collective-permute-start(f32[8,256]{1,0:T(8,128)S(1)} %get-tuple-element.30.refs_7_), channel_id=1, source_target_pairs={{0,2},{1,3},{2,0},{3,1},{4,6},{5,7},{6,4},{7,5},{8,10},{9,11},{10,... | collective-permute-start | bytes 24584 | tf_op jit(solution)/shard_map/ppermute | solution.py:752
  9.5 2.6 %collective-permute-start.3 = (f32[8,256]{1,0:T(8,128)S(1)}, f32[8,256]{1,0:T(8,128)S(1)}, u32[]{:S(2)}, u32[]{:S(2)}) collective-permute-start(f32[8,256]{1,0:T(8,128)S(1)} %get-tuple-element.30.refs_7_), channel_id=1, source_target_pairs={{0,1},{1,0},{2,3},{3,2},{4,5},{5,4},{6,7},{7,6},{8,9},{9,8},{10,11... | collective-permute-start | bytes 24584 | tf_op jit(solution)/shard_map/ppermute | solution.py:752
  10.0 25.7 %copy-start.2 = (bf16[512,2048]{1,0:T(8,128)(2,1)S(1)}, bf16[512,2048]{1,0:T(8,128)(2,1)}, u32[]{:S(2)}) copy-start(bf16[512,2048]{1,0:T(8,128)(2,1)} %refs_5_.1) | copy-start | bytes 6291460
  12.3 7.6 %collective-permute-start.4 = (bf16[32,1536]{1,0:T(8,128)(2,1)S(1)}, bf16[32,1536]{1,0:T(8,128)(2,1)S(1)}, u32[]{:S(2)}, u32[]{:S(2)}) collective-permute-start(bf16[32,1536]{1,0:T(8,128)(2,1)S(1)} %get-tuple-element.31.refs_5_.refs_3_), channel_id=1, source_target_pairs={{0,24},{4,28},{8,16},{12,20},{16,8},{20,12},{24,0},{28,4},{1,25},{... | collective-permute-start | bytes 294920 | tf_op jit(solution)/shard_map/ppermute | solution.py:758
  16.0 8.7 %collective-permute-start.5 = (bf16[32,1536]{1,0:T(8,128)(2,1)S(1)}, bf16[32,1536]{1,0:T(8,128)(2,1)S(1)}, u32[]{:S(2)}, u32[]{:S(2)}) collective-permute-start(bf16[32,1536]{1,0:T(8,128)(2,1)S(1)} %get-tuple-element.31.refs_5_.refs_3_), channel_id=1, source_target_pairs={{0,16},{4,20},{8,24},{12,28},{16,0},{20,4},{24,8},{28,12},{1,17},{... | collective-permute-start | bytes 294920 | tf_op jit(solution)/shard_map/ppermute | solution.py:758
  16.0 12.0 %collective-permute-start.10 = (bf16[32,1536]{1,0:T(8,128)(2,1)S(1)}, bf16[32,1536]{1,0:T(8,128)(2,1)S(1)}, u32[]{:S(2)}, u32[]{:S(2)}) collective-permute-start(bf16[32,1536]{1,0:T(8,128)(2,1)S(1)} %get-tuple-element.31.refs_5_.refs_3_), channel_id=1, source_target_pairs={{0,8},{4,12},{8,0},{12,4},{16,24},{20,28},{24,16},{28,20},{1,9},{5... | collective-permute-start | bytes 294920 | tf_op jit(solution)/shard_map/ppermute | solution.py:758
  19.9 8.1 %collective-permute-start.9 = (bf16[32,512]{1,0:T(8,128)(2,1)S(1)}, bf16[32,512]{1,0:T(8,128)(2,1)S(1)}, u32[]{:S(2)}, u32[]{:S(2)}) collective-permute-start(bf16[32,512]{1,0:T(8,128)(2,1)S(1)} %get-tuple-element.35), channel_id=1, source_target_pairs={{0,4},{4,0},{8,12},{12,8},{16,20},{20,16},{24,28},{28,24},{1,5},{5... | collective-permute-start | bytes 98312 | tf_op jit(solution)/shard_map/ppermute | solution.py:755
  25.4 7.7 %collective-permute-start.6 = (bf16[48,512]{1,0:T(8,128)(2,1)S(1)}, bf16[48,512]{1,0:T(8,128)(2,1)S(1)}, u32[]{:S(2)}, u32[]{:S(2)}) collective-permute-start(bf16[48,512]{1,0:T(8,128)(2,1)S(1)} %get-tuple-element.32.refs_10_), channel_id=1, source_target_pairs={{0,24},{4,28},{8,16},{12,20},{16,8},{20,12},{24,0},{28,4},{1,25},{... | collective-permute-start | bytes 147464 | tf_op jit(solution)/shard_map/ppermute | solution.py:758
  28.0 5.1 %collective-permute-start.7 = (bf16[48,512]{1,0:T(8,128)(2,1)S(1)}, bf16[48,512]{1,0:T(8,128)(2,1)S(1)}, u32[]{:S(2)}, u32[]{:S(2)}) collective-permute-start(bf16[48,512]{1,0:T(8,128)(2,1)S(1)} %get-tuple-element.33), channel_id=1, source_target_pairs={{0,16},{4,20},{8,24},{12,28},{16,0},{20,4},{24,8},{28,12},{1,17},{... | collective-permute-start | bytes 147464 | tf_op jit(solution)/shard_map/ppermute | solution.py:758
  29.1 4.4 %collective-permute-start.11 = (bf16[48,512]{1,0:T(8,128)(2,1)S(1)}, bf16[48,512]{1,0:T(8,128)(2,1)S(1)}, u32[]{:S(2)}, u32[]{:S(2)}) collective-permute-start(bf16[48,512]{1,0:T(8,128)(2,1)S(1)} %get-tuple-element.36), channel_id=1, source_target_pairs={{0,8},{4,12},{8,0},{12,4},{16,24},{20,28},{24,16},{28,20},{1,9},{5... | collective-permute-start | bytes 147464 | tf_op jit(solution)/shard_map/ppermute | solution.py:758
  31.1 4.6 %collective-permute-start.12 = (bf16[48,512]{1,0:T(8,128)(2,1)S(1)}, bf16[48,512]{1,0:T(8,128)(2,1)S(1)}, u32[]{:S(2)}, u32[]{:S(2)}) collective-permute-start(bf16[48,512]{1,0:T(8,128)(2,1)S(1)} %get-tuple-element.37), channel_id=1, source_target_pairs={{0,4},{4,0},{8,12},{12,8},{16,20},{20,16},{24,28},{28,24},{1,5},{5... | collective-permute-start | bytes 147464 | tf_op jit(solution)/shard_map/ppermute | solution.py:755
  32.5 7.9 %collective-permute-start.15 = (bf16[288,512]{1,0:T(8,128)(2,1)S(1)}, bf16[288,512]{1,0:T(8,128)(2,1)S(1)}, u32[]{:S(2)}, u32[]{:S(2)}) collective-permute-start(bf16[288,512]{1,0:T(8,128)(2,1)S(1)} %get-tuple-element.44), channel_id=1, source_target_pairs={{0,4},{4,0},{8,12},{12,8},{16,20},{20,16},{24,28},{28,24},{1,5},{5... | collective-permute-start | bytes 884744 | tf_op jit(solution)/shard_map/ppermute | solution.py:755
  35.7 7.8 %copy-start.7 = (bf16[32,2048]{1,0:T(8,128)(2,1)S(1)}, bf16[32,2048]{1,0:T(8,128)(2,1)}, u32[]{:S(2)}) copy-start(bf16[32,2048]{1,0:T(8,128)(2,1)} %refs_3_.1) | copy-start | bytes 393220
  35.7 7.8 %copy-start.10 = (f32[512]{0:T(512)S(1)}, f32[512]{0:T(512)}, u32[]{:S(2)}) copy-start(f32[512]{0:T(512)} %param.20) | copy-start | bytes 6148
  36.5 1.4 %collective-permute-start.13 = (bf16[32,2048]{1,0:T(8,128)(2,1)S(1)}, bf16[32,2048]{1,0:T(8,128)(2,1)S(1)}, u32[]{:S(2)}, u32[]{:S(2)}) collective-permute-start(bf16[32,2048]{1,0:T(8,128)(2,1)S(1)} %get-tuple-element.40), channel_id=1, source_target_pairs={{0,1},{1,0},{2,3},{3,2},{4,5},{5,4},{6,7},{7,6},{8,9},{9,8},{10,11... | collective-permute-start | bytes 393224 | tf_op jit(solution)/shard_map/ppermute | solution.py:752
  37.9 5.6 %collective-permute-start.14 = (bf16[32,2048]{1,0:T(8,128)(2,1)S(1)}, bf16[32,2048]{1,0:T(8,128)(2,1)S(1)}, u32[]{:S(2)}, u32[]{:S(2)}) collective-permute-start(bf16[32,2048]{1,0:T(8,128)(2,1)S(1)} %get-tuple-element.42), channel_id=1, source_target_pairs={{0,2},{1,3},{2,0},{3,1},{4,6},{5,7},{6,4},{7,5},{8,10},{9,11},{10,... | collective-permute-start | bytes 393224 | tf_op jit(solution)/shard_map/ppermute | solution.py:752
  (6 other events, 18.0 us)

commit v4 on v3

--- a/solution.py
+++ b/solution.py
@@ -557,7 +557,9 @@
     out[own : own + 16, :] = flat.astype(BF16)
 
 
-def attend_planes(turns, row, limits, key_cache, value_cache, swapped, queries, outs, scores):
+def twin_attend_far(turns, limits, key_cache, value_cache, swapped, *refs):
+    count = len(turns)
+    queries, outs, scores = refs[:count], refs[count : 2 * count], refs[2 * count]
     block, width = key_cache.shape[1:]
     heads = width // HEAD_DIM
     own = queries[0].shape[0]
@@ -565,7 +567,7 @@
     factor = 1.0 / math.sqrt(HEAD_DIM)
     place = iota((1, block), 1)
     both = jnp.concatenate([me * block + place, (me ^ 1) * block + place], axis=1)
-    visible = [both < limits[row + at : row + at + 1, :] for at in range(len(turns))]
+    visible = [both < limits[at + 1 : at + 2, :] for at in range(count)]
     for at, turn in enumerate(turns):
         for h in range(heads):
             lanes = slice(h * HEAD_DIM, (h + 1) * HEAD_DIM)
@@ -586,21 +588,9 @@
         write_stats(stats, outs[at])
 
 
-def twin_attend_far(turns, limits, key_cache, value_cache, swapped, *refs):
-    count = len(turns)
-    queries, outs, scores = refs[:count], refs[count : 2 * count], refs[2 * count]
-    attend_planes(turns, 1, limits, key_cache, value_cache, swapped, queries, outs, scores)
-
-
-def twin_attend_near(
-    turns, row, limits, key_cache, value_cache, swapped, own_tree, mine, other, *refs
-):
-    count = row - 1 + len(turns)
-    queries, outs = refs[:count], refs[count : count + len(turns)]
-    crossing, local, copied, scores, own_scores = refs[count + len(turns) :]
-    attend_planes(
-        turns, row, limits, key_cache, value_cache, swapped, queries[row - 1 :], outs, scores
-    )
+def twin_attend_near(limits, key_cache, value_cache, own_tree, mine, other, *refs):
+    queries, (crossing, local, copied, own_scores) = refs[:-4], refs[-4:]
+    count = len(queries)
     block, width = key_cache.shape[1:]
     heads = width // HEAD_DIM
     own = other.shape[0]
@@ -766,7 +756,7 @@
         ]
         return jnp.stack([jnp.stack(part) for part in parts])
 
-    swapped, swapped_near = beside(picked(far[:2])), beside(picked(far[2:]))
+    swapped = beside(picked(far))
     query_raw, key_raw, squares = call(
         twin_project_qk,
         (shaped((own, width), F32), shaped((own, width), F32), shaped((8, 2 * LANES), F32)),
@@ -808,24 +798,21 @@
 
     rows = own + 16
     partials = call(
-        functools.partial(twin_attend_far, far[:2]),
-        (shaped((rows, width), BF16),) * 2,
-        (limits, key_cache, value_cache, swapped, *from_far[:2]),
-        [pltpu.VMEM((2, heads, own, 2 * block), F32)],
-    )
-    near, crossing, local, copied = call(
-        functools.partial(twin_attend_near, far[2:], 3),
-        (shaped((rows, width), BF16),) * 3 + (shaped((2 * requests * own + own, width), BF16),),
-        (limits, key_cache, value_cache, swapped_near, own_tree, packed, other, *from_far),
-        [
-            pltpu.VMEM((1, heads, own, 2 * block), F32),
-            pltpu.VMEM((heads, 2 * own, block + LANES), F32),
-        ],
+        functools.partial(twin_attend_far, far),
+        (shaped((rows, width), BF16),) * len(far),
+        (limits, key_cache, value_cache, swapped, *from_far),
+        [pltpu.VMEM((len(far), heads, own, 2 * block), F32)],
+    )
+    crossing, local, copied = call(
+        twin_attend_near,
+        (shaped((rows, width), BF16),) * 2 + (shaped((2 * requests * own + own, width), BF16),),
+        (limits, key_cache, value_cache, own_tree, packed, other, *from_far),
+        [pltpu.VMEM((heads, 2 * own, block + LANES), F32)],
         ties=partials[:1],
     )
-    partials = [over_planes(part, turn) for part, turn in zip((*partials, near), far)]
+    partials = [over_planes(part, turn) for part, turn in zip(partials, far)]
     partials += [beside(crossing)]
-    partials = [partials[0], partials[1], partials[2], partials[3], local]
+    partials = [partials[0], partials[1], partials[3], partials[2], local]
     copied = beside(copied)
 
     total, rounded = call(

time: 44.4 us -> 43.1 us (0.971)
  local copies, waits for them, and re-layouts: 2.53 us -> 1.51 us
    ppermute x5 -> x4, waiting for transfers between devices: 3.93 us -> 0.34 us  [beside(): return lax.ppermute(x, 'seq', [(i, i ^ 1) for i in range(seq)])]
    ppermute x6, waiting for transfers between devices: 6.94 us -> 9.32 us  [over_planes(): lax.ppermute(x, 'seq', [(i, (i // 2 ^ turn) * 2 + i % 2) for i in range(s...]
    unnamed x28 -> x26, local copies, waits for them, and re-layouts: 1.11 us -> 0.08 us
    ppermute x5, waiting for transfers between devices: 3.9 us -> 4.83 us  [over_tp(): return lax.ppermute(x, 'tp', [(i, i ^ k) for i in range(tp)])]
    ppermute x5, starting transfers between devices: 2.96 us -> 3.55 us  [over_tp(): return lax.ppermute(x, 'tp', [(i, i ^ k) for i in range(tp)])]
    ppermute x5 -> x4, starting transfers between devices: 6.44 us -> 5.96 us  [beside(): return lax.ppermute(x, 'seq', [(i, i ^ 1) for i in range(seq)])]
  transfers between devices with their start and end apart: 16 -> 15, of which waited for: 8 -> 8; matrix products, arithmetic and copies ran while one was open for 0% -> 0% of each run, Pallas kernels for 15% -> 15%
where the time goes in v4:
time: 43.1 us; the launch traced here: 42.9 us
  starting transfers between devices  18.6 us (43%)
  waiting for transfers between devices  14.5 us (34%)
  Pallas kernels  7.18 us (17%)
  local copies, waits for them, and re-layouts  1.51 us (4%)
  between operations  0.9 us (2%)
    ppermute x6, waiting for transfers between devices, over_planes(): lax.ppermute(x, 'seq', [(i, (i // 2 ^ turn) * 2 + i % 2) for i in range(s...  9.32 us
    ppermute x6, starting transfers between devices, over_planes(): lax.ppermute(x, 'seq', [(i, (i // 2 ^ turn) * 2 + i % 2) for i in range(s...  9.14 us
    pallas_call x10, Pallas kernels, call(): pl.pallas_call(run, out_shape=outs, in_specs=([VMEM] * count if specs is...  7.18 us
    ppermute x4, starting transfers between devices, beside(): return lax.ppermute(x, 'seq', [(i, i ^ 1) for i in range(seq)])  5.96 us
    ppermute x5, waiting for transfers between devices, over_tp(): return lax.ppermute(x, 'tp', [(i, i ^ k) for i in range(tp)])  4.83 us
    ppermute x5, starting transfers between devices, over_tp(): return lax.ppermute(x, 'tp', [(i, i ^ k) for i in range(tp)])  3.55 us
    dynamic_slice x1, local copies, waits for them, and re-layouts, picked(): lax.dynamic_index_in_dim(x, me ^ turn, 0, False)  1.43 us
  transfers between devices with their start and end apart: 15, of which 8 were waited for; matrix products, arithmetic and copies ran while one was open for 0% of the time, Pallas kernels for 15%

profile of v4, /device:TPU:0, one launch (start us, length us, event | category | flops | bytes accessed | tf_op | source)
XLA Modules:
  0.0 42.9 jit_solution(1146788808128131113)
XLA Ops:
  0.7 1.4 %constant_dynamic-slice_fusion.4 = (bf16[1,128,512]{2,1,0:T(8,128)(2,1)S(1)}, bf16[1,128,512]{2,1,0:T(8,128)(2,1)S(1)}, bf16[1,128,512]{2,1,0:T(8,128)(2,1)S(1)}...) fusion(bf16[4,128,512]{2,1,0:T(8,128)(2,1)} %refs_2_.9, ...), kind=kLoop, calls=%fused_computation.9 | loop fusion | bytes 1572876 | tf_op jit(solution)/shard_map/jit(dynamic_index_in_dim)/dynamic_slice | solution.py:754
  2.3 3.0 %collective-permute-start = (bf16[3,2,128,512]{3,2,1,0:T(8,128)(2,1)S(1)}, bf16[3,2,128,512]{3,2,1,0:T(8,128)(2,1)S(1)}, u32[]{:S(2)}, u32[]{:S(2)}) collective-permute-start(bf16[3,2,128,512]{3,2,1,0:T(8,128)(2,1)S(1)} %pad_maximum_fusion), channel_id=1, source_target_pairs={{0,4},{4,0},{8,12},{12,8},{16,20},{20,16},{24,28},{28,24},{1,5},{5... | collective-permute-start | bytes 2359304 | tf_op jit(solution)/shard_map/ppermute | solution.py:745
  5.4 0.9 %twin_project_qk.1 = (f32[32,512]{1,0:T(8,128)S(1)}, f32[32,512]{1,0:T(8,128)S(1)}, f32[8,256]{1,0:T(8,128)S(1)}) custom-call(bf16[32,2048]{1,0:T(8,128)(2,1)S(1)} %copy-done.6, bf16[2048,512]{1,0:T(8,128)(2,1)S(1)} %copy-done.3, bf16[2048,512]{1,0:T(8,128)(2,1)S(1)} %copy-done.4), custom_call_target="tpu_custom_call" | custom-call | tf_op jit(solution)/shard_map/twin_project_qk/pallas_call | solution.py:731
  6.4 0.7 %collective-permute-start.1 = (f32[8,256]{1,0:T(8,128)S(1)}, f32[8,256]{1,0:T(8,128)S(1)}, u32[]{:S(2)}, u32[]{:S(2)}) collective-permute-start(f32[8,256]{1,0:T(8,128)S(1)} %get-tuple-element.30.refs_7_), channel_id=1, source_target_pairs={{0,3},{1,2},{2,1},{3,0},{4,7},{5,6},{6,5},{7,4},{8,11},{9,10},{10,... | collective-permute-start | bytes 24584 | tf_op jit(solution)/shard_map/ppermute | solution.py:742
  7.1 0.9 %collective-permute-start.2 = (f32[8,256]{1,0:T(8,128)S(1)}, f32[8,256]{1,0:T(8,128)S(1)}, u32[]{:S(2)}, u32[]{:S(2)}) collective-permute-start(f32[8,256]{1,0:T(8,128)S(1)} %get-tuple-element.30.refs_7_), channel_id=1, source_target_pairs={{0,2},{1,3},{2,0},{3,1},{4,6},{5,7},{6,4},{7,5},{8,10},{9,11},{10,... | collective-permute-start | bytes 24584 | tf_op jit(solution)/shard_map/ppermute | solution.py:742
  8.8 1.2 %twin_tree.1 = (f32[64,32]{1,0:T(8,128)S(1)}, s32[4,1,64]{2,1,0:T(1,128)S(1)}, f32[32,128]{1,0:T(8,128)S(1)}, f32[32,128]{1,0:T(8,128)S(1)}, s32[4,256]{1,0:T(4,128)S(1)}) custom-call(s32[1,4]{1,0:T(1,128)S(1)} %bitcast.14, s32[1,4]{1,0:T(1,128)S(1)} %bitcast.15, s32[4,64]{1,0:T(4,128)S(1)} %copy-done.10, f32[1,128]{1,0:T(1,128)S(1)} %fusion.2.refs_3_), custom_call_target="tpu_custom_call" | custom-call | tf_op jit(solution)/shard_map/twin_tree/pallas_call | solution.py:731
  10.0 0.8 %collective-permute-done.2.refs_9_ = f32[8,256]{1,0:T(8,128)S(1)} collective-permute-done((f32[8,256]{1,0:T(8,128)S(1)}, f32[8,256]{1,0:T(8,128)S(1)}, u32[]{:S(2)}, u32[]{:S(2)}) %collective-permute-start.2) | collective-permute-done | bytes 8224 | tf_op jit(solution)/shard_map/ppermute | solution.py:742
  11.0 3.7 %collective-permute-start.4 = (bf16[32,1536]{1,0:T(8,128)(2,1)S(1)}, bf16[32,1536]{1,0:T(8,128)(2,1)S(1)}, u32[]{:S(2)}, u32[]{:S(2)}) collective-permute-start(bf16[32,1536]{1,0:T(8,128)(2,1)S(1)} %get-tuple-element.31.refs_4_.refs_3_), channel_id=1, source_target_pairs={{0,24},{4,28},{8,16},{12,20},{16,8},{20,12},{24,0},{28,4},{1,25},{... | collective-permute-start | bytes 294920 | tf_op jit(solution)/shard_map/ppermute | solution.py:748
  14.7 0.8 %collective-permute-start.6 = (bf16[32,1536]{1,0:T(8,128)(2,1)S(1)}, bf16[32,1536]{1,0:T(8,128)(2,1)S(1)}, u32[]{:S(2)}, u32[]{:S(2)}) collective-permute-start(bf16[32,1536]{1,0:T(8,128)(2,1)S(1)} %get-tuple-element.31.refs_4_.refs_3_), channel_id=1, source_target_pairs={{0,8},{4,12},{8,0},{12,4},{16,24},{20,28},{24,16},{28,20},{1,9},{5... | collective-permute-start | bytes 294920 | tf_op jit(solution)/shard_map/ppermute | solution.py:748
  15.5 1.0 %collective-permute-start.9 = (bf16[32,512]{1,0:T(8,128)(2,1)S(1)}, bf16[32,512]{1,0:T(8,128)(2,1)S(1)}, u32[]{:S(2)}, u32[]{:S(2)}) collective-permute-start(bf16[32,512]{1,0:T(8,128)(2,1)S(1)} %get-tuple-element.35), channel_id=1, source_target_pairs={{0,4},{4,0},{8,12},{12,8},{16,20},{20,16},{24,28},{28,24},{1,5},{5... | collective-permute-start | bytes 98312 | tf_op jit(solution)/shard_map/ppermute | solution.py:745
  16.5 2.1 %collective-permute-done.4.refs_4_.refs_6_ = bf16[32,1536]{1,0:T(8,128)(2,1)S(1)} collective-permute-done((bf16[32,1536]{1,0:T(8,128)(2,1)S(1)}, bf16[32,1536]{1,0:T(8,128)(2,1)S(1)}, u32[]{:S(2)}, u32[]{:S(2)}) %collective-permute-start.4) | collective-permute-done | bytes 98336 | tf_op jit(solution)/shard_map/ppermute | solution.py:748
  18.6 4.6 %collective-permute-done.5.refs_5_.refs_7_ = bf16[32,1536]{1,0:T(8,128)(2,1)S(1)} collective-permute-done((bf16[32,1536]{1,0:T(8,128)(2,1)S(1)}, bf16[32,1536]{1,0:T(8,128)(2,1)S(1)}, u32[]{:S(2)}, u32[]{:S(2)}) %collective-permute-start.5) | collective-permute-done | bytes 98336 | tf_op jit(solution)/shard_map/ppermute | solution.py:748
  23.3 0.9 %twin_attend_far.1 = (bf16[48,512]{1,0:T(8,128)(2,1)S(1)}, bf16[48,512]{1,0:T(8,128)(2,1)S(1)}, bf16[48,512]{1,0:T(8,128)(2,1)S(1)}) custom-call(s32[4,256]{1,0:T(4,128)S(1)} %get-tuple-element.25.refs_0_, bf16[4,128,512]{2,1,0:T(8,128)(2,1)S(1)} %copy-done, bf16[4,128,512]{2,1,0:T(8,128)(2,1)S(1)} %copy-done.1, ...), custom_call_target="tpu_custom_call" | custom-call | tf_op jit(solution)/shard_map/twin_attend_far/pallas_call | solution.py:731
  24.2 3.9 %collective-permute-start.7 = (bf16[48,512]{1,0:T(8,128)(2,1)S(1)}, bf16[48,512]{1,0:T(8,128)(2,1)S(1)}, u32[]{:S(2)}, u32[]{:S(2)}) collective-permute-start(bf16[48,512]{1,0:T(8,128)(2,1)S(1)} %get-tuple-element.32.refs_9_), channel_id=1, source_target_pairs={{0,24},{4,28},{8,16},{12,20},{16,8},{20,12},{24,0},{28,4},{1,25},{... | collective-permute-start | bytes 147464 | tf_op jit(solution)/shard_map/ppermute | solution.py:748
  28.7 1.6 %collective-permute-start.10 = (bf16[48,512]{1,0:T(8,128)(2,1)S(1)}, bf16[48,512]{1,0:T(8,128)(2,1)S(1)}, u32[]{:S(2)}, u32[]{:S(2)}) collective-permute-start(bf16[48,512]{1,0:T(8,128)(2,1)S(1)} %get-tuple-element.36), channel_id=1, source_target_pairs={{0,4},{4,0},{8,12},{12,8},{16,20},{20,16},{24,28},{28,24},{1,5},{5... | collective-permute-start | bytes 147464 | tf_op jit(solution)/shard_map/ppermute | solution.py:745
  30.3 0.8 %collective-permute-start.11 = (bf16[48,512]{1,0:T(8,128)(2,1)S(1)}, bf16[48,512]{1,0:T(8,128)(2,1)S(1)}, u32[]{:S(2)}, u32[]{:S(2)}) collective-permute-start(bf16[48,512]{1,0:T(8,128)(2,1)S(1)} %get-tuple-element.37), channel_id=1, source_target_pairs={{0,8},{4,12},{8,0},{12,4},{16,24},{20,28},{24,16},{28,20},{1,9},{5... | collective-permute-start | bytes 147464 | tf_op jit(solution)/shard_map/ppermute | solution.py:748
  31.4 1.6 %collective-permute-done.8.refs_1_ = bf16[48,512]{1,0:T(8,128)(2,1)S(1)} collective-permute-done((bf16[48,512]{1,0:T(8,128)(2,1)S(1)}, bf16[48,512]{1,0:T(8,128)(2,1)S(1)}, u32[]{:S(2)}, u32[]{:S(2)}) %collective-permute-start.8) | collective-permute-done | bytes 49184 | tf_op jit(solution)/shard_map/ppermute | solution.py:748
  33.4 1.0 %collective-permute-done.11.refs_3_ = bf16[48,512]{1,0:T(8,128)(2,1)S(1)} collective-permute-done((bf16[48,512]{1,0:T(8,128)(2,1)S(1)}, bf16[48,512]{1,0:T(8,128)(2,1)S(1)}, u32[]{:S(2)}, u32[]{:S(2)}) %collective-permute-start.11) | collective-permute-done | bytes 49184 | tf_op jit(solution)/shard_map/ppermute | solution.py:748
  34.4 0.8 %twin_merge_and_project.1 = (f32[32,2048]{1,0:T(8,128)S(1)}, bf16[32,2048]{1,0:T(8,128)(2,1)S(1)}) custom-call(bf16[48,512]{1,0:T(8,128)(2,1)S(1)} %collective-permute-done.7.refs_0_, bf16[48,512]{1,0:T(8,128)(2,1)S(1)} %collective-permute-done.8.refs_1_, bf16[48,512]{1,0:T(8,128)(2,1)S(1)} %collective-permute-done.10.refs_2_, ...), custom_call_target="tpu_custom_call" | custom-call | tf_op jit(solution)/shard_map/twin_merge_and_project/pallas_call | solution.py:731
  35.2 1.3 %collective-permute-done.12.refs_1_ = bf16[32,2048]{1,0:T(8,128)(2,1)S(1)} collective-permute-done((bf16[32,2048]{1,0:T(8,128)(2,1)S(1)}, bf16[32,2048]{1,0:T(8,128)(2,1)S(1)}, u32[]{:S(2)}, u32[]{:S(2)}) %collective-permute-start.12) | collective-permute-done | bytes 131104 | tf_op jit(solution)/shard_map/ppermute | solution.py:742
  36.5 1.6 %collective-permute-start.13 = (bf16[32,2048]{1,0:T(8,128)(2,1)S(1)}, bf16[32,2048]{1,0:T(8,128)(2,1)S(1)}, u32[]{:S(2)}, u32[]{:S(2)}) collective-permute-start(bf16[32,2048]{1,0:T(8,128)(2,1)S(1)} %get-tuple-element.42), channel_id=1, source_target_pairs={{0,2},{1,3},{2,0},{3,1},{4,6},{5,7},{6,4},{7,5},{8,10},{9,11},{10,... | collective-permute-start | bytes 393224 | tf_op jit(solution)/shard_map/ppermute | solution.py:742
  38.1 1.4 %twin_compact.1 = (bf16[4,128,512]{2,1,0:T(8,128)(2,1)}, bf16[4,128,512]{2,1,0:T(8,128)(2,1)}) custom-call(s32[4,1,64]{2,1,0:T(1,128)S(1)} %get-tuple-element.43.refs_0_, bf16[4,128,512]{2,1,0:T(8,128)(2,1)S(1)} %copy-done, bf16[4,128,512]{2,1,0:T(8,128)(2,1)S(1)} %copy-done.1, bf16[32,1536]{1,0:T(8,128)(2,1)S(1)} %get-tuple-element.31.refs_4_.refs_3_, ...), custom_call_target="tpu_custom_call" | custom-call | tf_op jit(solution)/shard_map/twin_compact/pallas_call | solution.py:731
  39.5 2.7 %collective-permute-done.13.refs_1_ = bf16[32,2048]{1,0:T(8,128)(2,1)S(1)} collective-permute-done((bf16[32,2048]{1,0:T(8,128)(2,1)S(1)}, bf16[32,2048]{1,0:T(8,128)(2,1)S(1)}, u32[]{:S(2)}, u32[]{:S(2)}) %collective-permute-start.13) | collective-permute-done | bytes 131104 | tf_op jit(solution)/shard_map/ppermute | solution.py:742
  42.2 0.7 %twin_finish.1 = bf16[32,512]{1,0:T(8,128)(2,1)} custom-call(f32[32,2048]{1,0:T(8,128)S(1)} %get-tuple-element.41.refs_0_, bf16[32,2048]{1,0:T(8,128)(2,1)S(1)} %collective-permute-done.13.refs_1_, f32[1,512]{1,0:T(1,128)S(1)} %bitcast.13, bf16[32,2048]{1,0:T(8,128)(2,1)S(1)} %copy-done.6), custom_call_target="tpu_custom_call" | custom-call | tf_op jit(solution)/shard_map/twin_finish/pallas_call | solution.py:731
  (48 shorter events, 2.6 us)
Async XLA Ops:
  0.7 4.7 %copy-start.3 = (bf16[2048,512]{1,0:T(8,128)(2,1)S(1)}, bf16[2048,512]{1,0:T(8,128)(2,1)}, u32[]{:S(2)}) copy-start(bf16[2048,512]{1,0:T(8,128)(2,1)} %refs_1_.5) | copy-start | bytes 6291460
  0.7 4.7 %copy-start.4 = (bf16[2048,512]{1,0:T(8,128)(2,1)S(1)}, bf16[2048,512]{1,0:T(8,128)(2,1)}, u32[]{:S(2)}) copy-start(bf16[2048,512]{1,0:T(8,128)(2,1)} %refs_2_.6) | copy-start | bytes 6291460
  0.7 4.7 %copy-start.6 = (bf16[32,2048]{1,0:T(8,128)(2,1)S(1)}, bf16[32,2048]{1,0:T(8,128)(2,1)}, u32[]{:S(2)}) copy-start(bf16[32,2048]{1,0:T(8,128)(2,1)} %refs_3_.1) | copy-start | bytes 393220
  2.3 6.0 %copy-start.5 = (bf16[2048,512]{1,0:T(8,128)(2,1)S(1)}, bf16[2048,512]{1,0:T(8,128)(2,1)}, u32[]{:S(2)}) copy-start(bf16[2048,512]{1,0:T(8,128)(2,1)} %refs_1_.6) | copy-start | bytes 6291460
  2.3 20.9 %collective-permute-start = (bf16[3,2,128,512]{3,2,1,0:T(8,128)(2,1)S(1)}, bf16[3,2,128,512]{3,2,1,0:T(8,128)(2,1)S(1)}, u32[]{:S(2)}, u32[]{:S(2)}) collective-permute-start(bf16[3,2,128,512]{3,2,1,0:T(8,128)(2,1)S(1)} %pad_maximum_fusion), channel_id=1, source_target_pairs={{0,4},{4,0},{8,12},{12,8},{16,20},{20,16},{24,28},{28,24},{1,5},{5... | collective-permute-start | bytes 2359304 | tf_op jit(solution)/shard_map/ppermute | solution.py:745
  6.3 4.5 %copy-start.7 = (f32[512]{0:T(512)S(1)}, f32[512]{0:T(512)}, u32[]{:S(2)}) copy-start(f32[512]{0:T(512)} %param.18) | copy-start | bytes 6148
  6.3 16.9 %copy-start = (bf16[4,128,512]{2,1,0:T(8,128)(2,1)S(1)}, bf16[4,128,512]{2,1,0:T(8,128)(2,1)}, u32[]{:S(2)}) copy-start(bf16[4,128,512]{2,1,0:T(8,128)(2,1)} %refs_1_.9) | copy-start | bytes 1572868
  6.3 16.9 %copy-start.1 = (bf16[4,128,512]{2,1,0:T(8,128)(2,1)S(1)}, bf16[4,128,512]{2,1,0:T(8,128)(2,1)}, u32[]{:S(2)}) copy-start(bf16[4,128,512]{2,1,0:T(8,128)(2,1)} %refs_2_.9) | copy-start | bytes 1572868
  6.4 3.6 %collective-permute-start.1 = (f32[8,256]{1,0:T(8,128)S(1)}, f32[8,256]{1,0:T(8,128)S(1)}, u32[]{:S(2)}, u32[]{:S(2)}) collective-permute-start(f32[8,256]{1,0:T(8,128)S(1)} %get-tuple-element.30.refs_7_), channel_id=1, source_target_pairs={{0,3},{1,2},{2,1},{3,0},{4,7},{5,6},{6,5},{7,4},{8,11},{9,10},{10,... | collective-permute-start | bytes 24584 | tf_op jit(solution)/shard_map/ppermute | solution.py:742
  7.1 3.7 %collective-permute-start.2 = (f32[8,256]{1,0:T(8,128)S(1)}, f32[8,256]{1,0:T(8,128)S(1)}, u32[]{:S(2)}, u32[]{:S(2)}) collective-permute-start(f32[8,256]{1,0:T(8,128)S(1)} %get-tuple-element.30.refs_7_), channel_id=1, source_target_pairs={{0,2},{1,3},{2,0},{3,1},{4,6},{5,7},{6,4},{7,5},{8,10},{9,11},{10,... | collective-permute-start | bytes 24584 | tf_op jit(solution)/shard_map/ppermute | solution.py:742
  8.0 2.8 %collective-permute-start.3 = (f32[8,256]{1,0:T(8,128)S(1)}, f32[8,256]{1,0:T(8,128)S(1)}, u32[]{:S(2)}, u32[]{:S(2)}) collective-permute-start(f32[8,256]{1,0:T(8,128)S(1)} %get-tuple-element.30.refs_7_), channel_id=1, source_target_pairs={{0,1},{1,0},{2,3},{3,2},{4,5},{5,4},{6,7},{7,6},{8,9},{9,8},{10,11... | collective-permute-start | bytes 24584 | tf_op jit(solution)/shard_map/ppermute | solution.py:742
  8.7 25.6 %copy-start.2 = (bf16[512,2048]{1,0:T(8,128)(2,1)S(1)}, bf16[512,2048]{1,0:T(8,128)(2,1)}, u32[]{:S(2)}) copy-start(bf16[512,2048]{1,0:T(8,128)(2,1)} %refs_5_.1) | copy-start | bytes 6291460
  11.0 7.6 %collective-permute-start.4 = (bf16[32,1536]{1,0:T(8,128)(2,1)S(1)}, bf16[32,1536]{1,0:T(8,128)(2,1)S(1)}, u32[]{:S(2)}, u32[]{:S(2)}) collective-permute-start(bf16[32,1536]{1,0:T(8,128)(2,1)S(1)} %get-tuple-element.31.refs_4_.refs_3_), channel_id=1, source_target_pairs={{0,24},{4,28},{8,16},{12,20},{16,8},{20,12},{24,0},{28,4},{1,25},{... | collective-permute-start | bytes 294920 | tf_op jit(solution)/shard_map/ppermute | solution.py:748
  14.7 8.5 %collective-permute-start.5 = (bf16[32,1536]{1,0:T(8,128)(2,1)S(1)}, bf16[32,1536]{1,0:T(8,128)(2,1)S(1)}, u32[]{:S(2)}, u32[]{:S(2)}) collective-permute-start(bf16[32,1536]{1,0:T(8,128)(2,1)S(1)} %get-tuple-element.31.refs_4_.refs_3_), channel_id=1, source_target_pairs={{0,16},{4,20},{8,24},{12,28},{16,0},{20,4},{24,8},{28,12},{1,17},{... | collective-permute-start | bytes 294920 | tf_op jit(solution)/shard_map/ppermute | solution.py:748
  14.7 8.5 %collective-permute-start.6 = (bf16[32,1536]{1,0:T(8,128)(2,1)S(1)}, bf16[32,1536]{1,0:T(8,128)(2,1)S(1)}, u32[]{:S(2)}, u32[]{:S(2)}) collective-permute-start(bf16[32,1536]{1,0:T(8,128)(2,1)S(1)} %get-tuple-element.31.refs_4_.refs_3_), channel_id=1, source_target_pairs={{0,8},{4,12},{8,0},{12,4},{16,24},{20,28},{24,16},{28,20},{1,9},{5... | collective-permute-start | bytes 294920 | tf_op jit(solution)/shard_map/ppermute | solution.py:748
  15.5 12.6 %collective-permute-start.9 = (bf16[32,512]{1,0:T(8,128)(2,1)S(1)}, bf16[32,512]{1,0:T(8,128)(2,1)S(1)}, u32[]{:S(2)}, u32[]{:S(2)}) collective-permute-start(bf16[32,512]{1,0:T(8,128)(2,1)S(1)} %get-tuple-element.35), channel_id=1, source_target_pairs={{0,4},{4,0},{8,12},{12,8},{16,20},{20,16},{24,28},{28,24},{1,5},{5... | collective-permute-start | bytes 98312 | tf_op jit(solution)/shard_map/ppermute | solution.py:745
  24.2 7.3 %collective-permute-start.7 = (bf16[48,512]{1,0:T(8,128)(2,1)S(1)}, bf16[48,512]{1,0:T(8,128)(2,1)S(1)}, u32[]{:S(2)}, u32[]{:S(2)}) collective-permute-start(bf16[48,512]{1,0:T(8,128)(2,1)S(1)} %get-tuple-element.32.refs_9_), channel_id=1, source_target_pairs={{0,24},{4,28},{8,16},{12,20},{16,8},{20,12},{24,0},{28,4},{1,25},{... | collective-permute-start | bytes 147464 | tf_op jit(solution)/shard_map/ppermute | solution.py:748
  28.1 5.0 %collective-permute-start.8 = (bf16[48,512]{1,0:T(8,128)(2,1)S(1)}, bf16[48,512]{1,0:T(8,128)(2,1)S(1)}, u32[]{:S(2)}, u32[]{:S(2)}) collective-permute-start(bf16[48,512]{1,0:T(8,128)(2,1)S(1)} %get-tuple-element.33), channel_id=1, source_target_pairs={{0,16},{4,20},{8,24},{12,28},{16,0},{20,4},{24,8},{28,12},{1,17},{... | collective-permute-start | bytes 147464 | tf_op jit(solution)/shard_map/ppermute | solution.py:748
  28.7 4.7 %collective-permute-start.10 = (bf16[48,512]{1,0:T(8,128)(2,1)S(1)}, bf16[48,512]{1,0:T(8,128)(2,1)S(1)}, u32[]{:S(2)}, u32[]{:S(2)}) collective-permute-start(bf16[48,512]{1,0:T(8,128)(2,1)S(1)} %get-tuple-element.36), channel_id=1, source_target_pairs={{0,4},{4,0},{8,12},{12,8},{16,20},{20,16},{24,28},{28,24},{1,5},{5... | collective-permute-start | bytes 147464 | tf_op jit(solution)/shard_map/ppermute | solution.py:745
  30.3 4.1 %collective-permute-start.11 = (bf16[48,512]{1,0:T(8,128)(2,1)S(1)}, bf16[48,512]{1,0:T(8,128)(2,1)S(1)}, u32[]{:S(2)}, u32[]{:S(2)}) collective-permute-start(bf16[48,512]{1,0:T(8,128)(2,1)S(1)} %get-tuple-element.37), channel_id=1, source_target_pairs={{0,8},{4,12},{8,0},{12,4},{16,24},{20,28},{24,16},{28,20},{1,9},{5... | collective-permute-start | bytes 147464 | tf_op jit(solution)/shard_map/ppermute | solution.py:748
  31.0 7.1 %collective-permute-start.14 = (bf16[288,512]{1,0:T(8,128)(2,1)S(1)}, bf16[288,512]{1,0:T(8,128)(2,1)S(1)}, u32[]{:S(2)}, u32[]{:S(2)}) collective-permute-start(bf16[288,512]{1,0:T(8,128)(2,1)S(1)} %get-tuple-element.44), channel_id=1, source_target_pairs={{0,4},{4,0},{8,12},{12,8},{16,20},{20,16},{24,28},{28,24},{1,5},{5... | collective-permute-start | bytes 884744 | tf_op jit(solution)/shard_map/ppermute | solution.py:745
  34.4 7.8 %copy-start.9 = (f32[512]{0:T(512)S(1)}, f32[512]{0:T(512)}, u32[]{:S(2)}) copy-start(f32[512]{0:T(512)} %param.20) | copy-start | bytes 6148
  35.1 1.4 %collective-permute-start.12 = (bf16[32,2048]{1,0:T(8,128)(2,1)S(1)}, bf16[32,2048]{1,0:T(8,128)(2,1)S(1)}, u32[]{:S(2)}, u32[]{:S(2)}) collective-permute-start(bf16[32,2048]{1,0:T(8,128)(2,1)S(1)} %get-tuple-element.40), channel_id=1, source_target_pairs={{0,1},{1,0},{2,3},{3,2},{4,5},{5,4},{6,7},{7,6},{8,9},{9,8},{10,11... | collective-permute-start | bytes 393224 | tf_op jit(solution)/shard_map/ppermute | solution.py:742
  36.5 5.6 %collective-permute-start.13 = (bf16[32,2048]{1,0:T(8,128)(2,1)S(1)}, bf16[32,2048]{1,0:T(8,128)(2,1)S(1)}, u32[]{:S(2)}, u32[]{:S(2)}) collective-permute-start(bf16[32,2048]{1,0:T(8,128)(2,1)S(1)} %get-tuple-element.42), channel_id=1, source_target_pairs={{0,2},{1,3},{2,0},{3,1},{4,6},{5,7},{6,4},{7,5},{8,10},{9,11},{10,... | collective-permute-start | bytes 393224 | tf_op jit(solution)/shard_map/ppermute | solution.py:742
  (4 other events, 12.0 us)

commit v5 on v4

--- a/solution.py
+++ b/solution.py
@@ -812,7 +812,7 @@
     )
     partials = [over_planes(part, turn) for part, turn in zip(partials, far)]
     partials += [beside(crossing)]
-    partials = [partials[0], partials[1], partials[3], partials[2], local]
+    partials = [partials[3], partials[2], partials[0], partials[1], local]
     copied = beside(copied)
 
     total, rounded = call(

time: 43.1 us -> 44 us (1.021)
  waiting for transfers between devices: 14.5 us -> 15.4 us
    ppermute x4, waiting for transfers between devices: 0.34 us -> 2.02 us  [beside(): return lax.ppermute(x, 'seq', [(i, i ^ 1) for i in range(seq)])]
    ppermute x6, waiting for transfers between devices: 9.32 us -> 8.59 us  [over_planes(): lax.ppermute(x, 'seq', [(i, (i // 2 ^ turn) * 2 + i % 2) for i in range(s...]
  transfers between devices with their start and end apart: 15 -> 15, of which waited for: 8 -> 7; matrix products, arithmetic and copies ran while one was open for 0% -> 0% of each run, Pallas kernels for 15% -> 15%
where the time goes in v5:
time: 44 us; the launch traced here: 43.8 us
  starting transfers between devices  18.6 us (42%)
  waiting for transfers between devices  15.4 us (35%)
  Pallas kernels  7.19 us (16%)
  local copies, waits for them, and re-layouts  1.51 us (3%)
  between operations  0.9 us (2%)
    ppermute x6, starting transfers between devices, over_planes(): lax.ppermute(x, 'seq', [(i, (i // 2 ^ turn) * 2 + i % 2) for i in range(s...  9.14 us
    ppermute x6, waiting for transfers between devices, over_planes(): lax.ppermute(x, 'seq', [(i, (i // 2 ^ turn) * 2 + i % 2) for i in range(s...  8.59 us
    pallas_call x10, Pallas kernels, call(): pl.pallas_call(run, out_shape=outs, in_specs=([VMEM] * count if specs is...  7.19 us
    ppermute x4, starting transfers between devices, beside(): return lax.ppermute(x, 'seq', [(i, i ^ 1) for i in range(seq)])  5.9 us
    ppermute x5, waiting for transfers between devices, over_tp(): return lax.ppermute(x, 'tp', [(i, i ^ k) for i in range(tp)])  4.83 us
    ppermute x5, starting transfers between devices, over_tp(): return lax.ppermute(x, 'tp', [(i, i ^ k) for i in range(tp)])  3.55 us
    ppermute x4, waiting for transfers between devices, beside(): return lax.ppermute(x, 'seq', [(i, i ^ 1) for i in range(seq)])  2.02 us
    dynamic_slice x1, local copies, waits for them, and re-layouts, picked(): lax.dynamic_index_in_dim(x, me ^ turn, 0, False)  1.43 us
  transfers between devices with their start and end apart: 15, of which 7 were waited for; matrix products, arithmetic and copies ran while one was open for 0% of the time, Pallas kernels for 15%

profile of v5, /device:TPU:0, one launch (start us, length us, event | category | flops | bytes accessed | tf_op | source)
XLA Modules:
  0.0 43.8 jit_solution(10222856936816266716)
XLA Ops:
  0.7 1.4 %constant_dynamic-slice_fusion.4 = (bf16[1,128,512]{2,1,0:T(8,128)(2,1)S(1)}, bf16[1,128,512]{2,1,0:T(8,128)(2,1)S(1)}, bf16[1,128,512]{2,1,0:T(8,128)(2,1)S(1)}...) fusion(bf16[4,128,512]{2,1,0:T(8,128)(2,1)} %refs_2_.9, ...), kind=kLoop, calls=%fused_computation.9 | loop fusion | bytes 1572876 | tf_op jit(solution)/shard_map/jit(dynamic_index_in_dim)/dynamic_slice | solution.py:754
  2.3 3.0 %collective-permute-start.7 = (bf16[3,2,128,512]{3,2,1,0:T(8,128)(2,1)S(1)}, bf16[3,2,128,512]{3,2,1,0:T(8,128)(2,1)S(1)}, u32[]{:S(2)}, u32[]{:S(2)}) collective-permute-start(bf16[3,2,128,512]{3,2,1,0:T(8,128)(2,1)S(1)} %pad_maximum_fusion), channel_id=1, source_target_pairs={{0,4},{4,0},{8,12},{12,8},{16,20},{20,16},{24,28},{28,24},{1,5},{5... | collective-permute-start | bytes 2359304 | tf_op jit(solution)/shard_map/ppermute | solution.py:745
  5.4 0.9 %twin_project_qk.1 = (f32[32,512]{1,0:T(8,128)S(1)}, f32[32,512]{1,0:T(8,128)S(1)}, f32[8,256]{1,0:T(8,128)S(1)}) custom-call(bf16[32,2048]{1,0:T(8,128)(2,1)S(1)} %copy-done.6, bf16[2048,512]{1,0:T(8,128)(2,1)S(1)} %copy-done.3, bf16[2048,512]{1,0:T(8,128)(2,1)S(1)} %copy-done.4), custom_call_target="tpu_custom_call" | custom-call | tf_op jit(solution)/shard_map/twin_project_qk/pallas_call | solution.py:731
  6.4 0.7 %collective-permute-start = (f32[8,256]{1,0:T(8,128)S(1)}, f32[8,256]{1,0:T(8,128)S(1)}, u32[]{:S(2)}, u32[]{:S(2)}) collective-permute-start(f32[8,256]{1,0:T(8,128)S(1)} %get-tuple-element.31.refs_7_), channel_id=1, source_target_pairs={{0,3},{1,2},{2,1},{3,0},{4,7},{5,6},{6,5},{7,4},{8,11},{9,10},{10,... | collective-permute-start | bytes 24584 | tf_op jit(solution)/shard_map/ppermute | solution.py:742
  7.1 0.9 %collective-permute-start.1 = (f32[8,256]{1,0:T(8,128)S(1)}, f32[8,256]{1,0:T(8,128)S(1)}, u32[]{:S(2)}, u32[]{:S(2)}) collective-permute-start(f32[8,256]{1,0:T(8,128)S(1)} %get-tuple-element.31.refs_7_), channel_id=1, source_target_pairs={{0,2},{1,3},{2,0},{3,1},{4,6},{5,7},{6,4},{7,5},{8,10},{9,11},{10,... | collective-permute-start | bytes 24584 | tf_op jit(solution)/shard_map/ppermute | solution.py:742
  8.8 1.2 %twin_tree.1 = (f32[64,32]{1,0:T(8,128)S(1)}, s32[4,1,64]{2,1,0:T(1,128)S(1)}, f32[32,128]{1,0:T(8,128)S(1)}, f32[32,128]{1,0:T(8,128)S(1)}, s32[4,256]{1,0:T(4,128)S(1)}) custom-call(s32[1,4]{1,0:T(1,128)S(1)} %bitcast.14, s32[1,4]{1,0:T(1,128)S(1)} %bitcast.15, s32[4,64]{1,0:T(4,128)S(1)} %copy-done.10, f32[1,128]{1,0:T(1,128)S(1)} %fusion.2.refs_3_), custom_call_target="tpu_custom_call" | custom-call | tf_op jit(solution)/shard_map/twin_tree/pallas_call | solution.py:731
  10.0 0.8 %collective-permute-done.1.refs_9_ = f32[8,256]{1,0:T(8,128)S(1)} collective-permute-done((f32[8,256]{1,0:T(8,128)S(1)}, f32[8,256]{1,0:T(8,128)S(1)}, u32[]{:S(2)}, u32[]{:S(2)}) %collective-permute-start.1) | collective-permute-done | bytes 8224 | tf_op jit(solution)/shard_map/ppermute | solution.py:742
  11.0 3.7 %collective-permute-start.4 = (bf16[32,1536]{1,0:T(8,128)(2,1)S(1)}, bf16[32,1536]{1,0:T(8,128)(2,1)S(1)}, u32[]{:S(2)}, u32[]{:S(2)}) collective-permute-start(bf16[32,1536]{1,0:T(8,128)(2,1)S(1)} %get-tuple-element.32.refs_4_.refs_3_), channel_id=1, source_target_pairs={{0,24},{4,28},{8,16},{12,20},{16,8},{20,12},{24,0},{28,4},{1,25},{... | collective-permute-start | bytes 294920 | tf_op jit(solution)/shard_map/ppermute | solution.py:748
  14.7 0.8 %collective-permute-start.6 = (bf16[32,1536]{1,0:T(8,128)(2,1)S(1)}, bf16[32,1536]{1,0:T(8,128)(2,1)S(1)}, u32[]{:S(2)}, u32[]{:S(2)}) collective-permute-start(bf16[32,1536]{1,0:T(8,128)(2,1)S(1)} %get-tuple-element.32.refs_4_.refs_3_), channel_id=1, source_target_pairs={{0,8},{4,12},{8,0},{12,4},{16,24},{20,28},{24,16},{28,20},{1,9},{5... | collective-permute-start | bytes 294920 | tf_op jit(solution)/shard_map/ppermute | solution.py:748
  15.5 1.0 %collective-permute-start.3 = (bf16[32,512]{1,0:T(8,128)(2,1)S(1)}, bf16[32,512]{1,0:T(8,128)(2,1)S(1)}, u32[]{:S(2)}, u32[]{:S(2)}) collective-permute-start(bf16[32,512]{1,0:T(8,128)(2,1)S(1)} %get-tuple-element.33), channel_id=1, source_target_pairs={{0,4},{4,0},{8,12},{12,8},{16,20},{20,16},{24,28},{28,24},{1,5},{5... | collective-permute-start | bytes 98312 | tf_op jit(solution)/shard_map/ppermute | solution.py:745
  16.5 2.1 %collective-permute-done.4.refs_4_.refs_6_ = bf16[32,1536]{1,0:T(8,128)(2,1)S(1)} collective-permute-done((bf16[32,1536]{1,0:T(8,128)(2,1)S(1)}, bf16[32,1536]{1,0:T(8,128)(2,1)S(1)}, u32[]{:S(2)}, u32[]{:S(2)}) %collective-permute-start.4) | collective-permute-done | bytes 98336 | tf_op jit(solution)/shard_map/ppermute | solution.py:748
  18.6 4.6 %collective-permute-done.5.refs_5_.refs_7_ = bf16[32,1536]{1,0:T(8,128)(2,1)S(1)} collective-permute-done((bf16[32,1536]{1,0:T(8,128)(2,1)S(1)}, bf16[32,1536]{1,0:T(8,128)(2,1)S(1)}, u32[]{:S(2)}, u32[]{:S(2)}) %collective-permute-start.5) | collective-permute-done | bytes 98336 | tf_op jit(solution)/shard_map/ppermute | solution.py:748
  23.3 0.9 %twin_attend_far.1 = (bf16[48,512]{1,0:T(8,128)(2,1)S(1)}, bf16[48,512]{1,0:T(8,128)(2,1)S(1)}, bf16[48,512]{1,0:T(8,128)(2,1)S(1)}) custom-call(s32[4,256]{1,0:T(4,128)S(1)} %get-tuple-element.25.refs_0_, bf16[4,128,512]{2,1,0:T(8,128)(2,1)S(1)} %copy-done, bf16[4,128,512]{2,1,0:T(8,128)(2,1)S(1)} %copy-done.1, ...), custom_call_target="tpu_custom_call" | custom-call | tf_op jit(solution)/shard_map/twin_attend_far/pallas_call | solution.py:731
  24.2 3.9 %collective-permute-start.10 = (bf16[48,512]{1,0:T(8,128)(2,1)S(1)}, bf16[48,512]{1,0:T(8,128)(2,1)S(1)}, u32[]{:S(2)}, u32[]{:S(2)}) collective-permute-start(bf16[48,512]{1,0:T(8,128)(2,1)S(1)} %get-tuple-element.34.refs_9_), channel_id=1, source_target_pairs={{0,24},{4,28},{8,16},{12,20},{16,8},{20,12},{24,0},{28,4},{1,25},{... | collective-permute-start | bytes 147464 | tf_op jit(solution)/shard_map/ppermute | solution.py:748
  28.7 1.6 %collective-permute-start.8 = (bf16[48,512]{1,0:T(8,128)(2,1)S(1)}, bf16[48,512]{1,0:T(8,128)(2,1)S(1)}, u32[]{:S(2)}, u32[]{:S(2)}) collective-permute-start(bf16[48,512]{1,0:T(8,128)(2,1)S(1)} %get-tuple-element.35), channel_id=1, source_target_pairs={{0,4},{4,0},{8,12},{12,8},{16,20},{20,16},{24,28},{28,24},{1,5},{5... | collective-permute-start | bytes 147464 | tf_op jit(solution)/shard_map/ppermute | solution.py:745
  30.3 0.8 %collective-permute-start.9 = (bf16[48,512]{1,0:T(8,128)(2,1)S(1)}, bf16[48,512]{1,0:T(8,128)(2,1)S(1)}, u32[]{:S(2)}, u32[]{:S(2)}) collective-permute-start(bf16[48,512]{1,0:T(8,128)(2,1)S(1)} %get-tuple-element.36), channel_id=1, source_target_pairs={{0,8},{4,12},{8,0},{12,4},{16,24},{20,28},{24,16},{28,20},{1,9},{5... | collective-permute-start | bytes 147464 | tf_op jit(solution)/shard_map/ppermute | solution.py:748
  31.4 2.0 %collective-permute-done.8.refs_0_ = bf16[48,512]{1,0:T(8,128)(2,1)S(1)} collective-permute-done((bf16[48,512]{1,0:T(8,128)(2,1)S(1)}, bf16[48,512]{1,0:T(8,128)(2,1)S(1)}, u32[]{:S(2)}, u32[]{:S(2)}) %collective-permute-start.8) | collective-permute-done | bytes 49184 | tf_op jit(solution)/shard_map/ppermute | solution.py:745
  33.4 1.8 %collective-permute-done.11.refs_3_ = bf16[48,512]{1,0:T(8,128)(2,1)S(1)} collective-permute-done((bf16[48,512]{1,0:T(8,128)(2,1)S(1)}, bf16[48,512]{1,0:T(8,128)(2,1)S(1)}, u32[]{:S(2)}, u32[]{:S(2)}) %collective-permute-start.11) | collective-permute-done | bytes 49184 | tf_op jit(solution)/shard_map/ppermute | solution.py:748
  35.3 0.8 %twin_merge_and_project.1 = (f32[32,2048]{1,0:T(8,128)S(1)}, bf16[32,2048]{1,0:T(8,128)(2,1)S(1)}) custom-call(bf16[48,512]{1,0:T(8,128)(2,1)S(1)} %collective-permute-done.8.refs_0_, bf16[48,512]{1,0:T(8,128)(2,1)S(1)} %collective-permute-done.9.refs_1_, bf16[48,512]{1,0:T(8,128)(2,1)S(1)} %collective-permute-done.10.refs_2_, ...), custom_call_target="tpu_custom_call" | custom-call | tf_op jit(solution)/shard_map/twin_merge_and_project/pallas_call | solution.py:731
  36.1 1.3 %collective-permute-done.12.refs_1_ = bf16[32,2048]{1,0:T(8,128)(2,1)S(1)} collective-permute-done((bf16[32,2048]{1,0:T(8,128)(2,1)S(1)}, bf16[32,2048]{1,0:T(8,128)(2,1)S(1)}, u32[]{:S(2)}, u32[]{:S(2)}) %collective-permute-start.12) | collective-permute-done | bytes 131104 | tf_op jit(solution)/shard_map/ppermute | solution.py:742
  37.4 1.6 %collective-permute-start.13 = (bf16[32,2048]{1,0:T(8,128)(2,1)S(1)}, bf16[32,2048]{1,0:T(8,128)(2,1)S(1)}, u32[]{:S(2)}, u32[]{:S(2)}) collective-permute-start(bf16[32,2048]{1,0:T(8,128)(2,1)S(1)} %get-tuple-element.42), channel_id=1, source_target_pairs={{0,2},{1,3},{2,0},{3,1},{4,6},{5,7},{6,4},{7,5},{8,10},{9,11},{10,... | collective-permute-start | bytes 393224 | tf_op jit(solution)/shard_map/ppermute | solution.py:742
  39.0 1.4 %twin_compact.1 = (bf16[4,128,512]{2,1,0:T(8,128)(2,1)}, bf16[4,128,512]{2,1,0:T(8,128)(2,1)}) custom-call(s32[4,1,64]{2,1,0:T(1,128)S(1)} %get-tuple-element.43.refs_0_, bf16[4,128,512]{2,1,0:T(8,128)(2,1)S(1)} %copy-done, bf16[4,128,512]{2,1,0:T(8,128)(2,1)S(1)} %copy-done.1, bf16[32,1536]{1,0:T(8,128)(2,1)S(1)} %get-tuple-element.32.refs_4_.refs_3_, ...), custom_call_target="tpu_custom_call" | custom-call | tf_op jit(solution)/shard_map/twin_compact/pallas_call | solution.py:731
  40.4 2.7 %collective-permute-done.13.refs_1_ = bf16[32,2048]{1,0:T(8,128)(2,1)S(1)} collective-permute-done((bf16[32,2048]{1,0:T(8,128)(2,1)S(1)}, bf16[32,2048]{1,0:T(8,128)(2,1)S(1)}, u32[]{:S(2)}, u32[]{:S(2)}) %collective-permute-start.13) | collective-permute-done | bytes 131104 | tf_op jit(solution)/shard_map/ppermute | solution.py:742
  43.1 0.7 %twin_finish.1 = bf16[32,512]{1,0:T(8,128)(2,1)} custom-call(f32[32,2048]{1,0:T(8,128)S(1)} %get-tuple-element.41.refs_0_, bf16[32,2048]{1,0:T(8,128)(2,1)S(1)} %collective-permute-done.13.refs_1_, f32[1,512]{1,0:T(1,128)S(1)} %bitcast.13, bf16[32,2048]{1,0:T(8,128)(2,1)S(1)} %copy-done.6), custom_call_target="tpu_custom_call" | custom-call | tf_op jit(solution)/shard_map/twin_finish/pallas_call | solution.py:731
  (48 shorter events, 2.2 us)
Async XLA Ops:
  0.7 4.7 %copy-start.3 = (bf16[2048,512]{1,0:T(8,128)(2,1)S(1)}, bf16[2048,512]{1,0:T(8,128)(2,1)}, u32[]{:S(2)}) copy-start(bf16[2048,512]{1,0:T(8,128)(2,1)} %refs_1_.5) | copy-start | bytes 6291460
  0.7 4.7 %copy-start.4 = (bf16[2048,512]{1,0:T(8,128)(2,1)S(1)}, bf16[2048,512]{1,0:T(8,128)(2,1)}, u32[]{:S(2)}) copy-start(bf16[2048,512]{1,0:T(8,128)(2,1)} %refs_2_.6) | copy-start | bytes 6291460
  0.7 4.7 %copy-start.6 = (bf16[32,2048]{1,0:T(8,128)(2,1)S(1)}, bf16[32,2048]{1,0:T(8,128)(2,1)}, u32[]{:S(2)}) copy-start(bf16[32,2048]{1,0:T(8,128)(2,1)} %refs_3_.1) | copy-start | bytes 393220
  2.3 6.0 %copy-start.5 = (bf16[2048,512]{1,0:T(8,128)(2,1)S(1)}, bf16[2048,512]{1,0:T(8,128)(2,1)}, u32[]{:S(2)}) copy-start(bf16[2048,512]{1,0:T(8,128)(2,1)} %refs_1_.6) | copy-start | bytes 6291460
  2.3 20.9 %collective-permute-start.7 = (bf16[3,2,128,512]{3,2,1,0:T(8,128)(2,1)S(1)}, bf16[3,2,128,512]{3,2,1,0:T(8,128)(2,1)S(1)}, u32[]{:S(2)}, u32[]{:S(2)}) collective-permute-start(bf16[3,2,128,512]{3,2,1,0:T(8,128)(2,1)S(1)} %pad_maximum_fusion), channel_id=1, source_target_pairs={{0,4},{4,0},{8,12},{12,8},{16,20},{20,16},{24,28},{28,24},{1,5},{5... | collective-permute-start | bytes 2359304 | tf_op jit(solution)/shard_map/ppermute | solution.py:745
  6.3 4.5 %copy-start.7 = (f32[512]{0:T(512)S(1)}, f32[512]{0:T(512)}, u32[]{:S(2)}) copy-start(f32[512]{0:T(512)} %param.18) | copy-start | bytes 6148
  6.3 16.9 %copy-start = (bf16[4,128,512]{2,1,0:T(8,128)(2,1)S(1)}, bf16[4,128,512]{2,1,0:T(8,128)(2,1)}, u32[]{:S(2)}) copy-start(bf16[4,128,512]{2,1,0:T(8,128)(2,1)} %refs_1_.9) | copy-start | bytes 1572868
  6.3 16.9 %copy-start.1 = (bf16[4,128,512]{2,1,0:T(8,128)(2,1)S(1)}, bf16[4,128,512]{2,1,0:T(8,128)(2,1)}, u32[]{:S(2)}) copy-start(bf16[4,128,512]{2,1,0:T(8,128)(2,1)} %refs_2_.9) | copy-start | bytes 1572868
  6.4 3.6 %collective-permute-start = (f32[8,256]{1,0:T(8,128)S(1)}, f32[8,256]{1,0:T(8,128)S(1)}, u32[]{:S(2)}, u32[]{:S(2)}) collective-permute-start(f32[8,256]{1,0:T(8,128)S(1)} %get-tuple-element.31.refs_7_), channel_id=1, source_target_pairs={{0,3},{1,2},{2,1},{3,0},{4,7},{5,6},{6,5},{7,4},{8,11},{9,10},{10,... | collective-permute-start | bytes 24584 | tf_op jit(solution)/shard_map/ppermute | solution.py:742
  7.1 3.7 %collective-permute-start.1 = (f32[8,256]{1,0:T(8,128)S(1)}, f32[8,256]{1,0:T(8,128)S(1)}, u32[]{:S(2)}, u32[]{:S(2)}) collective-permute-start(f32[8,256]{1,0:T(8,128)S(1)} %get-tuple-element.31.refs_7_), channel_id=1, source_target_pairs={{0,2},{1,3},{2,0},{3,1},{4,6},{5,7},{6,4},{7,5},{8,10},{9,11},{10,... | collective-permute-start | bytes 24584 | tf_op jit(solution)/shard_map/ppermute | solution.py:742
  8.0 2.8 %collective-permute-start.2 = (f32[8,256]{1,0:T(8,128)S(1)}, f32[8,256]{1,0:T(8,128)S(1)}, u32[]{:S(2)}, u32[]{:S(2)}) collective-permute-start(f32[8,256]{1,0:T(8,128)S(1)} %get-tuple-element.31.refs_7_), channel_id=1, source_target_pairs={{0,1},{1,0},{2,3},{3,2},{4,5},{5,4},{6,7},{7,6},{8,9},{9,8},{10,11... | collective-permute-start | bytes 24584 | tf_op jit(solution)/shard_map/ppermute | solution.py:742
  8.7 26.5 %copy-start.2 = (bf16[512,2048]{1,0:T(8,128)(2,1)S(1)}, bf16[512,2048]{1,0:T(8,128)(2,1)}, u32[]{:S(2)}) copy-start(bf16[512,2048]{1,0:T(8,128)(2,1)} %refs_5_.1) | copy-start | bytes 6291460
  11.0 7.6 %collective-permute-start.4 = (bf16[32,1536]{1,0:T(8,128)(2,1)S(1)}, bf16[32,1536]{1,0:T(8,128)(2,1)S(1)}, u32[]{:S(2)}, u32[]{:S(2)}) collective-permute-start(bf16[32,1536]{1,0:T(8,128)(2,1)S(1)} %get-tuple-element.32.refs_4_.refs_3_), channel_id=1, source_target_pairs={{0,24},{4,28},{8,16},{12,20},{16,8},{20,12},{24,0},{28,4},{1,25},{... | collective-permute-start | bytes 294920 | tf_op jit(solution)/shard_map/ppermute | solution.py:748
  14.7 8.5 %collective-permute-start.5 = (bf16[32,1536]{1,0:T(8,128)(2,1)S(1)}, bf16[32,1536]{1,0:T(8,128)(2,1)S(1)}, u32[]{:S(2)}, u32[]{:S(2)}) collective-permute-start(bf16[32,1536]{1,0:T(8,128)(2,1)S(1)} %get-tuple-element.32.refs_4_.refs_3_), channel_id=1, source_target_pairs={{0,16},{4,20},{8,24},{12,28},{16,0},{20,4},{24,8},{28,12},{1,17},{... | collective-permute-start | bytes 294920 | tf_op jit(solution)/shard_map/ppermute | solution.py:748
  14.7 8.5 %collective-permute-start.6 = (bf16[32,1536]{1,0:T(8,128)(2,1)S(1)}, bf16[32,1536]{1,0:T(8,128)(2,1)S(1)}, u32[]{:S(2)}, u32[]{:S(2)}) collective-permute-start(bf16[32,1536]{1,0:T(8,128)(2,1)S(1)} %get-tuple-element.32.refs_4_.refs_3_), channel_id=1, source_target_pairs={{0,8},{4,12},{8,0},{12,4},{16,24},{20,28},{24,16},{28,20},{1,9},{5... | collective-permute-start | bytes 294920 | tf_op jit(solution)/shard_map/ppermute | solution.py:748
  15.5 12.6 %collective-permute-start.3 = (bf16[32,512]{1,0:T(8,128)(2,1)S(1)}, bf16[32,512]{1,0:T(8,128)(2,1)S(1)}, u32[]{:S(2)}, u32[]{:S(2)}) collective-permute-start(bf16[32,512]{1,0:T(8,128)(2,1)S(1)} %get-tuple-element.33), channel_id=1, source_target_pairs={{0,4},{4,0},{8,12},{12,8},{16,20},{20,16},{24,28},{28,24},{1,5},{5... | collective-permute-start | bytes 98312 | tf_op jit(solution)/shard_map/ppermute | solution.py:745
  24.2 9.2 %collective-permute-start.10 = (bf16[48,512]{1,0:T(8,128)(2,1)S(1)}, bf16[48,512]{1,0:T(8,128)(2,1)S(1)}, u32[]{:S(2)}, u32[]{:S(2)}) collective-permute-start(bf16[48,512]{1,0:T(8,128)(2,1)S(1)} %get-tuple-element.34.refs_9_), channel_id=1, source_target_pairs={{0,24},{4,28},{8,16},{12,20},{16,8},{20,12},{24,0},{28,4},{1,25},{... | collective-permute-start | bytes 147464 | tf_op jit(solution)/shard_map/ppermute | solution.py:748
  28.7 4.7 %collective-permute-start.8 = (bf16[48,512]{1,0:T(8,128)(2,1)S(1)}, bf16[48,512]{1,0:T(8,128)(2,1)S(1)}, u32[]{:S(2)}, u32[]{:S(2)}) collective-permute-start(bf16[48,512]{1,0:T(8,128)(2,1)S(1)} %get-tuple-element.35), channel_id=1, source_target_pairs={{0,4},{4,0},{8,12},{12,8},{16,20},{20,16},{24,28},{28,24},{1,5},{5... | collective-permute-start | bytes 147464 | tf_op jit(solution)/shard_map/ppermute | solution.py:745
  30.3 5.0 %collective-permute-start.11 = (bf16[48,512]{1,0:T(8,128)(2,1)S(1)}, bf16[48,512]{1,0:T(8,128)(2,1)S(1)}, u32[]{:S(2)}, u32[]{:S(2)}) collective-permute-start(bf16[48,512]{1,0:T(8,128)(2,1)S(1)} %get-tuple-element.37), channel_id=1, source_target_pairs={{0,16},{4,20},{8,24},{12,28},{16,0},{20,4},{24,8},{28,12},{1,17},{... | collective-permute-start | bytes 147464 | tf_op jit(solution)/shard_map/ppermute | solution.py:748
  30.3 5.0 %collective-permute-start.9 = (bf16[48,512]{1,0:T(8,128)(2,1)S(1)}, bf16[48,512]{1,0:T(8,128)(2,1)S(1)}, u32[]{:S(2)}, u32[]{:S(2)}) collective-permute-start(bf16[48,512]{1,0:T(8,128)(2,1)S(1)} %get-tuple-element.36), channel_id=1, source_target_pairs={{0,8},{4,12},{8,0},{12,4},{16,24},{20,28},{24,16},{28,20},{1,9},{5... | collective-permute-start | bytes 147464 | tf_op jit(solution)/shard_map/ppermute | solution.py:748
  31.0 8.0 %collective-permute-start.14 = (bf16[288,512]{1,0:T(8,128)(2,1)S(1)}, bf16[288,512]{1,0:T(8,128)(2,1)S(1)}, u32[]{:S(2)}, u32[]{:S(2)}) collective-permute-start(bf16[288,512]{1,0:T(8,128)(2,1)S(1)} %get-tuple-element.44), channel_id=1, source_target_pairs={{0,4},{4,0},{8,12},{12,8},{16,20},{20,16},{24,28},{28,24},{1,5},{5... | collective-permute-start | bytes 884744 | tf_op jit(solution)/shard_map/ppermute | solution.py:745
  35.3 7.8 %copy-start.9 = (f32[512]{0:T(512)S(1)}, f32[512]{0:T(512)}, u32[]{:S(2)}) copy-start(f32[512]{0:T(512)} %param.20) | copy-start | bytes 6148
  36.0 1.4 %collective-permute-start.12 = (bf16[32,2048]{1,0:T(8,128)(2,1)S(1)}, bf16[32,2048]{1,0:T(8,128)(2,1)S(1)}, u32[]{:S(2)}, u32[]{:S(2)}) collective-permute-start(bf16[32,2048]{1,0:T(8,128)(2,1)S(1)} %get-tuple-element.40), channel_id=1, source_target_pairs={{0,1},{1,0},{2,3},{3,2},{4,5},{5,4},{6,7},{7,6},{8,9},{9,8},{10,11... | collective-permute-start | bytes 393224 | tf_op jit(solution)/shard_map/ppermute | solution.py:742
  37.4 5.6 %collective-permute-start.13 = (bf16[32,2048]{1,0:T(8,128)(2,1)S(1)}, bf16[32,2048]{1,0:T(8,128)(2,1)S(1)}, u32[]{:S(2)}, u32[]{:S(2)}) collective-permute-start(bf16[32,2048]{1,0:T(8,128)(2,1)S(1)} %get-tuple-element.42), channel_id=1, source_target_pairs={{0,2},{1,3},{2,0},{3,1},{4,6},{5,7},{6,4},{7,5},{8,10},{9,11},{10,... | collective-permute-start | bytes 393224 | tf_op jit(solution)/shard_map/ppermute | solution.py:742
  (4 other events, 12.0 us)

commit v6 on v5

--- a/solution.py
+++ b/solution.py
@@ -602,7 +602,7 @@
         [jnp.where(here, 1.0, 0.0), own_tree[...], jnp.zeros((2 * own, rest), F32)], axis=1
     )
     near = near > 0.5
-    pair = stacked([mine[:, :width], other[...]])
+    pair = stacked([mine[:, :width], other[:, :width]])
     for h in range(heads):
         lanes = slice(h * HEAD_DIM, (h + 1) * HEAD_DIM)
         keys = jnp.concatenate(
@@ -624,12 +624,13 @@
         stats = kept(stats, h, heads, found)
     write_stats(stats[:own], local)
     write_stats(stats[own:], crossing)
-    for at, ref in enumerate((mine, *queries)):
+    for at, ref in enumerate(queries):
         for part in range(2):
             rows = slice((2 * at + part) * own, (2 * at + part + 1) * own)
             copied[rows, :] = ref[:, (part + 1) * width : (part + 2) * width]
-    last = 2 * (count + 1) * own
-    copied[last:, :] = jnp.zeros((copied.shape[0] - last, width), BF16)
+    last = 2 * count * own
+    if copied.shape[0] > last:
+        copied[last:, :] = jnp.zeros((copied.shape[0] - last, width), BF16)
 
 
 def twin_rows(mine, theirs, held):
@@ -679,7 +680,7 @@
 
 def twin_compact(far, targets, key_cache, value_cache, *refs):
     count = len(far) + 1
-    ours, (copied, new_keys, new_values, held) = refs[:count], refs[count:]
+    ours, (beside, copied, new_keys, new_values, held) = refs[:count], refs[count:]
     block, width = key_cache.shape[1:]
     own = ours[0].shape[0]
     me = lax.axis_index("seq")
@@ -691,8 +692,8 @@
         placing = placing.astype(BF16)
         for part, (cache, out) in enumerate(((key_cache, new_keys), (value_cache, new_values))):
             lanes = slice((part + 1) * width, (part + 2) * width)
-            rows = slice((2 * at + part) * own, (2 * at + part + 1) * own)
-            theirs = copied[rows, :]
+            first = (2 * (at - 1) + part) * own
+            theirs = copied[first : first + own, :] if at else beside[:, lanes]
             fresh = twin_rows(ours[at][:, lanes], theirs, held.at[at, part])
             moved = dot(placing, fresh)
             out[request] = jnp.where(written, moved, cache[request].astype(F32)).astype(BF16)
@@ -794,7 +795,7 @@
         ),
     )
     from_far = [over_planes(packed, turn) for turn in far]
-    other = beside(queries)
+    other = beside(packed)
 
     rows = own + 16
     partials = call(
@@ -805,14 +806,14 @@
     )
     crossing, local, copied = call(
         twin_attend_near,
-        (shaped((rows, width), BF16),) * 2 + (shaped((2 * requests * own + own, width), BF16),),
+        (shaped((rows, width), BF16),) * 2 + (shaped((2 * len(far) * own, width), BF16),),
         (limits, key_cache, value_cache, own_tree, packed, other, *from_far),
         [pltpu.VMEM((heads, 2 * own, block + LANES), F32)],
         ties=partials[:1],
     )
     partials = [over_planes(part, turn) for part, turn in zip(partials, far)]
     partials += [beside(crossing)]
-    partials = [partials[3], partials[2], partials[0], partials[1], local]
+    partials = [partials[0], partials[1], partials[2], partials[3], local]
     copied = beside(copied)
 
     total, rounded = call(
@@ -832,7 +833,7 @@
     new_key_cache, new_value_cache = call(
         functools.partial(twin_compact, far),
         (shaped(key_cache.shape, BF16), shaped(value_cache.shape, BF16)),
-        (targets, key_cache, value_cache, packed, *from_far, copied),
+        (targets, key_cache, value_cache, packed, *from_far, other, copied),
         [pltpu.VMEM((requests, 2, 2, own, width), BF16)],
     )
     hidden_out = call(

time: 44 us -> 44.6 us (1.014)
  starting transfers between devices: 18.6 us -> 20.1 us
  waiting for transfers between devices: 15.4 us -> 14 us
  Pallas kernels: 7.19 us -> 7.8 us
    ppermute x5, waiting for transfers between devices: 4.83 us -> 0.85 us  [over_tp(): return lax.ppermute(x, 'tp', [(i, i ^ k) for i in range(tp)])]
    ppermute x4, waiting for transfers between devices: 2.02 us -> 4.43 us  [beside(): return lax.ppermute(x, 'seq', [(i, i ^ 1) for i in range(seq)])]
    ppermute x4, starting transfers between devices: 5.9 us -> 7.41 us  [beside(): return lax.ppermute(x, 'seq', [(i, i ^ 1) for i in range(seq)])]
    pallas_call x10, Pallas kernels: 7.19 us -> 7.8 us  [call(): pl.pallas_call(run, out_shape=outs, in_specs=([VMEM] * count if specs is...]
  transfers between devices with their start and end apart: 15 -> 15, of which waited for: 7 -> 6; matrix products, arithmetic and copies ran while one was open for 0% -> 0% of each run, Pallas kernels for 15% -> 14%
where the time goes in v6:
time: 44.6 us; the launch traced here: 44.5 us
  starting transfers between devices  20.1 us (45%)
  waiting for transfers between devices  14 us (31%)
  Pallas kernels  7.8 us (17%)
  local copies, waits for them, and re-layouts  1.51 us (3%)
  between operations  0.89 us (2%)
    ppermute x6, starting transfers between devices, over_planes(): lax.ppermute(x, 'seq', [(i, (i // 2 ^ turn) * 2 + i % 2) for i in range(s...  9.1 us
    ppermute x6, waiting for transfers between devices, over_planes(): lax.ppermute(x, 'seq', [(i, (i // 2 ^ turn) * 2 + i % 2) for i in range(s...  8.75 us
    pallas_call x10, Pallas kernels, call(): pl.pallas_call(run, out_shape=outs, in_specs=([VMEM] * count if specs is...  7.8 us
    ppermute x4, starting transfers between devices, beside(): return lax.ppermute(x, 'seq', [(i, i ^ 1) for i in range(seq)])  7.41 us
    ppermute x4, waiting for transfers between devices, beside(): return lax.ppermute(x, 'seq', [(i, i ^ 1) for i in range(seq)])  4.43 us
    ppermute x5, starting transfers between devices, over_tp(): return lax.ppermute(x, 'tp', [(i, i ^ k) for i in range(tp)])  3.55 us
    dynamic_slice x1, local copies, waits for them, and re-layouts, picked(): lax.dynamic_index_in_dim(x, me ^ turn, 0, False)  1.43 us
  transfers between devices with their start and end apart: 15, of which 6 were waited for; matrix products, arithmetic and copies ran while one was open for 0% of the time, Pallas kernels for 14%

profile of v6, /device:TPU:0, one launch (start us, length us, event | category | flops | bytes accessed | tf_op | source)
XLA Modules:
  0.0 44.5 jit_solution(18392467769794037364)
XLA Ops:
  0.7 1.4 %constant_dynamic-slice_fusion.4 = (bf16[1,128,512]{2,1,0:T(8,128)(2,1)S(1)}, bf16[1,128,512]{2,1,0:T(8,128)(2,1)S(1)}, bf16[1,128,512]{2,1,0:T(8,128)(2,1)S(1)}...) fusion(bf16[4,128,512]{2,1,0:T(8,128)(2,1)} %refs_2_.9, ...), kind=kLoop, calls=%fused_computation.9 | loop fusion | bytes 1572876 | tf_op jit(solution)/shard_map/jit(dynamic_index_in_dim)/dynamic_slice | solution.py:755
  2.3 3.0 %collective-permute-start = (bf16[3,2,128,512]{3,2,1,0:T(8,128)(2,1)S(1)}, bf16[3,2,128,512]{3,2,1,0:T(8,128)(2,1)S(1)}, u32[]{:S(2)}, u32[]{:S(2)}) collective-permute-start(bf16[3,2,128,512]{3,2,1,0:T(8,128)(2,1)S(1)} %pad_maximum_fusion), channel_id=1, source_target_pairs={{0,4},{4,0},{8,12},{12,8},{16,20},{20,16},{24,28},{28,24},{1,5},{5... | collective-permute-start | bytes 2359304 | tf_op jit(solution)/shard_map/ppermute | solution.py:746
  5.4 0.9 %twin_project_qk.1 = (f32[32,512]{1,0:T(8,128)S(1)}, f32[32,512]{1,0:T(8,128)S(1)}, f32[8,256]{1,0:T(8,128)S(1)}) custom-call(bf16[32,2048]{1,0:T(8,128)(2,1)S(1)} %copy-done.6, bf16[2048,512]{1,0:T(8,128)(2,1)S(1)} %copy-done.3, bf16[2048,512]{1,0:T(8,128)(2,1)S(1)} %copy-done.4), custom_call_target="tpu_custom_call" | custom-call | tf_op jit(solution)/shard_map/twin_project_qk/pallas_call | solution.py:732
  6.4 0.7 %collective-permute-start.1 = (f32[8,256]{1,0:T(8,128)S(1)}, f32[8,256]{1,0:T(8,128)S(1)}, u32[]{:S(2)}, u32[]{:S(2)}) collective-permute-start(f32[8,256]{1,0:T(8,128)S(1)} %get-tuple-element.29.refs_7_), channel_id=1, source_target_pairs={{0,3},{1,2},{2,1},{3,0},{4,7},{5,6},{6,5},{7,4},{8,11},{9,10},{10,... | collective-permute-start | bytes 24584 | tf_op jit(solution)/shard_map/ppermute | solution.py:743
  7.1 0.9 %collective-permute-start.2 = (f32[8,256]{1,0:T(8,128)S(1)}, f32[8,256]{1,0:T(8,128)S(1)}, u32[]{:S(2)}, u32[]{:S(2)}) collective-permute-start(f32[8,256]{1,0:T(8,128)S(1)} %get-tuple-element.29.refs_7_), channel_id=1, source_target_pairs={{0,2},{1,3},{2,0},{3,1},{4,6},{5,7},{6,4},{7,5},{8,10},{9,11},{10,... | collective-permute-start | bytes 24584 | tf_op jit(solution)/shard_map/ppermute | solution.py:743
  8.8 1.2 %twin_tree.1 = (f32[64,32]{1,0:T(8,128)S(1)}, s32[4,1,64]{2,1,0:T(1,128)S(1)}, f32[32,128]{1,0:T(8,128)S(1)}, f32[32,128]{1,0:T(8,128)S(1)}, s32[4,256]{1,0:T(4,128)S(1)}) custom-call(s32[1,4]{1,0:T(1,128)S(1)} %bitcast.14, s32[1,4]{1,0:T(1,128)S(1)} %bitcast.15, s32[4,64]{1,0:T(4,128)S(1)} %copy-done.10, f32[1,128]{1,0:T(1,128)S(1)} %fusion.2.refs_3_), custom_call_target="tpu_custom_call" | custom-call | tf_op jit(solution)/shard_map/twin_tree/pallas_call | solution.py:732
  10.0 0.8 %collective-permute-done.2.refs_9_ = f32[8,256]{1,0:T(8,128)S(1)} collective-permute-done((f32[8,256]{1,0:T(8,128)S(1)}, f32[8,256]{1,0:T(8,128)S(1)}, u32[]{:S(2)}, u32[]{:S(2)}) %collective-permute-start.2) | collective-permute-done | bytes 8224 | tf_op jit(solution)/shard_map/ppermute | solution.py:743
  10.8 0.8 %twin_prepare.1 = (bf16[32,512]{1,0:T(8,128)(2,1)}, bf16[32,1536]{1,0:T(8,128)(2,1)S(1)}) custom-call(f32[32,512]{1,0:T(8,128)S(1)} %get-tuple-element.25.refs_0_, f32[32,512]{1,0:T(8,128)S(1)} %get-tuple-element.26.refs_1_, bf16[32,512]{1,0:T(8,128)(2,1)S(1)} %twin_project_v.1.refs_2_, f32[1,512]{1,0:T(1,128)S(1)} %bitcast.11, f32[1,512]{1,0:T(1,128)S(1)} %bitcast.12, ...), custom_call_target="tpu_custom_call" | custom-call | tf_op jit(solution)/shard_map/twin_prepare/pallas_call | solution.py:732
  11.6 3.6 %collective-permute-start.4 = (bf16[32,1536]{1,0:T(8,128)(2,1)S(1)}, bf16[32,1536]{1,0:T(8,128)(2,1)S(1)}, u32[]{:S(2)}, u32[]{:S(2)}) collective-permute-start(bf16[32,1536]{1,0:T(8,128)(2,1)S(1)} %get-tuple-element.30.refs_4_.refs_3_), channel_id=1, source_target_pairs={{0,24},{4,28},{8,16},{12,20},{16,8},{20,12},{24,0},{28,4},{1,25},{... | collective-permute-start | bytes 294920 | tf_op jit(solution)/shard_map/ppermute | solution.py:749
  15.2 0.8 %collective-permute-start.6 = (bf16[32,1536]{1,0:T(8,128)(2,1)S(1)}, bf16[32,1536]{1,0:T(8,128)(2,1)S(1)}, u32[]{:S(2)}, u32[]{:S(2)}) collective-permute-start(bf16[32,1536]{1,0:T(8,128)(2,1)S(1)} %get-tuple-element.30.refs_4_.refs_3_), channel_id=1, source_target_pairs={{0,8},{4,12},{8,0},{12,4},{16,24},{20,28},{24,16},{28,20},{1,9},{5... | collective-permute-start | bytes 294920 | tf_op jit(solution)/shard_map/ppermute | solution.py:749
  16.0 1.0 %collective-permute-start.10 = (bf16[32,1536]{1,0:T(8,128)(2,1)S(1)}, bf16[32,1536]{1,0:T(8,128)(2,1)S(1)}, u32[]{:S(2)}, u32[]{:S(2)}) collective-permute-start(bf16[32,1536]{1,0:T(8,128)(2,1)S(1)} %get-tuple-element.30.refs_4_.refs_3_), channel_id=1, source_target_pairs={{0,4},{4,0},{8,12},{12,8},{16,20},{20,16},{24,28},{28,24},{1,5},{5... | collective-permute-start | bytes 294920 | tf_op jit(solution)/shard_map/ppermute | solution.py:746
  17.0 2.1 %collective-permute-done.4.refs_4_.refs_6_ = bf16[32,1536]{1,0:T(8,128)(2,1)S(1)} collective-permute-done((bf16[32,1536]{1,0:T(8,128)(2,1)S(1)}, bf16[32,1536]{1,0:T(8,128)(2,1)S(1)}, u32[]{:S(2)}, u32[]{:S(2)}) %collective-permute-start.4) | collective-permute-done | bytes 98336 | tf_op jit(solution)/shard_map/ppermute | solution.py:749
  19.2 4.6 %collective-permute-done.5.refs_5_.refs_7_ = bf16[32,1536]{1,0:T(8,128)(2,1)S(1)} collective-permute-done((bf16[32,1536]{1,0:T(8,128)(2,1)S(1)}, bf16[32,1536]{1,0:T(8,128)(2,1)S(1)}, u32[]{:S(2)}, u32[]{:S(2)}) %collective-permute-start.5) | collective-permute-done | bytes 98336 | tf_op jit(solution)/shard_map/ppermute | solution.py:749
  23.8 0.9 %twin_attend_far.1 = (bf16[48,512]{1,0:T(8,128)(2,1)S(1)}, bf16[48,512]{1,0:T(8,128)(2,1)S(1)}, bf16[48,512]{1,0:T(8,128)(2,1)S(1)}) custom-call(s32[4,256]{1,0:T(4,128)S(1)} %get-tuple-element.24.refs_0_, bf16[4,128,512]{2,1,0:T(8,128)(2,1)S(1)} %copy-done, bf16[4,128,512]{2,1,0:T(8,128)(2,1)S(1)} %copy-done.1, ...), custom_call_target="tpu_custom_call" | custom-call | tf_op jit(solution)/shard_map/twin_attend_far/pallas_call | solution.py:732
  24.7 4.1 %collective-permute-start.7 = (bf16[48,512]{1,0:T(8,128)(2,1)S(1)}, bf16[48,512]{1,0:T(8,128)(2,1)S(1)}, u32[]{:S(2)}, u32[]{:S(2)}) collective-permute-start(bf16[48,512]{1,0:T(8,128)(2,1)S(1)} %get-tuple-element.31.refs_9_), channel_id=1, source_target_pairs={{0,24},{4,28},{8,16},{12,20},{16,8},{20,12},{24,0},{28,4},{1,25},{... | collective-permute-start | bytes 147464 | tf_op jit(solution)/shard_map/ppermute | solution.py:749
  28.8 0.6 %collective-permute-start.9 = (bf16[48,512]{1,0:T(8,128)(2,1)S(1)}, bf16[48,512]{1,0:T(8,128)(2,1)S(1)}, u32[]{:S(2)}, u32[]{:S(2)}) collective-permute-start(bf16[48,512]{1,0:T(8,128)(2,1)S(1)} %get-tuple-element.33), channel_id=1, source_target_pairs={{0,8},{4,12},{8,0},{12,4},{16,24},{20,28},{24,16},{28,20},{1,9},{5... | collective-permute-start | bytes 147464 | tf_op jit(solution)/shard_map/ppermute | solution.py:749
  30.0 1.7 %collective-permute-start.11 = (bf16[48,512]{1,0:T(8,128)(2,1)S(1)}, bf16[48,512]{1,0:T(8,128)(2,1)S(1)}, u32[]{:S(2)}, u32[]{:S(2)}) collective-permute-start(bf16[48,512]{1,0:T(8,128)(2,1)S(1)} %get-tuple-element.35), channel_id=1, source_target_pairs={{0,4},{4,0},{8,12},{12,8},{16,20},{20,16},{24,28},{28,24},{1,5},{5... | collective-permute-start | bytes 147464 | tf_op jit(solution)/shard_map/ppermute | solution.py:746
  31.7 2.0 %collective-permute-done.8.refs_1_ = bf16[48,512]{1,0:T(8,128)(2,1)S(1)} collective-permute-done((bf16[48,512]{1,0:T(8,128)(2,1)S(1)}, bf16[48,512]{1,0:T(8,128)(2,1)S(1)}, u32[]{:S(2)}, u32[]{:S(2)}) %collective-permute-start.8) | collective-permute-done | bytes 49184 | tf_op jit(solution)/shard_map/ppermute | solution.py:749
  34.2 0.8 %twin_merge_and_project.1 = (f32[32,2048]{1,0:T(8,128)S(1)}, bf16[32,2048]{1,0:T(8,128)(2,1)S(1)}) custom-call(bf16[48,512]{1,0:T(8,128)(2,1)S(1)} %collective-permute-done.7.refs_0_, bf16[48,512]{1,0:T(8,128)(2,1)S(1)} %collective-permute-done.8.refs_1_, bf16[48,512]{1,0:T(8,128)(2,1)S(1)} %collective-permute-done.9.refs_2_, ...), custom_call_target="tpu_custom_call" | custom-call | tf_op jit(solution)/shard_map/twin_merge_and_project/pallas_call | solution.py:732
  35.0 1.7 %collective-permute-start.14 = (bf16[192,512]{1,0:T(8,128)(2,1)S(1)}, bf16[192,512]{1,0:T(8,128)(2,1)S(1)}, u32[]{:S(2)}, u32[]{:S(2)}) collective-permute-start(bf16[192,512]{1,0:T(8,128)(2,1)S(1)} %get-tuple-element.42), channel_id=1, source_target_pairs={{0,4},{4,0},{8,12},{12,8},{16,20},{20,16},{24,28},{28,24},{1,5},{5... | collective-permute-start | bytes 589832 | tf_op jit(solution)/shard_map/ppermute | solution.py:746
  36.8 1.6 %collective-permute-start.13 = (bf16[32,2048]{1,0:T(8,128)(2,1)S(1)}, bf16[32,2048]{1,0:T(8,128)(2,1)S(1)}, u32[]{:S(2)}, u32[]{:S(2)}) collective-permute-start(bf16[32,2048]{1,0:T(8,128)(2,1)S(1)} %get-tuple-element.40), channel_id=1, source_target_pairs={{0,2},{1,3},{2,0},{3,1},{4,6},{5,7},{6,4},{7,5},{8,10},{9,11},{10,... | collective-permute-start | bytes 393224 | tf_op jit(solution)/shard_map/ppermute | solution.py:743
  38.4 4.0 %collective-permute-done.14.refs_8_ = bf16[192,512]{1,0:T(8,128)(2,1)S(1)} collective-permute-done((bf16[192,512]{1,0:T(8,128)(2,1)S(1)}, bf16[192,512]{1,0:T(8,128)(2,1)S(1)}, u32[]{:S(2)}, u32[]{:S(2)}) %collective-permute-start.14) | collective-permute-done | bytes 196640 | tf_op jit(solution)/shard_map/ppermute | solution.py:746
  42.3 1.4 %twin_compact.1 = (bf16[4,128,512]{2,1,0:T(8,128)(2,1)}, bf16[4,128,512]{2,1,0:T(8,128)(2,1)}) custom-call(s32[4,1,64]{2,1,0:T(1,128)S(1)} %get-tuple-element.41.refs_0_, bf16[4,128,512]{2,1,0:T(8,128)(2,1)S(1)} %copy-done, bf16[4,128,512]{2,1,0:T(8,128)(2,1)S(1)} %copy-done.1, bf16[32,1536]{1,0:T(8,128)(2,1)S(1)} %get-tuple-element.30.refs_4_.refs_3_, ...), custom_call_target="tpu_custom_call" | custom-call | tf_op jit(solution)/shard_map/twin_compact/pallas_call | solution.py:732
  43.7 0.7 %twin_finish.1 = bf16[32,512]{1,0:T(8,128)(2,1)} custom-call(f32[32,2048]{1,0:T(8,128)S(1)} %get-tuple-element.39.refs_0_, bf16[32,2048]{1,0:T(8,128)(2,1)S(1)} %collective-permute-done.13.refs_1_, f32[1,512]{1,0:T(1,128)S(1)} %bitcast.13, bf16[32,2048]{1,0:T(8,128)(2,1)S(1)} %copy-done.6), custom_call_target="tpu_custom_call" | custom-call | tf_op jit(solution)/shard_map/twin_finish/pallas_call | solution.py:732
  (48 shorter events, 2.2 us)
Async XLA Ops:
  0.7 4.7 %copy-start.3 = (bf16[2048,512]{1,0:T(8,128)(2,1)S(1)}, bf16[2048,512]{1,0:T(8,128)(2,1)}, u32[]{:S(2)}) copy-start(bf16[2048,512]{1,0:T(8,128)(2,1)} %refs_1_.5) | copy-start | bytes 6291460
  0.7 4.7 %copy-start.4 = (bf16[2048,512]{1,0:T(8,128)(2,1)S(1)}, bf16[2048,512]{1,0:T(8,128)(2,1)}, u32[]{:S(2)}) copy-start(bf16[2048,512]{1,0:T(8,128)(2,1)} %refs_2_.6) | copy-start | bytes 6291460
  0.7 4.7 %copy-start.6 = (bf16[32,2048]{1,0:T(8,128)(2,1)S(1)}, bf16[32,2048]{1,0:T(8,128)(2,1)}, u32[]{:S(2)}) copy-start(bf16[32,2048]{1,0:T(8,128)(2,1)} %refs_3_.1) | copy-start | bytes 393220
  2.3 6.0 %copy-start.5 = (bf16[2048,512]{1,0:T(8,128)(2,1)S(1)}, bf16[2048,512]{1,0:T(8,128)(2,1)}, u32[]{:S(2)}) copy-start(bf16[2048,512]{1,0:T(8,128)(2,1)} %refs_1_.6) | copy-start | bytes 6291460
  2.3 21.4 %collective-permute-start = (bf16[3,2,128,512]{3,2,1,0:T(8,128)(2,1)S(1)}, bf16[3,2,128,512]{3,2,1,0:T(8,128)(2,1)S(1)}, u32[]{:S(2)}, u32[]{:S(2)}) collective-permute-start(bf16[3,2,128,512]{3,2,1,0:T(8,128)(2,1)S(1)} %pad_maximum_fusion), channel_id=1, source_target_pairs={{0,4},{4,0},{8,12},{12,8},{16,20},{20,16},{24,28},{28,24},{1,5},{5... | collective-permute-start | bytes 2359304 | tf_op jit(solution)/shard_map/ppermute | solution.py:746
  6.3 4.5 %copy-start.7 = (f32[512]{0:T(512)S(1)}, f32[512]{0:T(512)}, u32[]{:S(2)}) copy-start(f32[512]{0:T(512)} %param.18) | copy-start | bytes 6148
  6.3 17.4 %copy-start = (bf16[4,128,512]{2,1,0:T(8,128)(2,1)S(1)}, bf16[4,128,512]{2,1,0:T(8,128)(2,1)}, u32[]{:S(2)}) copy-start(bf16[4,128,512]{2,1,0:T(8,128)(2,1)} %refs_1_.9) | copy-start | bytes 1572868
  6.3 17.4 %copy-start.1 = (bf16[4,128,512]{2,1,0:T(8,128)(2,1)S(1)}, bf16[4,128,512]{2,1,0:T(8,128)(2,1)}, u32[]{:S(2)}) copy-start(bf16[4,128,512]{2,1,0:T(8,128)(2,1)} %refs_2_.9) | copy-start | bytes 1572868
  6.4 3.6 %collective-permute-start.1 = (f32[8,256]{1,0:T(8,128)S(1)}, f32[8,256]{1,0:T(8,128)S(1)}, u32[]{:S(2)}, u32[]{:S(2)}) collective-permute-start(f32[8,256]{1,0:T(8,128)S(1)} %get-tuple-element.29.refs_7_), channel_id=1, source_target_pairs={{0,3},{1,2},{2,1},{3,0},{4,7},{5,6},{6,5},{7,4},{8,11},{9,10},{10,... | collective-permute-start | bytes 24584 | tf_op jit(solution)/shard_map/ppermute | solution.py:743
  7.1 3.7 %collective-permute-start.2 = (f32[8,256]{1,0:T(8,128)S(1)}, f32[8,256]{1,0:T(8,128)S(1)}, u32[]{:S(2)}, u32[]{:S(2)}) collective-permute-start(f32[8,256]{1,0:T(8,128)S(1)} %get-tuple-element.29.refs_7_), channel_id=1, source_target_pairs={{0,2},{1,3},{2,0},{3,1},{4,6},{5,7},{6,4},{7,5},{8,10},{9,11},{10,... | collective-permute-start | bytes 24584 | tf_op jit(solution)/shard_map/ppermute | solution.py:743
  8.0 2.8 %collective-permute-start.3 = (f32[8,256]{1,0:T(8,128)S(1)}, f32[8,256]{1,0:T(8,128)S(1)}, u32[]{:S(2)}, u32[]{:S(2)}) collective-permute-start(f32[8,256]{1,0:T(8,128)S(1)} %get-tuple-element.29.refs_7_), channel_id=1, source_target_pairs={{0,1},{1,0},{2,3},{3,2},{4,5},{5,4},{6,7},{7,6},{8,9},{9,8},{10,11... | collective-permute-start | bytes 24584 | tf_op jit(solution)/shard_map/ppermute | solution.py:743
  8.7 25.5 %copy-start.2 = (bf16[512,2048]{1,0:T(8,128)(2,1)S(1)}, bf16[512,2048]{1,0:T(8,128)(2,1)}, u32[]{:S(2)}) copy-start(bf16[512,2048]{1,0:T(8,128)(2,1)} %refs_5_.1) | copy-start | bytes 6291460
  11.6 7.5 %collective-permute-start.4 = (bf16[32,1536]{1,0:T(8,128)(2,1)S(1)}, bf16[32,1536]{1,0:T(8,128)(2,1)S(1)}, u32[]{:S(2)}, u32[]{:S(2)}) collective-permute-start(bf16[32,1536]{1,0:T(8,128)(2,1)S(1)} %get-tuple-element.30.refs_4_.refs_3_), channel_id=1, source_target_pairs={{0,24},{4,28},{8,16},{12,20},{16,8},{20,12},{24,0},{28,4},{1,25},{... | collective-permute-start | bytes 294920 | tf_op jit(solution)/shard_map/ppermute | solution.py:749
  15.2 8.5 %collective-permute-start.5 = (bf16[32,1536]{1,0:T(8,128)(2,1)S(1)}, bf16[32,1536]{1,0:T(8,128)(2,1)S(1)}, u32[]{:S(2)}, u32[]{:S(2)}) collective-permute-start(bf16[32,1536]{1,0:T(8,128)(2,1)S(1)} %get-tuple-element.30.refs_4_.refs_3_), channel_id=1, source_target_pairs={{0,16},{4,20},{8,24},{12,28},{16,0},{20,4},{24,8},{28,12},{1,17},{... | collective-permute-start | bytes 294920 | tf_op jit(solution)/shard_map/ppermute | solution.py:749
  15.2 8.5 %collective-permute-start.6 = (bf16[32,1536]{1,0:T(8,128)(2,1)S(1)}, bf16[32,1536]{1,0:T(8,128)(2,1)S(1)}, u32[]{:S(2)}, u32[]{:S(2)}) collective-permute-start(bf16[32,1536]{1,0:T(8,128)(2,1)S(1)} %get-tuple-element.30.refs_4_.refs_3_), channel_id=1, source_target_pairs={{0,8},{4,12},{8,0},{12,4},{16,24},{20,28},{24,16},{28,20},{1,9},{5... | collective-permute-start | bytes 294920 | tf_op jit(solution)/shard_map/ppermute | solution.py:749
  16.0 13.4 %collective-permute-start.10 = (bf16[32,1536]{1,0:T(8,128)(2,1)S(1)}, bf16[32,1536]{1,0:T(8,128)(2,1)S(1)}, u32[]{:S(2)}, u32[]{:S(2)}) collective-permute-start(bf16[32,1536]{1,0:T(8,128)(2,1)S(1)} %get-tuple-element.30.refs_4_.refs_3_), channel_id=1, source_target_pairs={{0,4},{4,0},{8,12},{12,8},{16,20},{20,16},{24,28},{28,24},{1,5},{5... | collective-permute-start | bytes 294920 | tf_op jit(solution)/shard_map/ppermute | solution.py:746
  24.7 7.1 %collective-permute-start.7 = (bf16[48,512]{1,0:T(8,128)(2,1)S(1)}, bf16[48,512]{1,0:T(8,128)(2,1)S(1)}, u32[]{:S(2)}, u32[]{:S(2)}) collective-permute-start(bf16[48,512]{1,0:T(8,128)(2,1)S(1)} %get-tuple-element.31.refs_9_), channel_id=1, source_target_pairs={{0,24},{4,28},{8,16},{12,20},{16,8},{20,12},{24,0},{28,4},{1,25},{... | collective-permute-start | bytes 147464 | tf_op jit(solution)/shard_map/ppermute | solution.py:749
  28.8 5.0 %collective-permute-start.8 = (bf16[48,512]{1,0:T(8,128)(2,1)S(1)}, bf16[48,512]{1,0:T(8,128)(2,1)S(1)}, u32[]{:S(2)}, u32[]{:S(2)}) collective-permute-start(bf16[48,512]{1,0:T(8,128)(2,1)S(1)} %get-tuple-element.32), channel_id=1, source_target_pairs={{0,16},{4,20},{8,24},{12,28},{16,0},{20,4},{24,8},{28,12},{1,17},{... | collective-permute-start | bytes 147464 | tf_op jit(solution)/shard_map/ppermute | solution.py:749
  28.8 5.0 %collective-permute-start.9 = (bf16[48,512]{1,0:T(8,128)(2,1)S(1)}, bf16[48,512]{1,0:T(8,128)(2,1)S(1)}, u32[]{:S(2)}, u32[]{:S(2)}) collective-permute-start(bf16[48,512]{1,0:T(8,128)(2,1)S(1)} %get-tuple-element.33), channel_id=1, source_target_pairs={{0,8},{4,12},{8,0},{12,4},{16,24},{20,28},{24,16},{28,20},{1,9},{5... | collective-permute-start | bytes 147464 | tf_op jit(solution)/shard_map/ppermute | solution.py:749
  30.0 4.2 %collective-permute-start.11 = (bf16[48,512]{1,0:T(8,128)(2,1)S(1)}, bf16[48,512]{1,0:T(8,128)(2,1)S(1)}, u32[]{:S(2)}, u32[]{:S(2)}) collective-permute-start(bf16[48,512]{1,0:T(8,128)(2,1)S(1)} %get-tuple-element.35), channel_id=1, source_target_pairs={{0,4},{4,0},{8,12},{12,8},{16,20},{20,16},{24,28},{28,24},{1,5},{5... | collective-permute-start | bytes 147464 | tf_op jit(solution)/shard_map/ppermute | solution.py:746
  34.2 9.5 %copy-start.9 = (f32[512]{0:T(512)S(1)}, f32[512]{0:T(512)}, u32[]{:S(2)}) copy-start(f32[512]{0:T(512)} %param.20) | copy-start | bytes 6148
  35.0 1.8 %collective-permute-start.12 = (bf16[32,2048]{1,0:T(8,128)(2,1)S(1)}, bf16[32,2048]{1,0:T(8,128)(2,1)S(1)}, u32[]{:S(2)}, u32[]{:S(2)}) collective-permute-start(bf16[32,2048]{1,0:T(8,128)(2,1)S(1)} %get-tuple-element.38), channel_id=1, source_target_pairs={{0,1},{1,0},{2,3},{3,2},{4,5},{5,4},{6,7},{7,6},{8,9},{9,8},{10,11... | collective-permute-start | bytes 393224 | tf_op jit(solution)/shard_map/ppermute | solution.py:743
  35.0 7.3 %collective-permute-start.14 = (bf16[192,512]{1,0:T(8,128)(2,1)S(1)}, bf16[192,512]{1,0:T(8,128)(2,1)S(1)}, u32[]{:S(2)}, u32[]{:S(2)}) collective-permute-start(bf16[192,512]{1,0:T(8,128)(2,1)S(1)} %get-tuple-element.42), channel_id=1, source_target_pairs={{0,4},{4,0},{8,12},{12,8},{16,20},{20,16},{24,28},{28,24},{1,5},{5... | collective-permute-start | bytes 589832 | tf_op jit(solution)/shard_map/ppermute | solution.py:746
  36.8 6.9 %collective-permute-start.13 = (bf16[32,2048]{1,0:T(8,128)(2,1)S(1)}, bf16[32,2048]{1,0:T(8,128)(2,1)S(1)}, u32[]{:S(2)}, u32[]{:S(2)}) collective-permute-start(bf16[32,2048]{1,0:T(8,128)(2,1)S(1)} %get-tuple-element.40), channel_id=1, source_target_pairs={{0,2},{1,3},{2,0},{3,1},{4,6},{5,7},{6,4},{7,5},{8,10},{9,11},{10,... | collective-permute-start | bytes 393224 | tf_op jit(solution)/shard_map/ppermute | solution.py:743
  (4 other events, 12.0 us)

commit v7 on v5

--- a/solution.py
+++ b/solution.py
@@ -812,7 +812,7 @@
     )
     partials = [over_planes(part, turn) for part, turn in zip(partials, far)]
     partials += [beside(crossing)]
-    partials = [partials[3], partials[2], partials[0], partials[1], local]
+    partials = [partials[1], partials[0], partials[3], partials[2], local]
     copied = beside(copied)
 
     total, rounded = call(

time: 44 us -> 43.4 us (0.986)
  waiting for transfers between devices: 15.4 us -> 14.9 us
    ppermute x4, waiting for transfers between devices: 2.02 us -> 0.65 us  [beside(): return lax.ppermute(x, 'seq', [(i, i ^ 1) for i in range(seq)])]
    ppermute x6, waiting for transfers between devices: 8.59 us -> 9.42 us  [over_planes(): lax.ppermute(x, 'seq', [(i, (i // 2 ^ turn) * 2 + i % 2) for i in range(s...]
  transfers between devices with their start and end apart: 15 -> 15, of which waited for: 7 -> 8; matrix products, arithmetic and copies ran while one was open for 0% -> 0% of each run, Pallas kernels for 15% -> 15%
where the time goes in v7:
time: 43.4 us; the launch traced here: 43.2 us
  starting transfers between devices  18.6 us (43%)
  waiting for transfers between devices  14.9 us (34%)
  Pallas kernels  7.19 us (17%)
  local copies, waits for them, and re-layouts  1.51 us (3%)
  between operations  0.9 us (2%)
    ppermute x6, waiting for transfers between devices, over_planes(): lax.ppermute(x, 'seq', [(i, (i // 2 ^ turn) * 2 + i % 2) for i in range(s...  9.42 us
    ppermute x6, starting transfers between devices, over_planes(): lax.ppermute(x, 'seq', [(i, (i // 2 ^ turn) * 2 + i % 2) for i in range(s...  8.92 us
    pallas_call x10, Pallas kernels, call(): pl.pallas_call(run, out_shape=outs, in_specs=([VMEM] * count if specs is...  7.19 us
    ppermute x4, starting transfers between devices, beside(): return lax.ppermute(x, 'seq', [(i, i ^ 1) for i in range(seq)])  6.1 us
    ppermute x5, waiting for transfers between devices, over_tp(): return lax.ppermute(x, 'tp', [(i, i ^ k) for i in range(tp)])  4.83 us
    ppermute x5, starting transfers between devices, over_tp(): return lax.ppermute(x, 'tp', [(i, i ^ k) for i in range(tp)])  3.55 us
    dynamic_slice x1, local copies, waits for them, and re-layouts, picked(): lax.dynamic_index_in_dim(x, me ^ turn, 0, False)  1.43 us
  transfers between devices with their start and end apart: 15, of which 8 were waited for; matrix products, arithmetic and copies ran while one was open for 0% of the time, Pallas kernels for 15%

profile of v7, /device:TPU:0, one launch (start us, length us, event | category | flops | bytes accessed | tf_op | source)
XLA Modules:
  0.0 43.2 jit_solution(16349046305564292455)
XLA Ops:
  0.7 1.4 %constant_dynamic-slice_fusion.4 = (bf16[1,128,512]{2,1,0:T(8,128)(2,1)S(1)}, bf16[1,128,512]{2,1,0:T(8,128)(2,1)S(1)}, bf16[1,128,512]{2,1,0:T(8,128)(2,1)S(1)}...) fusion(bf16[4,128,512]{2,1,0:T(8,128)(2,1)} %refs_2_.9, ...), kind=kLoop, calls=%fused_computation.9 | loop fusion | bytes 1572876 | tf_op jit(solution)/shard_map/jit(dynamic_index_in_dim)/dynamic_slice | solution.py:754
  2.3 3.0 %collective-permute-start = (bf16[3,2,128,512]{3,2,1,0:T(8,128)(2,1)S(1)}, bf16[3,2,128,512]{3,2,1,0:T(8,128)(2,1)S(1)}, u32[]{:S(2)}, u32[]{:S(2)}) collective-permute-start(bf16[3,2,128,512]{3,2,1,0:T(8,128)(2,1)S(1)} %pad_maximum_fusion), channel_id=1, source_target_pairs={{0,4},{4,0},{8,12},{12,8},{16,20},{20,16},{24,28},{28,24},{1,5},{5... | collective-permute-start | bytes 2359304 | tf_op jit(solution)/shard_map/ppermute | solution.py:745
  5.4 0.9 %twin_project_qk.1 = (f32[32,512]{1,0:T(8,128)S(1)}, f32[32,512]{1,0:T(8,128)S(1)}, f32[8,256]{1,0:T(8,128)S(1)}) custom-call(bf16[32,2048]{1,0:T(8,128)(2,1)S(1)} %copy-done.6, bf16[2048,512]{1,0:T(8,128)(2,1)S(1)} %copy-done.3, bf16[2048,512]{1,0:T(8,128)(2,1)S(1)} %copy-done.4), custom_call_target="tpu_custom_call" | custom-call | tf_op jit(solution)/shard_map/twin_project_qk/pallas_call | solution.py:731
  6.4 0.7 %collective-permute-start.1 = (f32[8,256]{1,0:T(8,128)S(1)}, f32[8,256]{1,0:T(8,128)S(1)}, u32[]{:S(2)}, u32[]{:S(2)}) collective-permute-start(f32[8,256]{1,0:T(8,128)S(1)} %get-tuple-element.30.refs_7_), channel_id=1, source_target_pairs={{0,3},{1,2},{2,1},{3,0},{4,7},{5,6},{6,5},{7,4},{8,11},{9,10},{10,... | collective-permute-start | bytes 24584 | tf_op jit(solution)/shard_map/ppermute | solution.py:742
  7.1 0.9 %collective-permute-start.2 = (f32[8,256]{1,0:T(8,128)S(1)}, f32[8,256]{1,0:T(8,128)S(1)}, u32[]{:S(2)}, u32[]{:S(2)}) collective-permute-start(f32[8,256]{1,0:T(8,128)S(1)} %get-tuple-element.30.refs_7_), channel_id=1, source_target_pairs={{0,2},{1,3},{2,0},{3,1},{4,6},{5,7},{6,4},{7,5},{8,10},{9,11},{10,... | collective-permute-start | bytes 24584 | tf_op jit(solution)/shard_map/ppermute | solution.py:742
  8.8 1.2 %twin_tree.1 = (f32[64,32]{1,0:T(8,128)S(1)}, s32[4,1,64]{2,1,0:T(1,128)S(1)}, f32[32,128]{1,0:T(8,128)S(1)}, f32[32,128]{1,0:T(8,128)S(1)}, s32[4,256]{1,0:T(4,128)S(1)}) custom-call(s32[1,4]{1,0:T(1,128)S(1)} %bitcast.14, s32[1,4]{1,0:T(1,128)S(1)} %bitcast.15, s32[4,64]{1,0:T(4,128)S(1)} %copy-done.10, f32[1,128]{1,0:T(1,128)S(1)} %fusion.2.refs_3_), custom_call_target="tpu_custom_call" | custom-call | tf_op jit(solution)/shard_map/twin_tree/pallas_call | solution.py:731
  10.0 0.8 %collective-permute-done.2.refs_9_ = f32[8,256]{1,0:T(8,128)S(1)} collective-permute-done((f32[8,256]{1,0:T(8,128)S(1)}, f32[8,256]{1,0:T(8,128)S(1)}, u32[]{:S(2)}, u32[]{:S(2)}) %collective-permute-start.2) | collective-permute-done | bytes 8224 | tf_op jit(solution)/shard_map/ppermute | solution.py:742
  11.0 3.7 %collective-permute-start.4 = (bf16[32,1536]{1,0:T(8,128)(2,1)S(1)}, bf16[32,1536]{1,0:T(8,128)(2,1)S(1)}, u32[]{:S(2)}, u32[]{:S(2)}) collective-permute-start(bf16[32,1536]{1,0:T(8,128)(2,1)S(1)} %get-tuple-element.31.refs_4_.refs_3_), channel_id=1, source_target_pairs={{0,24},{4,28},{8,16},{12,20},{16,8},{20,12},{24,0},{28,4},{1,25},{... | collective-permute-start | bytes 294920 | tf_op jit(solution)/shard_map/ppermute | solution.py:748
  14.7 0.8 %collective-permute-start.6 = (bf16[32,1536]{1,0:T(8,128)(2,1)S(1)}, bf16[32,1536]{1,0:T(8,128)(2,1)S(1)}, u32[]{:S(2)}, u32[]{:S(2)}) collective-permute-start(bf16[32,1536]{1,0:T(8,128)(2,1)S(1)} %get-tuple-element.31.refs_4_.refs_3_), channel_id=1, source_target_pairs={{0,8},{4,12},{8,0},{12,4},{16,24},{20,28},{24,16},{28,20},{1,9},{5... | collective-permute-start | bytes 294920 | tf_op jit(solution)/shard_map/ppermute | solution.py:748
  15.5 1.0 %collective-permute-start.9 = (bf16[32,512]{1,0:T(8,128)(2,1)S(1)}, bf16[32,512]{1,0:T(8,128)(2,1)S(1)}, u32[]{:S(2)}, u32[]{:S(2)}) collective-permute-start(bf16[32,512]{1,0:T(8,128)(2,1)S(1)} %get-tuple-element.35), channel_id=1, source_target_pairs={{0,4},{4,0},{8,12},{12,8},{16,20},{20,16},{24,28},{28,24},{1,5},{5... | collective-permute-start | bytes 98312 | tf_op jit(solution)/shard_map/ppermute | solution.py:745
  16.5 2.1 %collective-permute-done.4.refs_4_.refs_6_ = bf16[32,1536]{1,0:T(8,128)(2,1)S(1)} collective-permute-done((bf16[32,1536]{1,0:T(8,128)(2,1)S(1)}, bf16[32,1536]{1,0:T(8,128)(2,1)S(1)}, u32[]{:S(2)}, u32[]{:S(2)}) %collective-permute-start.4) | collective-permute-done | bytes 98336 | tf_op jit(solution)/shard_map/ppermute | solution.py:748
  18.6 4.6 %collective-permute-done.5.refs_5_.refs_7_ = bf16[32,1536]{1,0:T(8,128)(2,1)S(1)} collective-permute-done((bf16[32,1536]{1,0:T(8,128)(2,1)S(1)}, bf16[32,1536]{1,0:T(8,128)(2,1)S(1)}, u32[]{:S(2)}, u32[]{:S(2)}) %collective-permute-start.5) | collective-permute-done | bytes 98336 | tf_op jit(solution)/shard_map/ppermute | solution.py:748
  23.3 0.9 %twin_attend_far.1 = (bf16[48,512]{1,0:T(8,128)(2,1)S(1)}, bf16[48,512]{1,0:T(8,128)(2,1)S(1)}, bf16[48,512]{1,0:T(8,128)(2,1)S(1)}) custom-call(s32[4,256]{1,0:T(4,128)S(1)} %get-tuple-element.25.refs_0_, bf16[4,128,512]{2,1,0:T(8,128)(2,1)S(1)} %copy-done, bf16[4,128,512]{2,1,0:T(8,128)(2,1)S(1)} %copy-done.1, ...), custom_call_target="tpu_custom_call" | custom-call | tf_op jit(solution)/shard_map/twin_attend_far/pallas_call | solution.py:731
  24.2 2.9 %collective-permute-start.7 = (bf16[48,512]{1,0:T(8,128)(2,1)S(1)}, bf16[48,512]{1,0:T(8,128)(2,1)S(1)}, u32[]{:S(2)}, u32[]{:S(2)}) collective-permute-start(bf16[48,512]{1,0:T(8,128)(2,1)S(1)} %get-tuple-element.32), channel_id=1, source_target_pairs={{0,16},{4,20},{8,24},{12,28},{16,0},{20,4},{24,8},{28,12},{1,17},{... | collective-permute-start | bytes 147464 | tf_op jit(solution)/shard_map/ppermute | solution.py:748
  27.0 1.3 %collective-permute-start.8 = (bf16[48,512]{1,0:T(8,128)(2,1)S(1)}, bf16[48,512]{1,0:T(8,128)(2,1)S(1)}, u32[]{:S(2)}, u32[]{:S(2)}) collective-permute-start(bf16[48,512]{1,0:T(8,128)(2,1)S(1)} %get-tuple-element.33.refs_9_), channel_id=1, source_target_pairs={{0,24},{4,28},{8,16},{12,20},{16,8},{20,12},{24,0},{28,4},{1,25},{... | collective-permute-start | bytes 147464 | tf_op jit(solution)/shard_map/ppermute | solution.py:748
  29.0 1.6 %collective-permute-start.10 = (bf16[48,512]{1,0:T(8,128)(2,1)S(1)}, bf16[48,512]{1,0:T(8,128)(2,1)S(1)}, u32[]{:S(2)}, u32[]{:S(2)}) collective-permute-start(bf16[48,512]{1,0:T(8,128)(2,1)S(1)} %get-tuple-element.36), channel_id=1, source_target_pairs={{0,4},{4,0},{8,12},{12,8},{16,20},{20,16},{24,28},{28,24},{1,5},{5... | collective-permute-start | bytes 147464 | tf_op jit(solution)/shard_map/ppermute | solution.py:745
  31.4 1.8 %collective-permute-done.8.refs_1_ = bf16[48,512]{1,0:T(8,128)(2,1)S(1)} collective-permute-done((bf16[48,512]{1,0:T(8,128)(2,1)S(1)}, bf16[48,512]{1,0:T(8,128)(2,1)S(1)}, u32[]{:S(2)}, u32[]{:S(2)}) %collective-permute-start.8) | collective-permute-done | bytes 49184 | tf_op jit(solution)/shard_map/ppermute | solution.py:748
  33.8 0.9 %collective-permute-done.11.refs_3_ = bf16[48,512]{1,0:T(8,128)(2,1)S(1)} collective-permute-done((bf16[48,512]{1,0:T(8,128)(2,1)S(1)}, bf16[48,512]{1,0:T(8,128)(2,1)S(1)}, u32[]{:S(2)}, u32[]{:S(2)}) %collective-permute-start.11) | collective-permute-done | bytes 49184 | tf_op jit(solution)/shard_map/ppermute | solution.py:748
  34.7 0.8 %twin_merge_and_project.1 = (f32[32,2048]{1,0:T(8,128)S(1)}, bf16[32,2048]{1,0:T(8,128)(2,1)S(1)}) custom-call(bf16[48,512]{1,0:T(8,128)(2,1)S(1)} %collective-permute-done.7.refs_0_, bf16[48,512]{1,0:T(8,128)(2,1)S(1)} %collective-permute-done.8.refs_1_, bf16[48,512]{1,0:T(8,128)(2,1)S(1)} %collective-permute-done.10.refs_2_, ...), custom_call_target="tpu_custom_call" | custom-call | tf_op jit(solution)/shard_map/twin_merge_and_project/pallas_call | solution.py:731
  35.5 1.3 %collective-permute-done.12.refs_1_ = bf16[32,2048]{1,0:T(8,128)(2,1)S(1)} collective-permute-done((bf16[32,2048]{1,0:T(8,128)(2,1)S(1)}, bf16[32,2048]{1,0:T(8,128)(2,1)S(1)}, u32[]{:S(2)}, u32[]{:S(2)}) %collective-permute-start.12) | collective-permute-done | bytes 131104 | tf_op jit(solution)/shard_map/ppermute | solution.py:742
  36.9 1.6 %collective-permute-start.13 = (bf16[32,2048]{1,0:T(8,128)(2,1)S(1)}, bf16[32,2048]{1,0:T(8,128)(2,1)S(1)}, u32[]{:S(2)}, u32[]{:S(2)}) collective-permute-start(bf16[32,2048]{1,0:T(8,128)(2,1)S(1)} %get-tuple-element.42), channel_id=1, source_target_pairs={{0,2},{1,3},{2,0},{3,1},{4,6},{5,7},{6,4},{7,5},{8,10},{9,11},{10,... | collective-permute-start | bytes 393224 | tf_op jit(solution)/shard_map/ppermute | solution.py:742
  38.5 1.4 %twin_compact.1 = (bf16[4,128,512]{2,1,0:T(8,128)(2,1)}, bf16[4,128,512]{2,1,0:T(8,128)(2,1)}) custom-call(s32[4,1,64]{2,1,0:T(1,128)S(1)} %get-tuple-element.43.refs_0_, bf16[4,128,512]{2,1,0:T(8,128)(2,1)S(1)} %copy-done, bf16[4,128,512]{2,1,0:T(8,128)(2,1)S(1)} %copy-done.1, bf16[32,1536]{1,0:T(8,128)(2,1)S(1)} %get-tuple-element.31.refs_4_.refs_3_, ...), custom_call_target="tpu_custom_call" | custom-call | tf_op jit(solution)/shard_map/twin_compact/pallas_call | solution.py:731
  39.8 2.7 %collective-permute-done.13.refs_1_ = bf16[32,2048]{1,0:T(8,128)(2,1)S(1)} collective-permute-done((bf16[32,2048]{1,0:T(8,128)(2,1)S(1)}, bf16[32,2048]{1,0:T(8,128)(2,1)S(1)}, u32[]{:S(2)}, u32[]{:S(2)}) %collective-permute-start.13) | collective-permute-done | bytes 131104 | tf_op jit(solution)/shard_map/ppermute | solution.py:742
  42.5 0.7 %twin_finish.1 = bf16[32,512]{1,0:T(8,128)(2,1)} custom-call(f32[32,2048]{1,0:T(8,128)S(1)} %get-tuple-element.41.refs_0_, bf16[32,2048]{1,0:T(8,128)(2,1)S(1)} %collective-permute-done.13.refs_1_, f32[1,512]{1,0:T(1,128)S(1)} %bitcast.13, bf16[32,2048]{1,0:T(8,128)(2,1)S(1)} %copy-done.6), custom_call_target="tpu_custom_call" | custom-call | tf_op jit(solution)/shard_map/twin_finish/pallas_call | solution.py:731
  (48 shorter events, 3.3 us)
Async XLA Ops:
  0.7 4.7 %copy-start.3 = (bf16[2048,512]{1,0:T(8,128)(2,1)S(1)}, bf16[2048,512]{1,0:T(8,128)(2,1)}, u32[]{:S(2)}) copy-start(bf16[2048,512]{1,0:T(8,128)(2,1)} %refs_1_.5) | copy-start | bytes 6291460
  0.7 4.7 %copy-start.4 = (bf16[2048,512]{1,0:T(8,128)(2,1)S(1)}, bf16[2048,512]{1,0:T(8,128)(2,1)}, u32[]{:S(2)}) copy-start(bf16[2048,512]{1,0:T(8,128)(2,1)} %refs_2_.6) | copy-start | bytes 6291460
  0.7 4.7 %copy-start.6 = (bf16[32,2048]{1,0:T(8,128)(2,1)S(1)}, bf16[32,2048]{1,0:T(8,128)(2,1)}, u32[]{:S(2)}) copy-start(bf16[32,2048]{1,0:T(8,128)(2,1)} %refs_3_.1) | copy-start | bytes 393220
  2.3 6.0 %copy-start.5 = (bf16[2048,512]{1,0:T(8,128)(2,1)S(1)}, bf16[2048,512]{1,0:T(8,128)(2,1)}, u32[]{:S(2)}) copy-start(bf16[2048,512]{1,0:T(8,128)(2,1)} %refs_1_.6) | copy-start | bytes 6291460
  2.3 20.9 %collective-permute-start = (bf16[3,2,128,512]{3,2,1,0:T(8,128)(2,1)S(1)}, bf16[3,2,128,512]{3,2,1,0:T(8,128)(2,1)S(1)}, u32[]{:S(2)}, u32[]{:S(2)}) collective-permute-start(bf16[3,2,128,512]{3,2,1,0:T(8,128)(2,1)S(1)} %pad_maximum_fusion), channel_id=1, source_target_pairs={{0,4},{4,0},{8,12},{12,8},{16,20},{20,16},{24,28},{28,24},{1,5},{5... | collective-permute-start | bytes 2359304 | tf_op jit(solution)/shard_map/ppermute | solution.py:745
  6.3 4.5 %copy-start.7 = (f32[512]{0:T(512)S(1)}, f32[512]{0:T(512)}, u32[]{:S(2)}) copy-start(f32[512]{0:T(512)} %param.18) | copy-start | bytes 6148
  6.3 16.9 %copy-start = (bf16[4,128,512]{2,1,0:T(8,128)(2,1)S(1)}, bf16[4,128,512]{2,1,0:T(8,128)(2,1)}, u32[]{:S(2)}) copy-start(bf16[4,128,512]{2,1,0:T(8,128)(2,1)} %refs_1_.9) | copy-start | bytes 1572868
  6.3 16.9 %copy-start.1 = (bf16[4,128,512]{2,1,0:T(8,128)(2,1)S(1)}, bf16[4,128,512]{2,1,0:T(8,128)(2,1)}, u32[]{:S(2)}) copy-start(bf16[4,128,512]{2,1,0:T(8,128)(2,1)} %refs_2_.9) | copy-start | bytes 1572868
  6.4 3.6 %collective-permute-start.1 = (f32[8,256]{1,0:T(8,128)S(1)}, f32[8,256]{1,0:T(8,128)S(1)}, u32[]{:S(2)}, u32[]{:S(2)}) collective-permute-start(f32[8,256]{1,0:T(8,128)S(1)} %get-tuple-element.30.refs_7_), channel_id=1, source_target_pairs={{0,3},{1,2},{2,1},{3,0},{4,7},{5,6},{6,5},{7,4},{8,11},{9,10},{10,... | collective-permute-start | bytes 24584 | tf_op jit(solution)/shard_map/ppermute | solution.py:742
  7.1 3.7 %collective-permute-start.2 = (f32[8,256]{1,0:T(8,128)S(1)}, f32[8,256]{1,0:T(8,128)S(1)}, u32[]{:S(2)}, u32[]{:S(2)}) collective-permute-start(f32[8,256]{1,0:T(8,128)S(1)} %get-tuple-element.30.refs_7_), channel_id=1, source_target_pairs={{0,2},{1,3},{2,0},{3,1},{4,6},{5,7},{6,4},{7,5},{8,10},{9,11},{10,... | collective-permute-start | bytes 24584 | tf_op jit(solution)/shard_map/ppermute | solution.py:742
  8.0 2.8 %collective-permute-start.3 = (f32[8,256]{1,0:T(8,128)S(1)}, f32[8,256]{1,0:T(8,128)S(1)}, u32[]{:S(2)}, u32[]{:S(2)}) collective-permute-start(f32[8,256]{1,0:T(8,128)S(1)} %get-tuple-element.30.refs_7_), channel_id=1, source_target_pairs={{0,1},{1,0},{2,3},{3,2},{4,5},{5,4},{6,7},{7,6},{8,9},{9,8},{10,11... | collective-permute-start | bytes 24584 | tf_op jit(solution)/shard_map/ppermute | solution.py:742
  8.7 25.9 %copy-start.2 = (bf16[512,2048]{1,0:T(8,128)(2,1)S(1)}, bf16[512,2048]{1,0:T(8,128)(2,1)}, u32[]{:S(2)}) copy-start(bf16[512,2048]{1,0:T(8,128)(2,1)} %refs_5_.1) | copy-start | bytes 6291460
  11.0 7.6 %collective-permute-start.4 = (bf16[32,1536]{1,0:T(8,128)(2,1)S(1)}, bf16[32,1536]{1,0:T(8,128)(2,1)S(1)}, u32[]{:S(2)}, u32[]{:S(2)}) collective-permute-start(bf16[32,1536]{1,0:T(8,128)(2,1)S(1)} %get-tuple-element.31.refs_4_.refs_3_), channel_id=1, source_target_pairs={{0,24},{4,28},{8,16},{12,20},{16,8},{20,12},{24,0},{28,4},{1,25},{... | collective-permute-start | bytes 294920 | tf_op jit(solution)/shard_map/ppermute | solution.py:748
  14.7 8.5 %collective-permute-start.5 = (bf16[32,1536]{1,0:T(8,128)(2,1)S(1)}, bf16[32,1536]{1,0:T(8,128)(2,1)S(1)}, u32[]{:S(2)}, u32[]{:S(2)}) collective-permute-start(bf16[32,1536]{1,0:T(8,128)(2,1)S(1)} %get-tuple-element.31.refs_4_.refs_3_), channel_id=1, source_target_pairs={{0,16},{4,20},{8,24},{12,28},{16,0},{20,4},{24,8},{28,12},{1,17},{... | collective-permute-start | bytes 294920 | tf_op jit(solution)/shard_map/ppermute | solution.py:748
  14.7 8.5 %collective-permute-start.6 = (bf16[32,1536]{1,0:T(8,128)(2,1)S(1)}, bf16[32,1536]{1,0:T(8,128)(2,1)S(1)}, u32[]{:S(2)}, u32[]{:S(2)}) collective-permute-start(bf16[32,1536]{1,0:T(8,128)(2,1)S(1)} %get-tuple-element.31.refs_4_.refs_3_), channel_id=1, source_target_pairs={{0,8},{4,12},{8,0},{12,4},{16,24},{20,28},{24,16},{28,20},{1,9},{5... | collective-permute-start | bytes 294920 | tf_op jit(solution)/shard_map/ppermute | solution.py:748
  15.5 12.9 %collective-permute-start.9 = (bf16[32,512]{1,0:T(8,128)(2,1)S(1)}, bf16[32,512]{1,0:T(8,128)(2,1)S(1)}, u32[]{:S(2)}, u32[]{:S(2)}) collective-permute-start(bf16[32,512]{1,0:T(8,128)(2,1)S(1)} %get-tuple-element.35), channel_id=1, source_target_pairs={{0,4},{4,0},{8,12},{12,8},{16,20},{20,16},{24,28},{28,24},{1,5},{5... | collective-permute-start | bytes 98312 | tf_op jit(solution)/shard_map/ppermute | solution.py:745
  24.2 7.2 %collective-permute-start.7 = (bf16[48,512]{1,0:T(8,128)(2,1)S(1)}, bf16[48,512]{1,0:T(8,128)(2,1)S(1)}, u32[]{:S(2)}, u32[]{:S(2)}) collective-permute-start(bf16[48,512]{1,0:T(8,128)(2,1)S(1)} %get-tuple-element.32), channel_id=1, source_target_pairs={{0,16},{4,20},{8,24},{12,28},{16,0},{20,4},{24,8},{28,12},{1,17},{... | collective-permute-start | bytes 147464 | tf_op jit(solution)/shard_map/ppermute | solution.py:748
  27.0 6.1 %collective-permute-start.8 = (bf16[48,512]{1,0:T(8,128)(2,1)S(1)}, bf16[48,512]{1,0:T(8,128)(2,1)S(1)}, u32[]{:S(2)}, u32[]{:S(2)}) collective-permute-start(bf16[48,512]{1,0:T(8,128)(2,1)S(1)} %get-tuple-element.33.refs_9_), channel_id=1, source_target_pairs={{0,24},{4,28},{8,16},{12,20},{16,8},{20,12},{24,0},{28,4},{1,25},{... | collective-permute-start | bytes 147464 | tf_op jit(solution)/shard_map/ppermute | solution.py:748
  29.0 4.7 %collective-permute-start.10 = (bf16[48,512]{1,0:T(8,128)(2,1)S(1)}, bf16[48,512]{1,0:T(8,128)(2,1)S(1)}, u32[]{:S(2)}, u32[]{:S(2)}) collective-permute-start(bf16[48,512]{1,0:T(8,128)(2,1)S(1)} %get-tuple-element.36), channel_id=1, source_target_pairs={{0,4},{4,0},{8,12},{12,8},{16,20},{20,16},{24,28},{28,24},{1,5},{5... | collective-permute-start | bytes 147464 | tf_op jit(solution)/shard_map/ppermute | solution.py:745
  30.6 4.1 %collective-permute-start.11 = (bf16[48,512]{1,0:T(8,128)(2,1)S(1)}, bf16[48,512]{1,0:T(8,128)(2,1)S(1)}, u32[]{:S(2)}, u32[]{:S(2)}) collective-permute-start(bf16[48,512]{1,0:T(8,128)(2,1)S(1)} %get-tuple-element.37), channel_id=1, source_target_pairs={{0,8},{4,12},{8,0},{12,4},{16,24},{20,28},{24,16},{28,20},{1,9},{5... | collective-permute-start | bytes 147464 | tf_op jit(solution)/shard_map/ppermute | solution.py:748
  30.8 7.6 %collective-permute-start.14 = (bf16[288,512]{1,0:T(8,128)(2,1)S(1)}, bf16[288,512]{1,0:T(8,128)(2,1)S(1)}, u32[]{:S(2)}, u32[]{:S(2)}) collective-permute-start(bf16[288,512]{1,0:T(8,128)(2,1)S(1)} %get-tuple-element.44), channel_id=1, source_target_pairs={{0,4},{4,0},{8,12},{12,8},{16,20},{20,16},{24,28},{28,24},{1,5},{5... | collective-permute-start | bytes 884744 | tf_op jit(solution)/shard_map/ppermute | solution.py:745
  34.7 7.8 %copy-start.9 = (f32[512]{0:T(512)S(1)}, f32[512]{0:T(512)}, u32[]{:S(2)}) copy-start(f32[512]{0:T(512)} %param.20) | copy-start | bytes 6148
  35.5 1.4 %collective-permute-start.12 = (bf16[32,2048]{1,0:T(8,128)(2,1)S(1)}, bf16[32,2048]{1,0:T(8,128)(2,1)S(1)}, u32[]{:S(2)}, u32[]{:S(2)}) collective-permute-start(bf16[32,2048]{1,0:T(8,128)(2,1)S(1)} %get-tuple-element.40), channel_id=1, source_target_pairs={{0,1},{1,0},{2,3},{3,2},{4,5},{5,4},{6,7},{7,6},{8,9},{9,8},{10,11... | collective-permute-start | bytes 393224 | tf_op jit(solution)/shard_map/ppermute | solution.py:742
  36.9 5.6 %collective-permute-start.13 = (bf16[32,2048]{1,0:T(8,128)(2,1)S(1)}, bf16[32,2048]{1,0:T(8,128)(2,1)S(1)}, u32[]{:S(2)}, u32[]{:S(2)}) collective-permute-start(bf16[32,2048]{1,0:T(8,128)(2,1)S(1)} %get-tuple-element.42), channel_id=1, source_target_pairs={{0,2},{1,3},{2,0},{3,1},{4,6},{5,7},{6,4},{7,5},{8,10},{9,11},{10,... | collective-permute-start | bytes 393224 | tf_op jit(solution)/shard_map/ppermute | solution.py:742
  (4 other events, 12.0 us)

commit v8 on v4

--- a/solution.py
+++ b/solution.py
@@ -661,19 +661,34 @@
     rounded[...] = product.astype(BF16)
 
 
+def own_half(width):
+    half = width // 2
+    return pl.ds(pl.multiple_of(lax.rem(lax.axis_index("tp"), 2) * half, half), half)
+
+
+def other_half(width):
+    half = width // 2
+    return pl.ds(pl.multiple_of((1 - lax.rem(lax.axis_index("tp"), 2)) * half, half), half)
+
+
 def twin_add(mine, theirs, total, rounded):
-    both = mine[...] + theirs[...].astype(F32)
-    total[...] = both
-    rounded[...] = both.astype(BF16)
-
-
-def twin_finish(mine, theirs, gain, hidden, out):
+    width = mine.shape[1]
+    total[...] = mine[...] + theirs[...].astype(F32)
+    lanes = own_half(width)
+    rounded[...] = (mine[:, lanes] + theirs[:, lanes].astype(F32)).astype(BF16)
+
+
+def twin_finish(mine, here, passed, gain, hidden, out, total):
     model_width = mine.shape[1]
     columns = out.shape[1]
-    total = mine[...] + theirs[...].astype(F32)
-    scale = lax.rsqrt(sum_squares(total) / model_width + EPS)
+    square = 0.0
+    for lanes, ref in ((own_half(model_width), here), (other_half(model_width), passed)):
+        both = mine[:, lanes] + ref[...].astype(F32)
+        total[:, lanes] = both
+        square = square + sum_squares(both)
+    scale = lax.rsqrt(square / model_width + EPS)
     lanes = pl.ds(pl.multiple_of(lax.axis_index("tp") * columns, columns), columns)
-    normed = (mine[:, lanes] + theirs[:, lanes].astype(F32)) * scale * gain[...]
+    normed = total[:, lanes] * scale * gain[...]
     out[...] = (hidden[:, lanes].astype(F32) + normed).astype(BF16)
 
 
@@ -820,25 +835,25 @@
         (shaped((own, model), F32), shaped((own, model), BF16)),
         (*partials, out_weight),
     )
-    bit = 1
-    while 2 * bit < tp:
-        total, rounded = call(
-            twin_add,
-            (shaped((own, model), F32), shaped((own, model), BF16)),
-            (total, over_tp(rounded, bit)),
-        )
-        bit *= 2
-    arrived = over_tp(rounded, bit)
+    total, rounded = call(
+        twin_add,
+        (shaped((own, model), F32), shaped((own, model // 2), BF16)),
+        (total, over_tp(rounded, 1)),
+    )
+    here = over_tp(rounded, 2)
     new_key_cache, new_value_cache = call(
         functools.partial(twin_compact, far),
         (shaped(key_cache.shape, BF16), shaped(value_cache.shape, BF16)),
         (targets, key_cache, value_cache, packed, *from_far, copied),
         [pltpu.VMEM((requests, 2, 2, own, width), BF16)],
     )
+    ready, new_key_cache = lax.optimization_barrier((here, new_key_cache))
+    passed = over_tp(ready, 1)
     hidden_out = call(
         twin_finish,
         shaped((own, columns), BF16),
-        (total, arrived, post_gain[None, :], hidden_in),
+        (total, here, passed, post_gain[None, :], hidden_in),
+        [pltpu.VMEM((own, model), F32)],
     )
     return (hidden_out, new_key_cache, new_value_cache)
 
@@ -857,8 +872,7 @@
         and LANES % own == 0
         and own <= width
         and 3 * (width // HEAD_DIM) <= 16
-        and tp > 1
-        and tp & (tp - 1) == 0
+        and tp == 4
     )
     return (body_twin if twin else body_general)(*args)
 

time: 43.1 us -> 44.4 us (1.030)
  waiting for transfers between devices: 14.5 us -> 16 us
    ppermute x4, waiting for transfers between devices: 0.34 us -> 3 us  [beside(): return lax.ppermute(x, 'seq', [(i, i ^ 1) for i in range(seq)])]
    ppermute x6, waiting for transfers between devices: 9.32 us -> 8.17 us  [over_planes(): lax.ppermute(x, 'seq', [(i, (i // 2 ^ turn) * 2 + i % 2) for i in range(s...]
    ppermute x6, starting transfers between devices: 9.14 us -> 8.62 us  [over_planes(): lax.ppermute(x, 'seq', [(i, (i // 2 ^ turn) * 2 + i % 2) for i in range(s...]
    ppermute x5 -> x6, waiting for transfers between devices: 4.83 us -> 4.8 us  [over_tp(): return lax.ppermute(x, 'tp', [(i, i ^ k) for i in range(tp)])]
    ppermute x5 -> x6, starting transfers between devices: 3.55 us -> 3.55 us  [over_tp(): return lax.ppermute(x, 'tp', [(i, i ^ k) for i in range(tp)])]
  transfers between devices with their start and end apart: 15 -> 16, of which waited for: 8 -> 9; matrix products, arithmetic and copies ran while one was open for 0% -> 0% of each run, Pallas kernels for 15% -> 13%
where the time goes in v8:
time: 44.4 us; the launch traced here: 44.3 us
  starting transfers between devices  18.5 us (42%)
  waiting for transfers between devices  16 us (36%)
  Pallas kernels  7.19 us (16%)
  local copies, waits for them, and re-layouts  1.51 us (3%)
  between operations  0.91 us (2%)
    ppermute x6, starting transfers between devices, over_planes(): lax.ppermute(x, 'seq', [(i, (i // 2 ^ turn) * 2 + i % 2) for i in range(s...  8.62 us
    ppermute x6, waiting for transfers between devices, over_planes(): lax.ppermute(x, 'seq', [(i, (i // 2 ^ turn) * 2 + i % 2) for i in range(s...  8.17 us
    pallas_call x10, Pallas kernels, call(): pl.pallas_call(run, out_shape=outs, in_specs=([VMEM] * count if specs is...  7.19 us
    ppermute x4, starting transfers between devices, beside(): return lax.ppermute(x, 'seq', [(i, i ^ 1) for i in range(seq)])  6.33 us
    ppermute x6, waiting for transfers between devices, over_tp(): return lax.ppermute(x, 'tp', [(i, i ^ k) for i in range(tp)])  4.8 us
    ppermute x6, starting transfers between devices, over_tp(): return lax.ppermute(x, 'tp', [(i, i ^ k) for i in range(tp)])  3.55 us
    ppermute x4, waiting for transfers between devices, beside(): return lax.ppermute(x, 'seq', [(i, i ^ 1) for i in range(seq)])  3 us
    dynamic_slice x1, local copies, waits for them, and re-layouts, picked(): lax.dynamic_index_in_dim(x, me ^ turn, 0, False)  1.43 us
  transfers between devices with their start and end apart: 16, of which 9 were waited for; matrix products, arithmetic and copies ran while one was open for 0% of the time, Pallas kernels for 13%

profile of v8, /device:TPU:0, one launch (start us, length us, event | category | flops | bytes accessed | tf_op | source)
XLA Modules:
  0.0 44.3 jit_solution(7867010859777648480)
XLA Ops:
  0.7 1.4 %constant_dynamic-slice_fusion.4 = (bf16[1,128,512]{2,1,0:T(8,128)(2,1)S(1)}, bf16[1,128,512]{2,1,0:T(8,128)(2,1)S(1)}, bf16[1,128,512]{2,1,0:T(8,128)(2,1)S(1)}...) fusion(bf16[4,128,512]{2,1,0:T(8,128)(2,1)} %refs_2_.9, ...), kind=kLoop, calls=%fused_computation.9 | loop fusion | bytes 1572876 | tf_op jit(solution)/shard_map/jit(dynamic_index_in_dim)/dynamic_slice | solution.py:769
  2.3 3.0 %collective-permute-start = (bf16[3,2,128,512]{3,2,1,0:T(8,128)(2,1)S(1)}, bf16[3,2,128,512]{3,2,1,0:T(8,128)(2,1)S(1)}, u32[]{:S(2)}, u32[]{:S(2)}) collective-permute-start(bf16[3,2,128,512]{3,2,1,0:T(8,128)(2,1)S(1)} %pad_maximum_fusion), channel_id=1, source_target_pairs={{0,4},{4,0},{8,12},{12,8},{16,20},{20,16},{24,28},{28,24},{1,5},{5... | collective-permute-start | bytes 2359304 | tf_op jit(solution)/shard_map/ppermute | solution.py:760
  5.4 0.9 %twin_project_qk.1 = (f32[32,512]{1,0:T(8,128)S(1)}, f32[32,512]{1,0:T(8,128)S(1)}, f32[8,256]{1,0:T(8,128)S(1)}) custom-call(bf16[32,2048]{1,0:T(8,128)(2,1)S(1)} %copy-done.6, bf16[2048,512]{1,0:T(8,128)(2,1)S(1)} %copy-done.3, bf16[2048,512]{1,0:T(8,128)(2,1)S(1)} %copy-done.4), custom_call_target="tpu_custom_call" | custom-call | tf_op jit(solution)/shard_map/twin_project_qk/pallas_call | solution.py:746
  6.4 0.7 %collective-permute-start.1 = (f32[8,256]{1,0:T(8,128)S(1)}, f32[8,256]{1,0:T(8,128)S(1)}, u32[]{:S(2)}, u32[]{:S(2)}) collective-permute-start(f32[8,256]{1,0:T(8,128)S(1)} %get-tuple-element.32.refs_7_), channel_id=1, source_target_pairs={{0,3},{1,2},{2,1},{3,0},{4,7},{5,6},{6,5},{7,4},{8,11},{9,10},{10,... | collective-permute-start | bytes 24584 | tf_op jit(solution)/shard_map/ppermute | solution.py:757
  7.1 0.9 %collective-permute-start.2 = (f32[8,256]{1,0:T(8,128)S(1)}, f32[8,256]{1,0:T(8,128)S(1)}, u32[]{:S(2)}, u32[]{:S(2)}) collective-permute-start(f32[8,256]{1,0:T(8,128)S(1)} %get-tuple-element.32.refs_7_), channel_id=1, source_target_pairs={{0,2},{1,3},{2,0},{3,1},{4,6},{5,7},{6,4},{7,5},{8,10},{9,11},{10,... | collective-permute-start | bytes 24584 | tf_op jit(solution)/shard_map/ppermute | solution.py:757
  8.8 1.2 %twin_tree.1 = (f32[64,32]{1,0:T(8,128)S(1)}, s32[4,1,64]{2,1,0:T(1,128)S(1)}, f32[32,128]{1,0:T(8,128)S(1)}, f32[32,128]{1,0:T(8,128)S(1)}, s32[4,256]{1,0:T(4,128)S(1)}) custom-call(s32[1,4]{1,0:T(1,128)S(1)} %bitcast.14, s32[1,4]{1,0:T(1,128)S(1)} %bitcast.15, s32[4,64]{1,0:T(4,128)S(1)} %copy-done.10, f32[1,128]{1,0:T(1,128)S(1)} %fusion.2.refs_3_), custom_call_target="tpu_custom_call" | custom-call | tf_op jit(solution)/shard_map/twin_tree/pallas_call | solution.py:746
  10.0 0.8 %collective-permute-done.2.refs_9_ = f32[8,256]{1,0:T(8,128)S(1)} collective-permute-done((f32[8,256]{1,0:T(8,128)S(1)}, f32[8,256]{1,0:T(8,128)S(1)}, u32[]{:S(2)}, u32[]{:S(2)}) %collective-permute-start.2) | collective-permute-done | bytes 8224 | tf_op jit(solution)/shard_map/ppermute | solution.py:757
  11.0 3.7 %collective-permute-start.4 = (bf16[32,1536]{1,0:T(8,128)(2,1)S(1)}, bf16[32,1536]{1,0:T(8,128)(2,1)S(1)}, u32[]{:S(2)}, u32[]{:S(2)}) collective-permute-start(bf16[32,1536]{1,0:T(8,128)(2,1)S(1)} %get-tuple-element.33.refs_4_.refs_3_), channel_id=1, source_target_pairs={{0,24},{4,28},{8,16},{12,20},{16,8},{20,12},{24,0},{28,4},{1,25},{... | collective-permute-start | bytes 294920 | tf_op jit(solution)/shard_map/ppermute | solution.py:763
  14.7 0.8 %collective-permute-start.6 = (bf16[32,1536]{1,0:T(8,128)(2,1)S(1)}, bf16[32,1536]{1,0:T(8,128)(2,1)S(1)}, u32[]{:S(2)}, u32[]{:S(2)}) collective-permute-start(bf16[32,1536]{1,0:T(8,128)(2,1)S(1)} %get-tuple-element.33.refs_4_.refs_3_), channel_id=1, source_target_pairs={{0,8},{4,12},{8,0},{12,4},{16,24},{20,28},{24,16},{28,20},{1,9},{5... | collective-permute-start | bytes 294920 | tf_op jit(solution)/shard_map/ppermute | solution.py:763
  15.5 1.0 %collective-permute-start.9 = (bf16[32,512]{1,0:T(8,128)(2,1)S(1)}, bf16[32,512]{1,0:T(8,128)(2,1)S(1)}, u32[]{:S(2)}, u32[]{:S(2)}) collective-permute-start(bf16[32,512]{1,0:T(8,128)(2,1)S(1)} %get-tuple-element.37), channel_id=1, source_target_pairs={{0,4},{4,0},{8,12},{12,8},{16,20},{20,16},{24,28},{28,24},{1,5},{5... | collective-permute-start | bytes 98312 | tf_op jit(solution)/shard_map/ppermute | solution.py:760
  16.5 2.1 %collective-permute-done.4.refs_4_.refs_6_ = bf16[32,1536]{1,0:T(8,128)(2,1)S(1)} collective-permute-done((bf16[32,1536]{1,0:T(8,128)(2,1)S(1)}, bf16[32,1536]{1,0:T(8,128)(2,1)S(1)}, u32[]{:S(2)}, u32[]{:S(2)}) %collective-permute-start.4) | collective-permute-done | bytes 98336 | tf_op jit(solution)/shard_map/ppermute | solution.py:763
  18.6 4.6 %collective-permute-done.5.refs_5_.refs_7_ = bf16[32,1536]{1,0:T(8,128)(2,1)S(1)} collective-permute-done((bf16[32,1536]{1,0:T(8,128)(2,1)S(1)}, bf16[32,1536]{1,0:T(8,128)(2,1)S(1)}, u32[]{:S(2)}, u32[]{:S(2)}) %collective-permute-start.5) | collective-permute-done | bytes 98336 | tf_op jit(solution)/shard_map/ppermute | solution.py:763
  23.3 0.9 %twin_attend_far.1 = (bf16[48,512]{1,0:T(8,128)(2,1)S(1)}, bf16[48,512]{1,0:T(8,128)(2,1)S(1)}, bf16[48,512]{1,0:T(8,128)(2,1)S(1)}) custom-call(s32[4,256]{1,0:T(4,128)S(1)} %get-tuple-element.27.refs_0_, bf16[4,128,512]{2,1,0:T(8,128)(2,1)S(1)} %copy-done, bf16[4,128,512]{2,1,0:T(8,128)(2,1)S(1)} %copy-done.1, ...), custom_call_target="tpu_custom_call" | custom-call | tf_op jit(solution)/shard_map/twin_attend_far/pallas_call | solution.py:746
  24.8 1.8 %collective-permute-start.14 = (bf16[288,512]{1,0:T(8,128)(2,1)S(1)}, bf16[288,512]{1,0:T(8,128)(2,1)S(1)}, u32[]{:S(2)}, u32[]{:S(2)}) collective-permute-start(bf16[288,512]{1,0:T(8,128)(2,1)S(1)} %get-tuple-element.46), channel_id=1, source_target_pairs={{0,4},{4,0},{8,12},{12,8},{16,20},{20,16},{24,28},{28,24},{1,5},{5... | collective-permute-start | bytes 884744 | tf_op jit(solution)/shard_map/ppermute | solution.py:760
  26.6 3.6 %collective-permute-start.7 = (bf16[48,512]{1,0:T(8,128)(2,1)S(1)}, bf16[48,512]{1,0:T(8,128)(2,1)S(1)}, u32[]{:S(2)}, u32[]{:S(2)}) collective-permute-start(bf16[48,512]{1,0:T(8,128)(2,1)S(1)} %get-tuple-element.34.refs_9_), channel_id=1, source_target_pairs={{0,24},{4,28},{8,16},{12,20},{16,8},{20,12},{24,0},{28,4},{1,25},{... | collective-permute-start | bytes 147464 | tf_op jit(solution)/shard_map/ppermute | solution.py:763
  31.3 3.0 %collective-permute-done.10.refs_2_ = bf16[48,512]{1,0:T(8,128)(2,1)S(1)} collective-permute-done((bf16[48,512]{1,0:T(8,128)(2,1)S(1)}, bf16[48,512]{1,0:T(8,128)(2,1)S(1)}, u32[]{:S(2)}, u32[]{:S(2)}) %collective-permute-start.10) | collective-permute-done | bytes 49184 | tf_op jit(solution)/shard_map/ppermute | solution.py:760
  34.8 0.9 %collective-permute-done.8.refs_1_ = bf16[48,512]{1,0:T(8,128)(2,1)S(1)} collective-permute-done((bf16[48,512]{1,0:T(8,128)(2,1)S(1)}, bf16[48,512]{1,0:T(8,128)(2,1)S(1)}, u32[]{:S(2)}, u32[]{:S(2)}) %collective-permute-start.8) | collective-permute-done | bytes 49184 | tf_op jit(solution)/shard_map/ppermute | solution.py:763
  35.7 0.8 %twin_merge_and_project.1 = (f32[32,2048]{1,0:T(8,128)S(1)}, bf16[32,2048]{1,0:T(8,128)(2,1)S(1)}) custom-call(bf16[48,512]{1,0:T(8,128)(2,1)S(1)} %collective-permute-done.7.refs_0_, bf16[48,512]{1,0:T(8,128)(2,1)S(1)} %collective-permute-done.8.refs_1_, bf16[48,512]{1,0:T(8,128)(2,1)S(1)} %collective-permute-done.10.refs_2_, ...), custom_call_target="tpu_custom_call" | custom-call | tf_op jit(solution)/shard_map/twin_merge_and_project/pallas_call | solution.py:746
  36.6 1.3 %collective-permute-done.12.refs_1_ = bf16[32,2048]{1,0:T(8,128)(2,1)S(1)} collective-permute-done((bf16[32,2048]{1,0:T(8,128)(2,1)S(1)}, bf16[32,2048]{1,0:T(8,128)(2,1)S(1)}, u32[]{:S(2)}, u32[]{:S(2)}) %collective-permute-start.12) | collective-permute-done | bytes 131104 | tf_op jit(solution)/shard_map/ppermute | solution.py:757
  37.9 1.6 %collective-permute-start.13 = (bf16[32,1024]{1,0:T(8,128)(2,1)S(1)}, bf16[32,1024]{1,0:T(8,128)(2,1)S(1)}, u32[]{:S(2)}, u32[]{:S(2)}) collective-permute-start(bf16[32,1024]{1,0:T(8,128)(2,1)S(1)} %get-tuple-element.44), channel_id=1, source_target_pairs={{0,2},{1,3},{2,0},{3,1},{4,6},{5,7},{6,4},{7,5},{8,10},{9,11},{10,... | collective-permute-start | bytes 196616 | tf_op jit(solution)/shard_map/ppermute | solution.py:757
  39.5 1.4 %twin_compact.1 = (bf16[4,128,512]{2,1,0:T(8,128)(2,1)}, bf16[4,128,512]{2,1,0:T(8,128)(2,1)}) custom-call(s32[4,1,64]{2,1,0:T(1,128)S(1)} %get-tuple-element.45.refs_0_, bf16[4,128,512]{2,1,0:T(8,128)(2,1)S(1)} %copy-done, bf16[4,128,512]{2,1,0:T(8,128)(2,1)S(1)} %copy-done.1, bf16[32,1536]{1,0:T(8,128)(2,1)S(1)} %get-tuple-element.33.refs_4_.refs_3_, ...), custom_call_target="tpu_custom_call" | custom-call | tf_op jit(solution)/shard_map/twin_compact/pallas_call | solution.py:746
  40.9 1.4 %collective-permute-done.13.refs_1_ = bf16[32,1024]{1,0:T(8,128)(2,1)S(1)} collective-permute-done((bf16[32,1024]{1,0:T(8,128)(2,1)S(1)}, bf16[32,1024]{1,0:T(8,128)(2,1)S(1)}, u32[]{:S(2)}, u32[]{:S(2)}) %collective-permute-start.13) | collective-permute-done | bytes 65568 | tf_op jit(solution)/shard_map/ppermute | solution.py:757
  42.3 1.3 %collective-permute-done.15.refs_2_ = bf16[32,1024]{1,0:T(8,128)(2,1)S(1)} collective-permute-done((bf16[32,1024]{1,0:T(8,128)(2,1)S(1)}, bf16[32,1024]{1,0:T(8,128)(2,1)S(1)}, u32[]{:S(2)}, u32[]{:S(2)}) %collective-permute-start.15) | collective-permute-done | bytes 65568 | tf_op jit(solution)/shard_map/ppermute | solution.py:757
  43.5 0.7 %twin_finish.1 = bf16[32,512]{1,0:T(8,128)(2,1)} custom-call(f32[32,2048]{1,0:T(8,128)S(1)} %get-tuple-element.43.refs_0_, bf16[32,1024]{1,0:T(8,128)(2,1)S(1)} %collective-permute-done.13.refs_1_, bf16[32,1024]{1,0:T(8,128)(2,1)S(1)} %collective-permute-done.15.refs_2_, f32[1,512]{1,0:T(1,128)S(1)} %bitcast.13, bf16[32,2048]{1,0:T(8,128)(2,1)S(1)} %copy-done.6), custom_call_target="tpu_custom_call" | custom-call | tf_op jit(solution)/shard_map/twin_finish/pallas_call | solution.py:746
  (50 shorter events, 3.5 us)
Async XLA Ops:
  0.7 4.7 %copy-start.3 = (bf16[2048,512]{1,0:T(8,128)(2,1)S(1)}, bf16[2048,512]{1,0:T(8,128)(2,1)}, u32[]{:S(2)}) copy-start(bf16[2048,512]{1,0:T(8,128)(2,1)} %refs_1_.5) | copy-start | bytes 6291460
  0.7 4.7 %copy-start.4 = (bf16[2048,512]{1,0:T(8,128)(2,1)S(1)}, bf16[2048,512]{1,0:T(8,128)(2,1)}, u32[]{:S(2)}) copy-start(bf16[2048,512]{1,0:T(8,128)(2,1)} %refs_2_.6) | copy-start | bytes 6291460
  0.7 4.7 %copy-start.6 = (bf16[32,2048]{1,0:T(8,128)(2,1)S(1)}, bf16[32,2048]{1,0:T(8,128)(2,1)}, u32[]{:S(2)}) copy-start(bf16[32,2048]{1,0:T(8,128)(2,1)} %refs_4_.1) | copy-start | bytes 393220
  2.3 6.0 %copy-start.5 = (bf16[2048,512]{1,0:T(8,128)(2,1)S(1)}, bf16[2048,512]{1,0:T(8,128)(2,1)}, u32[]{:S(2)}) copy-start(bf16[2048,512]{1,0:T(8,128)(2,1)} %refs_1_.6) | copy-start | bytes 6291460
  2.3 20.9 %collective-permute-start = (bf16[3,2,128,512]{3,2,1,0:T(8,128)(2,1)S(1)}, bf16[3,2,128,512]{3,2,1,0:T(8,128)(2,1)S(1)}, u32[]{:S(2)}, u32[]{:S(2)}) collective-permute-start(bf16[3,2,128,512]{3,2,1,0:T(8,128)(2,1)S(1)} %pad_maximum_fusion), channel_id=1, source_target_pairs={{0,4},{4,0},{8,12},{12,8},{16,20},{20,16},{24,28},{28,24},{1,5},{5... | collective-permute-start | bytes 2359304 | tf_op jit(solution)/shard_map/ppermute | solution.py:760
  6.3 16.9 %copy-start = (bf16[4,128,512]{2,1,0:T(8,128)(2,1)S(1)}, bf16[4,128,512]{2,1,0:T(8,128)(2,1)}, u32[]{:S(2)}) copy-start(bf16[4,128,512]{2,1,0:T(8,128)(2,1)} %refs_1_.9) | copy-start | bytes 1572868
  6.3 16.9 %copy-start.1 = (bf16[4,128,512]{2,1,0:T(8,128)(2,1)S(1)}, bf16[4,128,512]{2,1,0:T(8,128)(2,1)}, u32[]{:S(2)}) copy-start(bf16[4,128,512]{2,1,0:T(8,128)(2,1)} %refs_2_.9) | copy-start | bytes 1572868
  6.4 3.6 %collective-permute-start.1 = (f32[8,256]{1,0:T(8,128)S(1)}, f32[8,256]{1,0:T(8,128)S(1)}, u32[]{:S(2)}, u32[]{:S(2)}) collective-permute-start(f32[8,256]{1,0:T(8,128)S(1)} %get-tuple-element.32.refs_7_), channel_id=1, source_target_pairs={{0,3},{1,2},{2,1},{3,0},{4,7},{5,6},{6,5},{7,4},{8,11},{9,10},{10,... | collective-permute-start | bytes 24584 | tf_op jit(solution)/shard_map/ppermute | solution.py:757
  7.1 3.7 %collective-permute-start.2 = (f32[8,256]{1,0:T(8,128)S(1)}, f32[8,256]{1,0:T(8,128)S(1)}, u32[]{:S(2)}, u32[]{:S(2)}) collective-permute-start(f32[8,256]{1,0:T(8,128)S(1)} %get-tuple-element.32.refs_7_), channel_id=1, source_target_pairs={{0,2},{1,3},{2,0},{3,1},{4,6},{5,7},{6,4},{7,5},{8,10},{9,11},{10,... | collective-permute-start | bytes 24584 | tf_op jit(solution)/shard_map/ppermute | solution.py:757
  8.0 2.8 %collective-permute-start.3 = (f32[8,256]{1,0:T(8,128)S(1)}, f32[8,256]{1,0:T(8,128)S(1)}, u32[]{:S(2)}, u32[]{:S(2)}) collective-permute-start(f32[8,256]{1,0:T(8,128)S(1)} %get-tuple-element.32.refs_7_), channel_id=1, source_target_pairs={{0,1},{1,0},{2,3},{3,2},{4,5},{5,4},{6,7},{7,6},{8,9},{9,8},{10,11... | collective-permute-start | bytes 24584 | tf_op jit(solution)/shard_map/ppermute | solution.py:757
  8.7 27.0 %copy-start.2 = (bf16[512,2048]{1,0:T(8,128)(2,1)S(1)}, bf16[512,2048]{1,0:T(8,128)(2,1)}, u32[]{:S(2)}) copy-start(bf16[512,2048]{1,0:T(8,128)(2,1)} %refs_5_.1) | copy-start | bytes 6291460
  11.0 7.6 %collective-permute-start.4 = (bf16[32,1536]{1,0:T(8,128)(2,1)S(1)}, bf16[32,1536]{1,0:T(8,128)(2,1)S(1)}, u32[]{:S(2)}, u32[]{:S(2)}) collective-permute-start(bf16[32,1536]{1,0:T(8,128)(2,1)S(1)} %get-tuple-element.33.refs_4_.refs_3_), channel_id=1, source_target_pairs={{0,24},{4,28},{8,16},{12,20},{16,8},{20,12},{24,0},{28,4},{1,25},{... | collective-permute-start | bytes 294920 | tf_op jit(solution)/shard_map/ppermute | solution.py:763
  14.7 8.5 %collective-permute-start.5 = (bf16[32,1536]{1,0:T(8,128)(2,1)S(1)}, bf16[32,1536]{1,0:T(8,128)(2,1)S(1)}, u32[]{:S(2)}, u32[]{:S(2)}) collective-permute-start(bf16[32,1536]{1,0:T(8,128)(2,1)S(1)} %get-tuple-element.33.refs_4_.refs_3_), channel_id=1, source_target_pairs={{0,16},{4,20},{8,24},{12,28},{16,0},{20,4},{24,8},{28,12},{1,17},{... | collective-permute-start | bytes 294920 | tf_op jit(solution)/shard_map/ppermute | solution.py:763
  14.7 8.5 %collective-permute-start.6 = (bf16[32,1536]{1,0:T(8,128)(2,1)S(1)}, bf16[32,1536]{1,0:T(8,128)(2,1)S(1)}, u32[]{:S(2)}, u32[]{:S(2)}) collective-permute-start(bf16[32,1536]{1,0:T(8,128)(2,1)S(1)} %get-tuple-element.33.refs_4_.refs_3_), channel_id=1, source_target_pairs={{0,8},{4,12},{8,0},{12,4},{16,24},{20,28},{24,16},{28,20},{1,9},{5... | collective-permute-start | bytes 294920 | tf_op jit(solution)/shard_map/ppermute | solution.py:763
  15.5 8.7 %collective-permute-start.9 = (bf16[32,512]{1,0:T(8,128)(2,1)S(1)}, bf16[32,512]{1,0:T(8,128)(2,1)S(1)}, u32[]{:S(2)}, u32[]{:S(2)}) collective-permute-start(bf16[32,512]{1,0:T(8,128)(2,1)S(1)} %get-tuple-element.37), channel_id=1, source_target_pairs={{0,4},{4,0},{8,12},{12,8},{16,20},{20,16},{24,28},{28,24},{1,5},{5... | collective-permute-start | bytes 98312 | tf_op jit(solution)/shard_map/ppermute | solution.py:760
  24.8 14.7 %collective-permute-start.14 = (bf16[288,512]{1,0:T(8,128)(2,1)S(1)}, bf16[288,512]{1,0:T(8,128)(2,1)S(1)}, u32[]{:S(2)}, u32[]{:S(2)}) collective-permute-start(bf16[288,512]{1,0:T(8,128)(2,1)S(1)} %get-tuple-element.46), channel_id=1, source_target_pairs={{0,4},{4,0},{8,12},{12,8},{16,20},{20,16},{24,28},{28,24},{1,5},{5... | collective-permute-start | bytes 884744 | tf_op jit(solution)/shard_map/ppermute | solution.py:760
  26.6 8.2 %collective-permute-start.7 = (bf16[48,512]{1,0:T(8,128)(2,1)S(1)}, bf16[48,512]{1,0:T(8,128)(2,1)S(1)}, u32[]{:S(2)}, u32[]{:S(2)}) collective-permute-start(bf16[48,512]{1,0:T(8,128)(2,1)S(1)} %get-tuple-element.34.refs_9_), channel_id=1, source_target_pairs={{0,24},{4,28},{8,16},{12,20},{16,8},{20,12},{24,0},{28,4},{1,25},{... | collective-permute-start | bytes 147464 | tf_op jit(solution)/shard_map/ppermute | solution.py:763
  30.2 4.1 %collective-permute-start.10 = (bf16[48,512]{1,0:T(8,128)(2,1)S(1)}, bf16[48,512]{1,0:T(8,128)(2,1)S(1)}, u32[]{:S(2)}, u32[]{:S(2)}) collective-permute-start(bf16[48,512]{1,0:T(8,128)(2,1)S(1)} %get-tuple-element.38), channel_id=1, source_target_pairs={{0,4},{4,0},{8,12},{12,8},{16,20},{20,16},{24,28},{28,24},{1,5},{5... | collective-permute-start | bytes 147464 | tf_op jit(solution)/shard_map/ppermute | solution.py:760
  30.7 4.1 %collective-permute-start.11 = (bf16[48,512]{1,0:T(8,128)(2,1)S(1)}, bf16[48,512]{1,0:T(8,128)(2,1)S(1)}, u32[]{:S(2)}, u32[]{:S(2)}) collective-permute-start(bf16[48,512]{1,0:T(8,128)(2,1)S(1)} %get-tuple-element.39), channel_id=1, source_target_pairs={{0,8},{4,12},{8,0},{12,4},{16,24},{20,28},{24,16},{28,20},{1,9},{5... | collective-permute-start | bytes 147464 | tf_op jit(solution)/shard_map/ppermute | solution.py:763
  30.7 5.0 %collective-permute-start.8 = (bf16[48,512]{1,0:T(8,128)(2,1)S(1)}, bf16[48,512]{1,0:T(8,128)(2,1)S(1)}, u32[]{:S(2)}, u32[]{:S(2)}) collective-permute-start(bf16[48,512]{1,0:T(8,128)(2,1)S(1)} %get-tuple-element.35), channel_id=1, source_target_pairs={{0,16},{4,20},{8,24},{12,28},{16,0},{20,4},{24,8},{28,12},{1,17},{... | collective-permute-start | bytes 147464 | tf_op jit(solution)/shard_map/ppermute | solution.py:763
  35.7 7.8 %copy-start.9 = (f32[512]{0:T(512)S(1)}, f32[512]{0:T(512)}, u32[]{:S(2)}) copy-start(f32[512]{0:T(512)} %param.20) | copy-start | bytes 6148
  36.5 1.4 %collective-permute-start.12 = (bf16[32,2048]{1,0:T(8,128)(2,1)S(1)}, bf16[32,2048]{1,0:T(8,128)(2,1)S(1)}, u32[]{:S(2)}, u32[]{:S(2)}) collective-permute-start(bf16[32,2048]{1,0:T(8,128)(2,1)S(1)} %get-tuple-element.42), channel_id=1, source_target_pairs={{0,1},{1,0},{2,3},{3,2},{4,5},{5,4},{6,7},{7,6},{8,9},{9,8},{10,11... | collective-permute-start | bytes 393224 | tf_op jit(solution)/shard_map/ppermute | solution.py:757
  37.9 4.3 %collective-permute-start.13 = (bf16[32,1024]{1,0:T(8,128)(2,1)S(1)}, bf16[32,1024]{1,0:T(8,128)(2,1)S(1)}, u32[]{:S(2)}, u32[]{:S(2)}) collective-permute-start(bf16[32,1024]{1,0:T(8,128)(2,1)S(1)} %get-tuple-element.44), channel_id=1, source_target_pairs={{0,2},{1,3},{2,0},{3,1},{4,6},{5,7},{6,4},{7,5},{8,10},{9,11},{10,... | collective-permute-start | bytes 196616 | tf_op jit(solution)/shard_map/ppermute | solution.py:757
  42.3 1.3 %collective-permute-start.15 = (bf16[32,1024]{1,0:T(8,128)(2,1)S(1)}, bf16[32,1024]{1,0:T(8,128)(2,1)S(1)}, u32[]{:S(2)}, u32[]{:S(2)}) collective-permute-start(bf16[32,1024]{1,0:T(8,128)(2,1)S(1)} %collective-permute-done.13.refs_1_), channel_id=1, source_target_pairs={{0,1},{1,0},{2,3},{3,2},{4,5},{5,4},{6,7},{7,6},{8,9},{9,8},{10,11... | collective-permute-start | bytes 196616 | tf_op jit(solution)/shard_map/ppermute | solution.py:757
  (5 other events, 16.5 us)

commit v9 on v4

--- a/solution.py
+++ b/solution.py
@@ -533,9 +533,9 @@
     packed[:, 2 * width :] = value[...]
 
 
-def weigh(s, visible):
+def weigh(s):
     peak = jnp.max(s, axis=1, keepdims=True).astype(BF16).astype(F32)
-    weights = jnp.exp(jnp.where(visible, s - peak, NEG))
+    weights = jnp.exp(s - jnp.maximum(peak, 0.1 * NEG))
     total = jnp.sum(weights, axis=1, keepdims=True)
     high = total.astype(BF16).astype(F32)
     return weights.astype(BF16), (peak, high, total - high)
@@ -573,16 +573,16 @@
             lanes = slice(h * HEAD_DIM, (h + 1) * HEAD_DIM)
             q = queries[at][:, lanes]
             first = dot_t(q, key_cache[plane() ^ turn, :, lanes])
-            second = dot_t(q, swapped[at, 0, :, lanes])
+            second = dot_t(q, swapped[2 * at, :, lanes])
             product = jnp.concatenate([first, second], axis=1) * factor
             scores[at, h] = jnp.where(visible[at], product, NEG)
     for at, turn in enumerate(turns):
         stats = jnp.zeros((own, LANES), F32)
         for h in range(heads):
             lanes = slice(h * HEAD_DIM, (h + 1) * HEAD_DIM)
-            weights, found = weigh(scores[at, h], visible[at])
+            weights, found = weigh(scores[at, h])
             out = dot(weights[:, :block], value_cache[plane() ^ turn, :, lanes])
-            out = out + dot(weights[:, block:], swapped[at, 1, :, lanes])
+            out = out + dot(weights[:, block:], swapped[2 * at + 1, :, lanes])
             outs[at][:own, lanes] = out.astype(BF16)
             stats = kept(stats, h, heads, found)
         write_stats(stats, outs[at])
@@ -614,7 +614,7 @@
     stats = jnp.zeros((2 * own, LANES), F32)
     for h in range(heads):
         lanes = slice(h * HEAD_DIM, (h + 1) * HEAD_DIM)
-        weights, found = weigh(own_scores[h], near)
+        weights, found = weigh(own_scores[h])
         out = dot(weights[:, :block], value_cache[plane(), :, lanes])
         values = mine[:, 2 * width + h * HEAD_DIM : 2 * width + (h + 1) * HEAD_DIM]
         out = out + dot(weights[:, block : block + own], values)
@@ -750,11 +750,13 @@
     me = lax.axis_index("seq") // 2
 
     def picked(turns):
-        parts = [
-            [lax.dynamic_index_in_dim(x, me ^ turn, 0, False) for x in (key_cache, value_cache)]
-            for turn in turns
-        ]
-        return jnp.stack([jnp.stack(part) for part in parts])
+        return jnp.stack(
+            [
+                lax.dynamic_index_in_dim(x, me ^ turn, 0, False)
+                for turn in turns
+                for x in (key_cache, value_cache)
+            ]
+        )
 
     swapped = beside(picked(far))
     query_raw, key_raw, squares = call(

time: 43.1 us -> 49 us (1.14)
  local copies, waits for them, and re-layouts: 1.51 us -> 9.67 us
  starting transfers between devices: 18.6 us -> 17.2 us
  waiting for transfers between devices: 14.5 us -> 13.8 us
    unnamed x26 -> x33, local copies, waits for them, and re-layouts: 0.08 us -> 8.75 us
    ppermute x4, waiting for transfers between devices: 0.34 us -> 2.54 us  [beside(): return lax.ppermute(x, 'seq', [(i, i ^ 1) for i in range(seq)])]
    ppermute x6, waiting for transfers between devices: 9.32 us -> 7.86 us  [over_planes(): lax.ppermute(x, 'seq', [(i, (i // 2 ^ turn) * 2 + i % 2) for i in range(s...]
    ppermute x5, waiting for transfers between devices: 4.83 us -> 3.39 us  [over_tp(): return lax.ppermute(x, 'tp', [(i, i ^ k) for i in range(tp)])]
    dynamic_slice x1 -> x0, local copies, waits for them, and re-layouts: 1.43 us -> none  [picked(): lax.dynamic_index_in_dim(x, me ^ turn, 0, False)]
    another operation x0 -> x1, local copies, waits for them, and re-layouts: none -> 0.92 us  [picked(): jnp.stack([lax.dynamic_index_in_dim(x, me ^ turn, 0, False) for turn in t...]
    ppermute x5, starting transfers between devices: 3.55 us -> 2.69 us  [over_tp(): return lax.ppermute(x, 'tp', [(i, i ^ k) for i in range(tp)])]
  transfers between devices with their start and end apart: 15 -> 15, of which waited for: 8 -> 9; matrix products, arithmetic and copies ran while one was open for 0% -> 0% of each run, Pallas kernels for 15% -> 13%
where the time goes in v9:
time: 49 us; the launch traced here: 48.7 us
  starting transfers between devices  17.2 us (35%)
  waiting for transfers between devices  13.8 us (28%)
  local copies, waits for them, and re-layouts  9.67 us (20%)
  Pallas kernels  7.18 us (15%)
  between operations  0.86 us (2%)
    ppermute x6, starting transfers between devices, over_planes(): lax.ppermute(x, 'seq', [(i, (i // 2 ^ turn) * 2 + i % 2) for i in range(s...  8.9 us
    unnamed x33, local copies, waits for them, and re-layouts  8.75 us
    ppermute x6, waiting for transfers between devices, over_planes(): lax.ppermute(x, 'seq', [(i, (i // 2 ^ turn) * 2 + i % 2) for i in range(s...  7.86 us
    pallas_call x10, Pallas kernels, call(): pl.pallas_call(run, out_shape=outs, in_specs=([VMEM] * count if specs is...  7.18 us
    ppermute x4, starting transfers between devices, beside(): return lax.ppermute(x, 'seq', [(i, i ^ 1) for i in range(seq)])  5.63 us
    ppermute x5, waiting for transfers between devices, over_tp(): return lax.ppermute(x, 'tp', [(i, i ^ k) for i in range(tp)])  3.39 us
    ppermute x5, starting transfers between devices, over_tp(): return lax.ppermute(x, 'tp', [(i, i ^ k) for i in range(tp)])  2.69 us
    ppermute x4, waiting for transfers between devices, beside(): return lax.ppermute(x, 'seq', [(i, i ^ 1) for i in range(seq)])  2.54 us
  transfers between devices with their start and end apart: 15, of which 9 were waited for; matrix products, arithmetic and copies ran while one was open for 0% of the time, Pallas kernels for 13%

profile of v9, /device:TPU:0, one launch (start us, length us, event | category | flops | bytes accessed | tf_op | source)
XLA Modules:
  0.0 48.7 jit_solution(12277905362352929591)
XLA Ops:
  0.7 0.9 %dynamic-slice_dynamic-update-slice_fusion.5 = bf16[6,128,512]{2,1,0:T(8,128)(2,1)S(1)} fusion(bf16[4,128,512]{2,1,0:T(8,128)(2,1)} %refs_1_.9, s32[]{:T(128)S(6)} %select_n.33), kind=kLoop, calls=%fused_computation.5 | loop fusion | bytes 262148
  1.6 0.9 %dynamic-slice_dynamic-update-slice_fusion.4 = bf16[6,128,512]{2,1,0:T(8,128)(2,1)S(1)} fusion(bf16[6,128,512]{2,1,0:T(8,128)(2,1)S(1)} %dynamic-slice_dynamic-update-slice_fusion.5, bf16[4,128,512]{2,1,0:T(8,128)(2,1)} %refs_2_.9, s32[]{:T(128)S(6)} %select_n.33), kind=kLoop, calls=%fused_computation.4 | loop fusion | bytes 262148
  2.5 0.9 %dynamic-slice_dynamic-update-slice_fusion.3 = bf16[6,128,512]{2,1,0:T(8,128)(2,1)S(1)} fusion(bf16[6,128,512]{2,1,0:T(8,128)(2,1)S(1)} %dynamic-slice_dynamic-update-slice_fusion.4, bf16[4,128,512]{2,1,0:T(8,128)(2,1)} %refs_1_.9, s32[]{:T(128)S(6)} %select_n.34), kind=kLoop, calls=%fused_computation.3 | loop fusion | bytes 262148
  3.4 0.9 %dynamic-slice_dynamic-update-slice_fusion.2 = bf16[6,128,512]{2,1,0:T(8,128)(2,1)S(1)} fusion(bf16[6,128,512]{2,1,0:T(8,128)(2,1)S(1)} %dynamic-slice_dynamic-update-slice_fusion.3, bf16[4,128,512]{2,1,0:T(8,128)(2,1)} %refs_2_.9, s32[]{:T(128)S(6)} %select_n.34), kind=kLoop, calls=%fused_computation.2 | loop fusion | bytes 262148
  4.4 0.9 %dynamic-slice_dynamic-update-slice_fusion.1 = bf16[6,128,512]{2,1,0:T(8,128)(2,1)S(1)} fusion(bf16[6,128,512]{2,1,0:T(8,128)(2,1)S(1)} %dynamic-slice_dynamic-update-slice_fusion.2, bf16[4,128,512]{2,1,0:T(8,128)(2,1)} %refs_1_.9, s32[]{:T(128)S(6)} %select_n.35), kind=kLoop, calls=%fused_computation.1 | loop fusion | bytes 262148
  5.3 0.9 %dynamic-slice_dynamic-update-slice_fusion = bf16[6,128,512]{2,1,0:T(8,128)(2,1)S(1)} fusion(bf16[6,128,512]{2,1,0:T(8,128)(2,1)S(1)} %dynamic-slice_dynamic-update-slice_fusion.1, bf16[4,128,512]{2,1,0:T(8,128)(2,1)} %refs_2_.9, s32[]{:T(128)S(6)} %select_n.35), kind=kLoop, calls=%fused_computation | loop fusion | bytes 262148 | tf_op jit(solution)/shard_map/stack | solution.py:753
  6.2 3.0 %collective-permute-start = (bf16[6,128,512]{2,1,0:T(8,128)(2,1)S(1)}, bf16[6,128,512]{2,1,0:T(8,128)(2,1)S(1)}, u32[]{:S(2)}, u32[]{:S(2)}) collective-permute-start(bf16[6,128,512]{2,1,0:T(8,128)(2,1)S(1)} %dynamic-slice_dynamic-update-slice_fusion), channel_id=1, source_target_pairs={{0,4},{4,0},{8,12},{12,8},{16,20},{20,16},{24,28},{28,24},{1,5},{5... | collective-permute-start | bytes 2359304 | tf_op jit(solution)/shard_map/ppermute | solution.py:745
  9.2 1.6 %copy-done.3 = bf16[2048,512]{1,0:T(8,128)(2,1)S(1)} copy-done((bf16[2048,512]{1,0:T(8,128)(2,1)S(1)}, bf16[2048,512]{1,0:T(8,128)(2,1)}, u32[]{:S(2)}) %copy-start.3) | copy-done | bytes 2097176
  10.8 1.6 %copy-done.4 = bf16[2048,512]{1,0:T(8,128)(2,1)S(1)} copy-done((bf16[2048,512]{1,0:T(8,128)(2,1)S(1)}, bf16[2048,512]{1,0:T(8,128)(2,1)}, u32[]{:S(2)}) %copy-start.4) | copy-done | bytes 2097176
  12.4 0.9 %copy-done.6 = bf16[32,2048]{1,0:T(8,128)(2,1)S(1)} copy-done((bf16[32,2048]{1,0:T(8,128)(2,1)S(1)}, bf16[32,2048]{1,0:T(8,128)(2,1)}, u32[]{:S(2)}) %copy-start.6) | copy-done | bytes 131096
  13.3 0.9 %twin_project_qk.1 = (f32[32,512]{1,0:T(8,128)S(1)}, f32[32,512]{1,0:T(8,128)S(1)}, f32[8,256]{1,0:T(8,128)S(1)}) custom-call(bf16[32,2048]{1,0:T(8,128)(2,1)S(1)} %copy-done.6, bf16[2048,512]{1,0:T(8,128)(2,1)S(1)} %copy-done.3, bf16[2048,512]{1,0:T(8,128)(2,1)S(1)} %copy-done.4), custom_call_target="tpu_custom_call" | custom-call | tf_op jit(solution)/shard_map/twin_project_qk/pallas_call | solution.py:731
  15.0 0.9 %collective-permute-start.2 = (f32[8,256]{1,0:T(8,128)S(1)}, f32[8,256]{1,0:T(8,128)S(1)}, u32[]{:S(2)}, u32[]{:S(2)}) collective-permute-start(f32[8,256]{1,0:T(8,128)S(1)} %get-tuple-element.30.refs_7_), channel_id=1, source_target_pairs={{0,2},{1,3},{2,0},{3,1},{4,6},{5,7},{6,4},{7,5},{8,10},{9,11},{10,... | collective-permute-start | bytes 24584 | tf_op jit(solution)/shard_map/ppermute | solution.py:742
  16.7 1.2 %twin_tree.1 = (f32[64,32]{1,0:T(8,128)S(1)}, s32[4,1,64]{2,1,0:T(1,128)S(1)}, f32[32,128]{1,0:T(8,128)S(1)}, f32[32,128]{1,0:T(8,128)S(1)}, s32[4,256]{1,0:T(4,128)S(1)}) custom-call(s32[1,4]{1,0:T(1,128)S(1)} %bitcast.8, s32[1,4]{1,0:T(1,128)S(1)} %bitcast.9, s32[4,64]{1,0:T(4,128)S(1)} %copy-done.11, f32[1,128]{1,0:T(1,128)S(1)} %fusion.2.refs_3_), custom_call_target="tpu_custom_call" | custom-call | tf_op jit(solution)/shard_map/twin_tree/pallas_call | solution.py:731
  19.0 3.7 %collective-permute-start.4 = (bf16[32,1536]{1,0:T(8,128)(2,1)S(1)}, bf16[32,1536]{1,0:T(8,128)(2,1)S(1)}, u32[]{:S(2)}, u32[]{:S(2)}) collective-permute-start(bf16[32,1536]{1,0:T(8,128)(2,1)S(1)} %get-tuple-element.31.refs_4_.refs_3_), channel_id=1, source_target_pairs={{0,24},{4,28},{8,16},{12,20},{16,8},{20,12},{24,0},{28,4},{1,25},{... | collective-permute-start | bytes 294920 | tf_op jit(solution)/shard_map/ppermute | solution.py:748
  24.0 2.6 %collective-permute-done.4.refs_4_.refs_6_ = bf16[32,1536]{1,0:T(8,128)(2,1)S(1)} collective-permute-done((bf16[32,1536]{1,0:T(8,128)(2,1)S(1)}, bf16[32,1536]{1,0:T(8,128)(2,1)S(1)}, u32[]{:S(2)}, u32[]{:S(2)}) %collective-permute-start.4) | collective-permute-done | bytes 98336 | tf_op jit(solution)/shard_map/ppermute | solution.py:748
  26.6 4.6 %collective-permute-done.5.refs_5_.refs_7_ = bf16[32,1536]{1,0:T(8,128)(2,1)S(1)} collective-permute-done((bf16[32,1536]{1,0:T(8,128)(2,1)S(1)}, bf16[32,1536]{1,0:T(8,128)(2,1)S(1)}, u32[]{:S(2)}, u32[]{:S(2)}) %collective-permute-start.5) | collective-permute-done | bytes 98336 | tf_op jit(solution)/shard_map/ppermute | solution.py:748
  31.2 0.9 %twin_attend_far.1 = (bf16[48,512]{1,0:T(8,128)(2,1)S(1)}, bf16[48,512]{1,0:T(8,128)(2,1)S(1)}, bf16[48,512]{1,0:T(8,128)(2,1)S(1)}) custom-call(s32[4,256]{1,0:T(4,128)S(1)} %get-tuple-element.25.refs_0_, bf16[4,128,512]{2,1,0:T(8,128)(2,1)S(1)} %copy-done, bf16[4,128,512]{2,1,0:T(8,128)(2,1)S(1)} %copy-done.1, ...), custom_call_target="tpu_custom_call" | custom-call | tf_op jit(solution)/shard_map/twin_attend_far/pallas_call | solution.py:731
  32.1 2.5 %collective-permute-start.7 = (bf16[48,512]{1,0:T(8,128)(2,1)S(1)}, bf16[48,512]{1,0:T(8,128)(2,1)S(1)}, u32[]{:S(2)}, u32[]{:S(2)}) collective-permute-start(bf16[48,512]{1,0:T(8,128)(2,1)S(1)} %get-tuple-element.32.refs_9_), channel_id=1, source_target_pairs={{0,24},{4,28},{8,16},{12,20},{16,8},{20,12},{24,0},{28,4},{1,25},{... | collective-permute-start | bytes 147464 | tf_op jit(solution)/shard_map/ppermute | solution.py:748
  35.9 1.9 %collective-permute-start.11 = (bf16[48,512]{1,0:T(8,128)(2,1)S(1)}, bf16[48,512]{1,0:T(8,128)(2,1)S(1)}, u32[]{:S(2)}, u32[]{:S(2)}) collective-permute-start(bf16[48,512]{1,0:T(8,128)(2,1)S(1)} %get-tuple-element.37), channel_id=1, source_target_pairs={{0,8},{4,12},{8,0},{12,4},{16,24},{20,28},{24,16},{28,20},{1,9},{5... | collective-permute-start | bytes 147464 | tf_op jit(solution)/shard_map/ppermute | solution.py:748
  37.8 1.5 %collective-permute-start.14 = (bf16[288,512]{1,0:T(8,128)(2,1)S(1)}, bf16[288,512]{1,0:T(8,128)(2,1)S(1)}, u32[]{:S(2)}, u32[]{:S(2)}) collective-permute-start(bf16[288,512]{1,0:T(8,128)(2,1)S(1)} %get-tuple-element.44), channel_id=1, source_target_pairs={{0,4},{4,0},{8,12},{12,8},{16,20},{20,16},{24,28},{28,24},{1,5},{5... | collective-permute-start | bytes 884744 | tf_op jit(solution)/shard_map/ppermute | solution.py:745
  41.0 1.3 %collective-permute-done.12.refs_1_ = bf16[32,2048]{1,0:T(8,128)(2,1)S(1)} collective-permute-done((bf16[32,2048]{1,0:T(8,128)(2,1)S(1)}, bf16[32,2048]{1,0:T(8,128)(2,1)S(1)}, u32[]{:S(2)}, u32[]{:S(2)}) %collective-permute-start.12) | collective-permute-done | bytes 131104 | tf_op jit(solution)/shard_map/ppermute | solution.py:742
  43.1 2.3 %collective-permute-done.14.refs_7_ = bf16[288,512]{1,0:T(8,128)(2,1)S(1)} collective-permute-done((bf16[288,512]{1,0:T(8,128)(2,1)S(1)}, bf16[288,512]{1,0:T(8,128)(2,1)S(1)}, u32[]{:S(2)}, u32[]{:S(2)}) %collective-permute-start.14) | collective-permute-done | bytes 294944 | tf_op jit(solution)/shard_map/ppermute | solution.py:745
  45.4 1.4 %twin_compact.1 = (bf16[4,128,512]{2,1,0:T(8,128)(2,1)}, bf16[4,128,512]{2,1,0:T(8,128)(2,1)}) custom-call(s32[4,1,64]{2,1,0:T(1,128)S(1)} %get-tuple-element.43.refs_0_, bf16[4,128,512]{2,1,0:T(8,128)(2,1)S(1)} %copy-done, bf16[4,128,512]{2,1,0:T(8,128)(2,1)S(1)} %copy-done.1, bf16[32,1536]{1,0:T(8,128)(2,1)S(1)} %get-tuple-element.31.refs_4_.refs_3_, ...), custom_call_target="tpu_custom_call" | custom-call | tf_op jit(solution)/shard_map/twin_compact/pallas_call | solution.py:731
  46.8 1.2 %collective-permute-done.13.refs_1_ = bf16[32,2048]{1,0:T(8,128)(2,1)S(1)} collective-permute-done((bf16[32,2048]{1,0:T(8,128)(2,1)S(1)}, bf16[32,2048]{1,0:T(8,128)(2,1)S(1)}, u32[]{:S(2)}, u32[]{:S(2)}) %collective-permute-start.13) | collective-permute-done | bytes 131104 | tf_op jit(solution)/shard_map/ppermute | solution.py:742
  (51 shorter events, 8.3 us)
Async XLA Ops:
  6.2 25.0 %collective-permute-start = (bf16[6,128,512]{2,1,0:T(8,128)(2,1)S(1)}, bf16[6,128,512]{2,1,0:T(8,128)(2,1)S(1)}, u32[]{:S(2)}, u32[]{:S(2)}) collective-permute-start(bf16[6,128,512]{2,1,0:T(8,128)(2,1)S(1)} %dynamic-slice_dynamic-update-slice_fusion), channel_id=1, source_target_pairs={{0,4},{4,0},{8,12},{12,8},{16,20},{20,16},{24,28},{28,24},{1,5},{5... | collective-permute-start | bytes 2359304 | tf_op jit(solution)/shard_map/ppermute | solution.py:745
  13.3 2.9 %copy-start.5 = (bf16[2048,512]{1,0:T(8,128)(2,1)S(1)}, bf16[2048,512]{1,0:T(8,128)(2,1)}, u32[]{:S(2)}) copy-start(bf16[2048,512]{1,0:T(8,128)(2,1)} %refs_1_.6) | copy-start | bytes 6291460
  14.2 2.5 %copy-start.11 = (s32[4,64]{1,0:T(4,128)S(1)}, s32[4,64]{1,0:T(4,128)}, u32[]{:S(2)}) copy-start(s32[4,64]{1,0:T(4,128)} %refs_2_.5) | copy-start | bytes 3076
  14.2 4.5 %copy-start.8 = (f32[512]{0:T(512)S(1)}, f32[512]{0:T(512)}, u32[]{:S(2)}) copy-start(f32[512]{0:T(512)} %param.18) | copy-start | bytes 6148
  14.3 4.5 %copy-start.9 = (f32[512]{0:T(512)S(1)}, f32[512]{0:T(512)}, u32[]{:S(2)}) copy-start(f32[512]{0:T(512)} %param.19) | copy-start | bytes 6148
  14.3 16.9 %copy-start = (bf16[4,128,512]{2,1,0:T(8,128)(2,1)S(1)}, bf16[4,128,512]{2,1,0:T(8,128)(2,1)}, u32[]{:S(2)}) copy-start(bf16[4,128,512]{2,1,0:T(8,128)(2,1)} %refs_1_.9) | copy-start | bytes 1572868
  14.3 16.9 %copy-start.1 = (bf16[4,128,512]{2,1,0:T(8,128)(2,1)S(1)}, bf16[4,128,512]{2,1,0:T(8,128)(2,1)}, u32[]{:S(2)}) copy-start(bf16[4,128,512]{2,1,0:T(8,128)(2,1)} %refs_2_.9) | copy-start | bytes 1572868
  14.3 3.6 %collective-permute-start.1 = (f32[8,256]{1,0:T(8,128)S(1)}, f32[8,256]{1,0:T(8,128)S(1)}, u32[]{:S(2)}, u32[]{:S(2)}) collective-permute-start(f32[8,256]{1,0:T(8,128)S(1)} %get-tuple-element.30.refs_7_), channel_id=1, source_target_pairs={{0,3},{1,2},{2,1},{3,0},{4,7},{5,6},{6,5},{7,4},{8,11},{9,10},{10,... | collective-permute-start | bytes 24584 | tf_op jit(solution)/shard_map/ppermute | solution.py:742
  15.0 3.7 %collective-permute-start.2 = (f32[8,256]{1,0:T(8,128)S(1)}, f32[8,256]{1,0:T(8,128)S(1)}, u32[]{:S(2)}, u32[]{:S(2)}) collective-permute-start(f32[8,256]{1,0:T(8,128)S(1)} %get-tuple-element.30.refs_7_), channel_id=1, source_target_pairs={{0,2},{1,3},{2,0},{3,1},{4,6},{5,7},{6,4},{7,5},{8,10},{9,11},{10,... | collective-permute-start | bytes 24584 | tf_op jit(solution)/shard_map/ppermute | solution.py:742
  16.0 2.8 %collective-permute-start.3 = (f32[8,256]{1,0:T(8,128)S(1)}, f32[8,256]{1,0:T(8,128)S(1)}, u32[]{:S(2)}, u32[]{:S(2)}) collective-permute-start(f32[8,256]{1,0:T(8,128)S(1)} %get-tuple-element.30.refs_7_), channel_id=1, source_target_pairs={{0,1},{1,0},{2,3},{3,2},{4,5},{5,4},{6,7},{7,6},{8,9},{9,8},{10,11... | collective-permute-start | bytes 24584 | tf_op jit(solution)/shard_map/ppermute | solution.py:742
  16.7 23.5 %copy-start.2 = (bf16[512,2048]{1,0:T(8,128)(2,1)S(1)}, bf16[512,2048]{1,0:T(8,128)(2,1)}, u32[]{:S(2)}) copy-start(bf16[512,2048]{1,0:T(8,128)(2,1)} %refs_5_.1) | copy-start | bytes 6291460
  19.0 7.6 %collective-permute-start.4 = (bf16[32,1536]{1,0:T(8,128)(2,1)S(1)}, bf16[32,1536]{1,0:T(8,128)(2,1)S(1)}, u32[]{:S(2)}, u32[]{:S(2)}) collective-permute-start(bf16[32,1536]{1,0:T(8,128)(2,1)S(1)} %get-tuple-element.31.refs_4_.refs_3_), channel_id=1, source_target_pairs={{0,24},{4,28},{8,16},{12,20},{16,8},{20,12},{24,0},{28,4},{1,25},{... | collective-permute-start | bytes 294920 | tf_op jit(solution)/shard_map/ppermute | solution.py:748
  22.6 8.5 %collective-permute-start.5 = (bf16[32,1536]{1,0:T(8,128)(2,1)S(1)}, bf16[32,1536]{1,0:T(8,128)(2,1)S(1)}, u32[]{:S(2)}, u32[]{:S(2)}) collective-permute-start(bf16[32,1536]{1,0:T(8,128)(2,1)S(1)} %get-tuple-element.31.refs_4_.refs_3_), channel_id=1, source_target_pairs={{0,16},{4,20},{8,24},{12,28},{16,0},{20,4},{24,8},{28,12},{1,17},{... | collective-permute-start | bytes 294920 | tf_op jit(solution)/shard_map/ppermute | solution.py:748
  22.6 8.5 %collective-permute-start.6 = (bf16[32,1536]{1,0:T(8,128)(2,1)S(1)}, bf16[32,1536]{1,0:T(8,128)(2,1)S(1)}, u32[]{:S(2)}, u32[]{:S(2)}) collective-permute-start(bf16[32,1536]{1,0:T(8,128)(2,1)S(1)} %get-tuple-element.31.refs_4_.refs_3_), channel_id=1, source_target_pairs={{0,8},{4,12},{8,0},{12,4},{16,24},{20,28},{24,16},{28,20},{1,9},{5... | collective-permute-start | bytes 294920 | tf_op jit(solution)/shard_map/ppermute | solution.py:748
  23.4 11.2 %collective-permute-start.9 = (bf16[32,512]{1,0:T(8,128)(2,1)S(1)}, bf16[32,512]{1,0:T(8,128)(2,1)S(1)}, u32[]{:S(2)}, u32[]{:S(2)}) collective-permute-start(bf16[32,512]{1,0:T(8,128)(2,1)S(1)} %get-tuple-element.35), channel_id=1, source_target_pairs={{0,4},{4,0},{8,12},{12,8},{16,20},{20,16},{24,28},{28,24},{1,5},{5... | collective-permute-start | bytes 98312 | tf_op jit(solution)/shard_map/ppermute | solution.py:745
  32.1 7.2 %collective-permute-start.7 = (bf16[48,512]{1,0:T(8,128)(2,1)S(1)}, bf16[48,512]{1,0:T(8,128)(2,1)S(1)}, u32[]{:S(2)}, u32[]{:S(2)}) collective-permute-start(bf16[48,512]{1,0:T(8,128)(2,1)S(1)} %get-tuple-element.32.refs_9_), channel_id=1, source_target_pairs={{0,24},{4,28},{8,16},{12,20},{16,8},{20,12},{24,0},{28,4},{1,25},{... | collective-permute-start | bytes 147464 | tf_op jit(solution)/shard_map/ppermute | solution.py:748
  34.6 5.0 %collective-permute-start.8 = (bf16[48,512]{1,0:T(8,128)(2,1)S(1)}, bf16[48,512]{1,0:T(8,128)(2,1)S(1)}, u32[]{:S(2)}, u32[]{:S(2)}) collective-permute-start(bf16[48,512]{1,0:T(8,128)(2,1)S(1)} %get-tuple-element.33), channel_id=1, source_target_pairs={{0,16},{4,20},{8,24},{12,28},{16,0},{20,4},{24,8},{28,12},{1,17},{... | collective-permute-start | bytes 147464 | tf_op jit(solution)/shard_map/ppermute | solution.py:748
  35.3 4.6 %collective-permute-start.10 = (bf16[48,512]{1,0:T(8,128)(2,1)S(1)}, bf16[48,512]{1,0:T(8,128)(2,1)S(1)}, u32[]{:S(2)}, u32[]{:S(2)}) collective-permute-start(bf16[48,512]{1,0:T(8,128)(2,1)S(1)} %get-tuple-element.36), channel_id=1, source_target_pairs={{0,4},{4,0},{8,12},{12,8},{16,20},{20,16},{24,28},{28,24},{1,5},{5... | collective-permute-start | bytes 147464 | tf_op jit(solution)/shard_map/ppermute | solution.py:745
  35.9 4.3 %collective-permute-start.11 = (bf16[48,512]{1,0:T(8,128)(2,1)S(1)}, bf16[48,512]{1,0:T(8,128)(2,1)S(1)}, u32[]{:S(2)}, u32[]{:S(2)}) collective-permute-start(bf16[48,512]{1,0:T(8,128)(2,1)S(1)} %get-tuple-element.37), channel_id=1, source_target_pairs={{0,8},{4,12},{8,0},{12,4},{16,24},{20,28},{24,16},{28,20},{1,9},{5... | collective-permute-start | bytes 147464 | tf_op jit(solution)/shard_map/ppermute | solution.py:748
  37.8 7.6 %collective-permute-start.14 = (bf16[288,512]{1,0:T(8,128)(2,1)S(1)}, bf16[288,512]{1,0:T(8,128)(2,1)S(1)}, u32[]{:S(2)}, u32[]{:S(2)}) collective-permute-start(bf16[288,512]{1,0:T(8,128)(2,1)S(1)} %get-tuple-element.44), channel_id=1, source_target_pairs={{0,4},{4,0},{8,12},{12,8},{16,20},{20,16},{24,28},{28,24},{1,5},{5... | collective-permute-start | bytes 884744 | tf_op jit(solution)/shard_map/ppermute | solution.py:745
  40.2 7.8 %copy-start.7 = (bf16[32,2048]{1,0:T(8,128)(2,1)S(1)}, bf16[32,2048]{1,0:T(8,128)(2,1)}, u32[]{:S(2)}) copy-start(bf16[32,2048]{1,0:T(8,128)(2,1)} %refs_3_.1) | copy-start | bytes 393220
  40.2 7.8 %copy-start.10 = (f32[512]{0:T(512)S(1)}, f32[512]{0:T(512)}, u32[]{:S(2)}) copy-start(f32[512]{0:T(512)} %param.20) | copy-start | bytes 6148
  40.9 1.4 %collective-permute-start.12 = (bf16[32,2048]{1,0:T(8,128)(2,1)S(1)}, bf16[32,2048]{1,0:T(8,128)(2,1)S(1)}, u32[]{:S(2)}, u32[]{:S(2)}) collective-permute-start(bf16[32,2048]{1,0:T(8,128)(2,1)S(1)} %get-tuple-element.40), channel_id=1, source_target_pairs={{0,1},{1,0},{2,3},{3,2},{4,5},{5,4},{6,7},{7,6},{8,9},{9,8},{10,11... | collective-permute-start | bytes 393224 | tf_op jit(solution)/shard_map/ppermute | solution.py:742
  42.4 5.6 %collective-permute-start.13 = (bf16[32,2048]{1,0:T(8,128)(2,1)S(1)}, bf16[32,2048]{1,0:T(8,128)(2,1)S(1)}, u32[]{:S(2)}, u32[]{:S(2)}) collective-permute-start(bf16[32,2048]{1,0:T(8,128)(2,1)S(1)} %get-tuple-element.42), channel_id=1, source_target_pairs={{0,2},{1,3},{2,0},{3,1},{4,6},{5,7},{6,4},{7,5},{8,10},{9,11},{10,... | collective-permute-start | bytes 393224 | tf_op jit(solution)/shard_map/ppermute | solution.py:742
  (5 other events, 9.1 us)

commit v10 on v4

--- a/solution.py
+++ b/solution.py
@@ -533,9 +533,9 @@
     packed[:, 2 * width :] = value[...]
 
 
-def weigh(s, visible):
+def weigh(s):
     peak = jnp.max(s, axis=1, keepdims=True).astype(BF16).astype(F32)
-    weights = jnp.exp(jnp.where(visible, s - peak, NEG))
+    weights = jnp.exp(s - jnp.maximum(peak, 0.1 * NEG))
     total = jnp.sum(weights, axis=1, keepdims=True)
     high = total.astype(BF16).astype(F32)
     return weights.astype(BF16), (peak, high, total - high)
@@ -580,7 +580,7 @@
         stats = jnp.zeros((own, LANES), F32)
         for h in range(heads):
             lanes = slice(h * HEAD_DIM, (h + 1) * HEAD_DIM)
-            weights, found = weigh(scores[at, h], visible[at])
+            weights, found = weigh(scores[at, h])
             out = dot(weights[:, :block], value_cache[plane() ^ turn, :, lanes])
             out = out + dot(weights[:, block:], swapped[at, 1, :, lanes])
             outs[at][:own, lanes] = out.astype(BF16)
@@ -614,7 +614,7 @@
     stats = jnp.zeros((2 * own, LANES), F32)
     for h in range(heads):
         lanes = slice(h * HEAD_DIM, (h + 1) * HEAD_DIM)
-        weights, found = weigh(own_scores[h], near)
+        weights, found = weigh(own_scores[h])
         out = dot(weights[:, :block], value_cache[plane(), :, lanes])
         values = mine[:, 2 * width + h * HEAD_DIM : 2 * width + (h + 1) * HEAD_DIM]
         out = out + dot(weights[:, block : block + own], values)

time: 43.1 us -> 43.1 us (level)
  no operation moved by 1% of the time
where the time goes in v10:
time: 43.1 us; the launch traced here: 42.9 us
  starting transfers between devices  18.6 us (43%)
  waiting for transfers between devices  14.5 us (34%)
  Pallas kernels  7.19 us (17%)
  local copies, waits for them, and re-layouts  1.51 us (4%)
  between operations  0.9 us (2%)
    ppermute x6, waiting for transfers between devices, over_planes(): lax.ppermute(x, 'seq', [(i, (i // 2 ^ turn) * 2 + i % 2) for i in range(s...  9.32 us
    ppermute x6, starting transfers between devices, over_planes(): lax.ppermute(x, 'seq', [(i, (i // 2 ^ turn) * 2 + i % 2) for i in range(s...  9.14 us
    pallas_call x10, Pallas kernels, call(): pl.pallas_call(run, out_shape=outs, in_specs=([VMEM] * count if specs is...  7.19 us
    ppermute x4, starting transfers between devices, beside(): return lax.ppermute(x, 'seq', [(i, i ^ 1) for i in range(seq)])  5.96 us
    ppermute x5, waiting for transfers between devices, over_tp(): return lax.ppermute(x, 'tp', [(i, i ^ k) for i in range(tp)])  4.83 us
    ppermute x5, starting transfers between devices, over_tp(): return lax.ppermute(x, 'tp', [(i, i ^ k) for i in range(tp)])  3.55 us
    dynamic_slice x1, local copies, waits for them, and re-layouts, picked(): lax.dynamic_index_in_dim(x, me ^ turn, 0, False)  1.43 us
  transfers between devices with their start and end apart: 15, of which 8 were waited for; matrix products, arithmetic and copies ran while one was open for 0% of the time, Pallas kernels for 15%

profile of v10, /device:TPU:0, one launch (start us, length us, event | category | flops | bytes accessed | tf_op | source)
XLA Modules:
  0.0 42.9 jit_solution(7387547409972164942)
XLA Ops:
  0.7 1.4 %constant_dynamic-slice_fusion.4 = (bf16[1,128,512]{2,1,0:T(8,128)(2,1)S(1)}, bf16[1,128,512]{2,1,0:T(8,128)(2,1)S(1)}, bf16[1,128,512]{2,1,0:T(8,128)(2,1)S(1)}...) fusion(bf16[4,128,512]{2,1,0:T(8,128)(2,1)} %refs_2_.9, ...), kind=kLoop, calls=%fused_computation.9 | loop fusion | bytes 1572876 | tf_op jit(solution)/shard_map/jit(dynamic_index_in_dim)/dynamic_slice | solution.py:754
  2.3 3.0 %collective-permute-start = (bf16[3,2,128,512]{3,2,1,0:T(8,128)(2,1)S(1)}, bf16[3,2,128,512]{3,2,1,0:T(8,128)(2,1)S(1)}, u32[]{:S(2)}, u32[]{:S(2)}) collective-permute-start(bf16[3,2,128,512]{3,2,1,0:T(8,128)(2,1)S(1)} %pad_maximum_fusion), channel_id=1, source_target_pairs={{0,4},{4,0},{8,12},{12,8},{16,20},{20,16},{24,28},{28,24},{1,5},{5... | collective-permute-start | bytes 2359304 | tf_op jit(solution)/shard_map/ppermute | solution.py:745
  5.4 0.9 %twin_project_qk.1 = (f32[32,512]{1,0:T(8,128)S(1)}, f32[32,512]{1,0:T(8,128)S(1)}, f32[8,256]{1,0:T(8,128)S(1)}) custom-call(bf16[32,2048]{1,0:T(8,128)(2,1)S(1)} %copy-done.6, bf16[2048,512]{1,0:T(8,128)(2,1)S(1)} %copy-done.3, bf16[2048,512]{1,0:T(8,128)(2,1)S(1)} %copy-done.4), custom_call_target="tpu_custom_call" | custom-call | tf_op jit(solution)/shard_map/twin_project_qk/pallas_call | solution.py:731
  6.4 0.7 %collective-permute-start.1 = (f32[8,256]{1,0:T(8,128)S(1)}, f32[8,256]{1,0:T(8,128)S(1)}, u32[]{:S(2)}, u32[]{:S(2)}) collective-permute-start(f32[8,256]{1,0:T(8,128)S(1)} %get-tuple-element.30.refs_7_), channel_id=1, source_target_pairs={{0,3},{1,2},{2,1},{3,0},{4,7},{5,6},{6,5},{7,4},{8,11},{9,10},{10,... | collective-permute-start | bytes 24584 | tf_op jit(solution)/shard_map/ppermute | solution.py:742
  7.1 0.9 %collective-permute-start.2 = (f32[8,256]{1,0:T(8,128)S(1)}, f32[8,256]{1,0:T(8,128)S(1)}, u32[]{:S(2)}, u32[]{:S(2)}) collective-permute-start(f32[8,256]{1,0:T(8,128)S(1)} %get-tuple-element.30.refs_7_), channel_id=1, source_target_pairs={{0,2},{1,3},{2,0},{3,1},{4,6},{5,7},{6,4},{7,5},{8,10},{9,11},{10,... | collective-permute-start | bytes 24584 | tf_op jit(solution)/shard_map/ppermute | solution.py:742
  8.8 1.2 %twin_tree.1 = (f32[64,32]{1,0:T(8,128)S(1)}, s32[4,1,64]{2,1,0:T(1,128)S(1)}, f32[32,128]{1,0:T(8,128)S(1)}, f32[32,128]{1,0:T(8,128)S(1)}, s32[4,256]{1,0:T(4,128)S(1)}) custom-call(s32[1,4]{1,0:T(1,128)S(1)} %bitcast.14, s32[1,4]{1,0:T(1,128)S(1)} %bitcast.15, s32[4,64]{1,0:T(4,128)S(1)} %copy-done.10, f32[1,128]{1,0:T(1,128)S(1)} %fusion.2.refs_3_), custom_call_target="tpu_custom_call" | custom-call | tf_op jit(solution)/shard_map/twin_tree/pallas_call | solution.py:731
  10.0 0.8 %collective-permute-done.2.refs_9_ = f32[8,256]{1,0:T(8,128)S(1)} collective-permute-done((f32[8,256]{1,0:T(8,128)S(1)}, f32[8,256]{1,0:T(8,128)S(1)}, u32[]{:S(2)}, u32[]{:S(2)}) %collective-permute-start.2) | collective-permute-done | bytes 8224 | tf_op jit(solution)/shard_map/ppermute | solution.py:742
  11.0 3.7 %collective-permute-start.4 = (bf16[32,1536]{1,0:T(8,128)(2,1)S(1)}, bf16[32,1536]{1,0:T(8,128)(2,1)S(1)}, u32[]{:S(2)}, u32[]{:S(2)}) collective-permute-start(bf16[32,1536]{1,0:T(8,128)(2,1)S(1)} %get-tuple-element.31.refs_4_.refs_3_), channel_id=1, source_target_pairs={{0,24},{4,28},{8,16},{12,20},{16,8},{20,12},{24,0},{28,4},{1,25},{... | collective-permute-start | bytes 294920 | tf_op jit(solution)/shard_map/ppermute | solution.py:748
  14.7 0.8 %collective-permute-start.6 = (bf16[32,1536]{1,0:T(8,128)(2,1)S(1)}, bf16[32,1536]{1,0:T(8,128)(2,1)S(1)}, u32[]{:S(2)}, u32[]{:S(2)}) collective-permute-start(bf16[32,1536]{1,0:T(8,128)(2,1)S(1)} %get-tuple-element.31.refs_4_.refs_3_), channel_id=1, source_target_pairs={{0,8},{4,12},{8,0},{12,4},{16,24},{20,28},{24,16},{28,20},{1,9},{5... | collective-permute-start | bytes 294920 | tf_op jit(solution)/shard_map/ppermute | solution.py:748
  15.5 1.0 %collective-permute-start.9 = (bf16[32,512]{1,0:T(8,128)(2,1)S(1)}, bf16[32,512]{1,0:T(8,128)(2,1)S(1)}, u32[]{:S(2)}, u32[]{:S(2)}) collective-permute-start(bf16[32,512]{1,0:T(8,128)(2,1)S(1)} %get-tuple-element.35), channel_id=1, source_target_pairs={{0,4},{4,0},{8,12},{12,8},{16,20},{20,16},{24,28},{28,24},{1,5},{5... | collective-permute-start | bytes 98312 | tf_op jit(solution)/shard_map/ppermute | solution.py:745
  16.5 2.1 %collective-permute-done.4.refs_4_.refs_6_ = bf16[32,1536]{1,0:T(8,128)(2,1)S(1)} collective-permute-done((bf16[32,1536]{1,0:T(8,128)(2,1)S(1)}, bf16[32,1536]{1,0:T(8,128)(2,1)S(1)}, u32[]{:S(2)}, u32[]{:S(2)}) %collective-permute-start.4) | collective-permute-done | bytes 98336 | tf_op jit(solution)/shard_map/ppermute | solution.py:748
  18.6 4.6 %collective-permute-done.5.refs_5_.refs_7_ = bf16[32,1536]{1,0:T(8,128)(2,1)S(1)} collective-permute-done((bf16[32,1536]{1,0:T(8,128)(2,1)S(1)}, bf16[32,1536]{1,0:T(8,128)(2,1)S(1)}, u32[]{:S(2)}, u32[]{:S(2)}) %collective-permute-start.5) | collective-permute-done | bytes 98336 | tf_op jit(solution)/shard_map/ppermute | solution.py:748
  23.3 0.9 %twin_attend_far.1 = (bf16[48,512]{1,0:T(8,128)(2,1)S(1)}, bf16[48,512]{1,0:T(8,128)(2,1)S(1)}, bf16[48,512]{1,0:T(8,128)(2,1)S(1)}) custom-call(s32[4,256]{1,0:T(4,128)S(1)} %get-tuple-element.25.refs_0_, bf16[4,128,512]{2,1,0:T(8,128)(2,1)S(1)} %copy-done, bf16[4,128,512]{2,1,0:T(8,128)(2,1)S(1)} %copy-done.1, ...), custom_call_target="tpu_custom_call" | custom-call | tf_op jit(solution)/shard_map/twin_attend_far/pallas_call | solution.py:731
  24.2 3.9 %collective-permute-start.7 = (bf16[48,512]{1,0:T(8,128)(2,1)S(1)}, bf16[48,512]{1,0:T(8,128)(2,1)S(1)}, u32[]{:S(2)}, u32[]{:S(2)}) collective-permute-start(bf16[48,512]{1,0:T(8,128)(2,1)S(1)} %get-tuple-element.32.refs_9_), channel_id=1, source_target_pairs={{0,24},{4,28},{8,16},{12,20},{16,8},{20,12},{24,0},{28,4},{1,25},{... | collective-permute-start | bytes 147464 | tf_op jit(solution)/shard_map/ppermute | solution.py:748
  28.7 1.6 %collective-permute-start.10 = (bf16[48,512]{1,0:T(8,128)(2,1)S(1)}, bf16[48,512]{1,0:T(8,128)(2,1)S(1)}, u32[]{:S(2)}, u32[]{:S(2)}) collective-permute-start(bf16[48,512]{1,0:T(8,128)(2,1)S(1)} %get-tuple-element.36), channel_id=1, source_target_pairs={{0,4},{4,0},{8,12},{12,8},{16,20},{20,16},{24,28},{28,24},{1,5},{5... | collective-permute-start | bytes 147464 | tf_op jit(solution)/shard_map/ppermute | solution.py:745
  30.3 0.8 %collective-permute-start.11 = (bf16[48,512]{1,0:T(8,128)(2,1)S(1)}, bf16[48,512]{1,0:T(8,128)(2,1)S(1)}, u32[]{:S(2)}, u32[]{:S(2)}) collective-permute-start(bf16[48,512]{1,0:T(8,128)(2,1)S(1)} %get-tuple-element.37), channel_id=1, source_target_pairs={{0,8},{4,12},{8,0},{12,4},{16,24},{20,28},{24,16},{28,20},{1,9},{5... | collective-permute-start | bytes 147464 | tf_op jit(solution)/shard_map/ppermute | solution.py:748
  31.4 1.6 %collective-permute-done.8.refs_1_ = bf16[48,512]{1,0:T(8,128)(2,1)S(1)} collective-permute-done((bf16[48,512]{1,0:T(8,128)(2,1)S(1)}, bf16[48,512]{1,0:T(8,128)(2,1)S(1)}, u32[]{:S(2)}, u32[]{:S(2)}) %collective-permute-start.8) | collective-permute-done | bytes 49184 | tf_op jit(solution)/shard_map/ppermute | solution.py:748
  33.4 1.0 %collective-permute-done.11.refs_3_ = bf16[48,512]{1,0:T(8,128)(2,1)S(1)} collective-permute-done((bf16[48,512]{1,0:T(8,128)(2,1)S(1)}, bf16[48,512]{1,0:T(8,128)(2,1)S(1)}, u32[]{:S(2)}, u32[]{:S(2)}) %collective-permute-start.11) | collective-permute-done | bytes 49184 | tf_op jit(solution)/shard_map/ppermute | solution.py:748
  34.4 0.8 %twin_merge_and_project.1 = (f32[32,2048]{1,0:T(8,128)S(1)}, bf16[32,2048]{1,0:T(8,128)(2,1)S(1)}) custom-call(bf16[48,512]{1,0:T(8,128)(2,1)S(1)} %collective-permute-done.7.refs_0_, bf16[48,512]{1,0:T(8,128)(2,1)S(1)} %collective-permute-done.8.refs_1_, bf16[48,512]{1,0:T(8,128)(2,1)S(1)} %collective-permute-done.10.refs_2_, ...), custom_call_target="tpu_custom_call" | custom-call | tf_op jit(solution)/shard_map/twin_merge_and_project/pallas_call | solution.py:731
  35.2 1.3 %collective-permute-done.12.refs_1_ = bf16[32,2048]{1,0:T(8,128)(2,1)S(1)} collective-permute-done((bf16[32,2048]{1,0:T(8,128)(2,1)S(1)}, bf16[32,2048]{1,0:T(8,128)(2,1)S(1)}, u32[]{:S(2)}, u32[]{:S(2)}) %collective-permute-start.12) | collective-permute-done | bytes 131104 | tf_op jit(solution)/shard_map/ppermute | solution.py:742
  36.5 1.6 %collective-permute-start.13 = (bf16[32,2048]{1,0:T(8,128)(2,1)S(1)}, bf16[32,2048]{1,0:T(8,128)(2,1)S(1)}, u32[]{:S(2)}, u32[]{:S(2)}) collective-permute-start(bf16[32,2048]{1,0:T(8,128)(2,1)S(1)} %get-tuple-element.42), channel_id=1, source_target_pairs={{0,2},{1,3},{2,0},{3,1},{4,6},{5,7},{6,4},{7,5},{8,10},{9,11},{10,... | collective-permute-start | bytes 393224 | tf_op jit(solution)/shard_map/ppermute | solution.py:742
  38.1 1.4 %twin_compact.1 = (bf16[4,128,512]{2,1,0:T(8,128)(2,1)}, bf16[4,128,512]{2,1,0:T(8,128)(2,1)}) custom-call(s32[4,1,64]{2,1,0:T(1,128)S(1)} %get-tuple-element.43.refs_0_, bf16[4,128,512]{2,1,0:T(8,128)(2,1)S(1)} %copy-done, bf16[4,128,512]{2,1,0:T(8,128)(2,1)S(1)} %copy-done.1, bf16[32,1536]{1,0:T(8,128)(2,1)S(1)} %get-tuple-element.31.refs_4_.refs_3_, ...), custom_call_target="tpu_custom_call" | custom-call | tf_op jit(solution)/shard_map/twin_compact/pallas_call | solution.py:731
  39.5 2.7 %collective-permute-done.13.refs_1_ = bf16[32,2048]{1,0:T(8,128)(2,1)S(1)} collective-permute-done((bf16[32,2048]{1,0:T(8,128)(2,1)S(1)}, bf16[32,2048]{1,0:T(8,128)(2,1)S(1)}, u32[]{:S(2)}, u32[]{:S(2)}) %collective-permute-start.13) | collective-permute-done | bytes 131104 | tf_op jit(solution)/shard_map/ppermute | solution.py:742
  42.2 0.7 %twin_finish.1 = bf16[32,512]{1,0:T(8,128)(2,1)} custom-call(f32[32,2048]{1,0:T(8,128)S(1)} %get-tuple-element.41.refs_0_, bf16[32,2048]{1,0:T(8,128)(2,1)S(1)} %collective-permute-done.13.refs_1_, f32[1,512]{1,0:T(1,128)S(1)} %bitcast.13, bf16[32,2048]{1,0:T(8,128)(2,1)S(1)} %copy-done.6), custom_call_target="tpu_custom_call" | custom-call | tf_op jit(solution)/shard_map/twin_finish/pallas_call | solution.py:731
  (48 shorter events, 2.6 us)
Async XLA Ops:
  0.7 4.7 %copy-start.3 = (bf16[2048,512]{1,0:T(8,128)(2,1)S(1)}, bf16[2048,512]{1,0:T(8,128)(2,1)}, u32[]{:S(2)}) copy-start(bf16[2048,512]{1,0:T(8,128)(2,1)} %refs_1_.5) | copy-start | bytes 6291460
  0.7 4.7 %copy-start.4 = (bf16[2048,512]{1,0:T(8,128)(2,1)S(1)}, bf16[2048,512]{1,0:T(8,128)(2,1)}, u32[]{:S(2)}) copy-start(bf16[2048,512]{1,0:T(8,128)(2,1)} %refs_2_.6) | copy-start | bytes 6291460
  0.7 4.7 %copy-start.6 = (bf16[32,2048]{1,0:T(8,128)(2,1)S(1)}, bf16[32,2048]{1,0:T(8,128)(2,1)}, u32[]{:S(2)}) copy-start(bf16[32,2048]{1,0:T(8,128)(2,1)} %refs_3_.1) | copy-start | bytes 393220
  2.3 6.0 %copy-start.5 = (bf16[2048,512]{1,0:T(8,128)(2,1)S(1)}, bf16[2048,512]{1,0:T(8,128)(2,1)}, u32[]{:S(2)}) copy-start(bf16[2048,512]{1,0:T(8,128)(2,1)} %refs_1_.6) | copy-start | bytes 6291460
  2.3 20.9 %collective-permute-start = (bf16[3,2,128,512]{3,2,1,0:T(8,128)(2,1)S(1)}, bf16[3,2,128,512]{3,2,1,0:T(8,128)(2,1)S(1)}, u32[]{:S(2)}, u32[]{:S(2)}) collective-permute-start(bf16[3,2,128,512]{3,2,1,0:T(8,128)(2,1)S(1)} %pad_maximum_fusion), channel_id=1, source_target_pairs={{0,4},{4,0},{8,12},{12,8},{16,20},{20,16},{24,28},{28,24},{1,5},{5... | collective-permute-start | bytes 2359304 | tf_op jit(solution)/shard_map/ppermute | solution.py:745
  6.3 4.5 %copy-start.7 = (f32[512]{0:T(512)S(1)}, f32[512]{0:T(512)}, u32[]{:S(2)}) copy-start(f32[512]{0:T(512)} %param.18) | copy-start | bytes 6148
  6.3 16.9 %copy-start = (bf16[4,128,512]{2,1,0:T(8,128)(2,1)S(1)}, bf16[4,128,512]{2,1,0:T(8,128)(2,1)}, u32[]{:S(2)}) copy-start(bf16[4,128,512]{2,1,0:T(8,128)(2,1)} %refs_1_.9) | copy-start | bytes 1572868
  6.3 16.9 %copy-start.1 = (bf16[4,128,512]{2,1,0:T(8,128)(2,1)S(1)}, bf16[4,128,512]{2,1,0:T(8,128)(2,1)}, u32[]{:S(2)}) copy-start(bf16[4,128,512]{2,1,0:T(8,128)(2,1)} %refs_2_.9) | copy-start | bytes 1572868
  6.4 3.6 %collective-permute-start.1 = (f32[8,256]{1,0:T(8,128)S(1)}, f32[8,256]{1,0:T(8,128)S(1)}, u32[]{:S(2)}, u32[]{:S(2)}) collective-permute-start(f32[8,256]{1,0:T(8,128)S(1)} %get-tuple-element.30.refs_7_), channel_id=1, source_target_pairs={{0,3},{1,2},{2,1},{3,0},{4,7},{5,6},{6,5},{7,4},{8,11},{9,10},{10,... | collective-permute-start | bytes 24584 | tf_op jit(solution)/shard_map/ppermute | solution.py:742
  7.1 3.7 %collective-permute-start.2 = (f32[8,256]{1,0:T(8,128)S(1)}, f32[8,256]{1,0:T(8,128)S(1)}, u32[]{:S(2)}, u32[]{:S(2)}) collective-permute-start(f32[8,256]{1,0:T(8,128)S(1)} %get-tuple-element.30.refs_7_), channel_id=1, source_target_pairs={{0,2},{1,3},{2,0},{3,1},{4,6},{5,7},{6,4},{7,5},{8,10},{9,11},{10,... | collective-permute-start | bytes 24584 | tf_op jit(solution)/shard_map/ppermute | solution.py:742
  8.0 2.8 %collective-permute-start.3 = (f32[8,256]{1,0:T(8,128)S(1)}, f32[8,256]{1,0:T(8,128)S(1)}, u32[]{:S(2)}, u32[]{:S(2)}) collective-permute-start(f32[8,256]{1,0:T(8,128)S(1)} %get-tuple-element.30.refs_7_), channel_id=1, source_target_pairs={{0,1},{1,0},{2,3},{3,2},{4,5},{5,4},{6,7},{7,6},{8,9},{9,8},{10,11... | collective-permute-start | bytes 24584 | tf_op jit(solution)/shard_map/ppermute | solution.py:742
  8.7 25.6 %copy-start.2 = (bf16[512,2048]{1,0:T(8,128)(2,1)S(1)}, bf16[512,2048]{1,0:T(8,128)(2,1)}, u32[]{:S(2)}) copy-start(bf16[512,2048]{1,0:T(8,128)(2,1)} %refs_5_.1) | copy-start | bytes 6291460
  11.0 7.6 %collective-permute-start.4 = (bf16[32,1536]{1,0:T(8,128)(2,1)S(1)}, bf16[32,1536]{1,0:T(8,128)(2,1)S(1)}, u32[]{:S(2)}, u32[]{:S(2)}) collective-permute-start(bf16[32,1536]{1,0:T(8,128)(2,1)S(1)} %get-tuple-element.31.refs_4_.refs_3_), channel_id=1, source_target_pairs={{0,24},{4,28},{8,16},{12,20},{16,8},{20,12},{24,0},{28,4},{1,25},{... | collective-permute-start | bytes 294920 | tf_op jit(solution)/shard_map/ppermute | solution.py:748
  14.7 8.5 %collective-permute-start.5 = (bf16[32,1536]{1,0:T(8,128)(2,1)S(1)}, bf16[32,1536]{1,0:T(8,128)(2,1)S(1)}, u32[]{:S(2)}, u32[]{:S(2)}) collective-permute-start(bf16[32,1536]{1,0:T(8,128)(2,1)S(1)} %get-tuple-element.31.refs_4_.refs_3_), channel_id=1, source_target_pairs={{0,16},{4,20},{8,24},{12,28},{16,0},{20,4},{24,8},{28,12},{1,17},{... | collective-permute-start | bytes 294920 | tf_op jit(solution)/shard_map/ppermute | solution.py:748
  14.7 8.5 %collective-permute-start.6 = (bf16[32,1536]{1,0:T(8,128)(2,1)S(1)}, bf16[32,1536]{1,0:T(8,128)(2,1)S(1)}, u32[]{:S(2)}, u32[]{:S(2)}) collective-permute-start(bf16[32,1536]{1,0:T(8,128)(2,1)S(1)} %get-tuple-element.31.refs_4_.refs_3_), channel_id=1, source_target_pairs={{0,8},{4,12},{8,0},{12,4},{16,24},{20,28},{24,16},{28,20},{1,9},{5... | collective-permute-start | bytes 294920 | tf_op jit(solution)/shard_map/ppermute | solution.py:748
  15.5 12.6 %collective-permute-start.9 = (bf16[32,512]{1,0:T(8,128)(2,1)S(1)}, bf16[32,512]{1,0:T(8,128)(2,1)S(1)}, u32[]{:S(2)}, u32[]{:S(2)}) collective-permute-start(bf16[32,512]{1,0:T(8,128)(2,1)S(1)} %get-tuple-element.35), channel_id=1, source_target_pairs={{0,4},{4,0},{8,12},{12,8},{16,20},{20,16},{24,28},{28,24},{1,5},{5... | collective-permute-start | bytes 98312 | tf_op jit(solution)/shard_map/ppermute | solution.py:745
  24.2 7.3 %collective-permute-start.7 = (bf16[48,512]{1,0:T(8,128)(2,1)S(1)}, bf16[48,512]{1,0:T(8,128)(2,1)S(1)}, u32[]{:S(2)}, u32[]{:S(2)}) collective-permute-start(bf16[48,512]{1,0:T(8,128)(2,1)S(1)} %get-tuple-element.32.refs_9_), channel_id=1, source_target_pairs={{0,24},{4,28},{8,16},{12,20},{16,8},{20,12},{24,0},{28,4},{1,25},{... | collective-permute-start | bytes 147464 | tf_op jit(solution)/shard_map/ppermute | solution.py:748
  28.1 5.0 %collective-permute-start.8 = (bf16[48,512]{1,0:T(8,128)(2,1)S(1)}, bf16[48,512]{1,0:T(8,128)(2,1)S(1)}, u32[]{:S(2)}, u32[]{:S(2)}) collective-permute-start(bf16[48,512]{1,0:T(8,128)(2,1)S(1)} %get-tuple-element.33), channel_id=1, source_target_pairs={{0,16},{4,20},{8,24},{12,28},{16,0},{20,4},{24,8},{28,12},{1,17},{... | collective-permute-start | bytes 147464 | tf_op jit(solution)/shard_map/ppermute | solution.py:748
  28.7 4.7 %collective-permute-start.10 = (bf16[48,512]{1,0:T(8,128)(2,1)S(1)}, bf16[48,512]{1,0:T(8,128)(2,1)S(1)}, u32[]{:S(2)}, u32[]{:S(2)}) collective-permute-start(bf16[48,512]{1,0:T(8,128)(2,1)S(1)} %get-tuple-element.36), channel_id=1, source_target_pairs={{0,4},{4,0},{8,12},{12,8},{16,20},{20,16},{24,28},{28,24},{1,5},{5... | collective-permute-start | bytes 147464 | tf_op jit(solution)/shard_map/ppermute | solution.py:745
  30.3 4.1 %collective-permute-start.11 = (bf16[48,512]{1,0:T(8,128)(2,1)S(1)}, bf16[48,512]{1,0:T(8,128)(2,1)S(1)}, u32[]{:S(2)}, u32[]{:S(2)}) collective-permute-start(bf16[48,512]{1,0:T(8,128)(2,1)S(1)} %get-tuple-element.37), channel_id=1, source_target_pairs={{0,8},{4,12},{8,0},{12,4},{16,24},{20,28},{24,16},{28,20},{1,9},{5... | collective-permute-start | bytes 147464 | tf_op jit(solution)/shard_map/ppermute | solution.py:748
  31.0 7.1 %collective-permute-start.14 = (bf16[288,512]{1,0:T(8,128)(2,1)S(1)}, bf16[288,512]{1,0:T(8,128)(2,1)S(1)}, u32[]{:S(2)}, u32[]{:S(2)}) collective-permute-start(bf16[288,512]{1,0:T(8,128)(2,1)S(1)} %get-tuple-element.44), channel_id=1, source_target_pairs={{0,4},{4,0},{8,12},{12,8},{16,20},{20,16},{24,28},{28,24},{1,5},{5... | collective-permute-start | bytes 884744 | tf_op jit(solution)/shard_map/ppermute | solution.py:745
  34.3 7.8 %copy-start.9 = (f32[512]{0:T(512)S(1)}, f32[512]{0:T(512)}, u32[]{:S(2)}) copy-start(f32[512]{0:T(512)} %param.20) | copy-start | bytes 6148
  35.1 1.4 %collective-permute-start.12 = (bf16[32,2048]{1,0:T(8,128)(2,1)S(1)}, bf16[32,2048]{1,0:T(8,128)(2,1)S(1)}, u32[]{:S(2)}, u32[]{:S(2)}) collective-permute-start(bf16[32,2048]{1,0:T(8,128)(2,1)S(1)} %get-tuple-element.40), channel_id=1, source_target_pairs={{0,1},{1,0},{2,3},{3,2},{4,5},{5,4},{6,7},{7,6},{8,9},{9,8},{10,11... | collective-permute-start | bytes 393224 | tf_op jit(solution)/shard_map/ppermute | solution.py:742
  36.5 5.6 %collective-permute-start.13 = (bf16[32,2048]{1,0:T(8,128)(2,1)S(1)}, bf16[32,2048]{1,0:T(8,128)(2,1)S(1)}, u32[]{:S(2)}, u32[]{:S(2)}) collective-permute-start(bf16[32,2048]{1,0:T(8,128)(2,1)S(1)} %get-tuple-element.42), channel_id=1, source_target_pairs={{0,2},{1,3},{2,0},{3,1},{4,6},{5,7},{6,4},{7,5},{8,10},{9,11},{10,... | collective-permute-start | bytes 393224 | tf_op jit(solution)/shard_map/ppermute | solution.py:742
  (4 other events, 12.0 us)
